TPU v7x, 32 devices: a whole 2x2x4 slice. The times are simulated.
32 devices in a mesh: row: 8 (over z, x), col: 4 (over y, core).
Axes of the slice: x: 2, y: 2, z: 4, core: 2. Of those that a mesh axis runs over, the one named last changes fastest.
Arguments:
- h_blocks: bfloat16 [4, 8, 16, 128, 128], P(None, 'row', 'col'), may hold values from -1.1953125 to 1.1953125
- p_blocks: bfloat16 [4, 8, 16, 128, 128], P(None, 'row', 'col'), may hold values from -1.1953125 to 1.1953125
- p1_blocks: bfloat16 [4, 8, 16, 128, 128], P(None, 'row', 'col'), may hold values from -1.1953125 to 1.1953125
- h_mask: int32 [4, 8, 16], P(None, 'row', 'col'), may hold values 0 or 1
- p_mask: int32 [4, 8, 16], P(None, 'row', 'col'), may hold values 0 or 1
- p1_mask: int32 [4, 8, 16], P(None, 'row', 'col'), may hold values 0 or 1
Outputs:
- commutator: bfloat16 [4, 8, 16, 128, 128], P(None, 'row', 'col')
- response: bfloat16 [4, 8, 16, 128, 128], P(None, 'row', 'col')
All inputs are finite; a program needn't handle non-finite values. No bound on the sum of `h_mask` or of `p_mask` or of `p1_mask` on one device may be relied on, other than what follows from the above.
Results may differ from a plain program's by a relative error of at most 0.001.
Values may be sent and summed in bfloat16 or wider, within the bound.
No kernel may reach another device: no remote copies, remote signals or barrier semaphores. Data moves between devices by JAX's collectives and lax.ppermute only.
A program may use at most 128 MiB of HBM per device.

v0:
```python
import jax
import jax.numpy as jnp
from jax import lax
from jax.sharding import PartitionSpec as P

K = 16


def spread(x, axis, root):
    mine = lax.axis_index(axis) == root
    return lax.psum(jnp.where(mine, x, jnp.zeros_like(x)), axis)


def masked_blocks(values, pattern):
    return values[:, 0] * pattern[:, 0][:, :, None, None].astype(values.dtype)


def block_product(left_operand, right_operand):
    return jnp.einsum(
        "mij,mkjl->mkil", left_operand, right_operand, preferred_element_type=jnp.float32
    )


def per_device(h_blocks, p_blocks, p1_blocks, h_mask, p_mask, p1_mask):
    row_count = lax.axis_size("row")
    col_count = lax.axis_size("col")
    row_index = lax.axis_index("row")
    col_index = lax.axis_index("col")
    slot_count = h_blocks.shape[2]
    half_band = K // 2
    own_blocks = jnp.stack(
        (
            masked_blocks(h_blocks, h_mask),
            masked_blocks(p_blocks, p_mask),
            masked_blocks(p1_blocks, p1_mask),
        )
    )
    output_phase = (col_index - row_index + half_band) % col_count
    zero_block = jnp.zeros(own_blocks.shape[1:], jnp.float32)
    totals = (zero_block, zero_block, zero_block, zero_block)
    everything = lax.all_gather(own_blocks[:, :, None], "row", axis=2, tiled=True)
    for offset in range(-half_band, half_band):
        device = (row_index + offset) % row_count
        fetched = lax.dynamic_index_in_dim(everything, device, axis=2, keepdims=False)
        position = offset + half_band
        left_slot = position // col_count
        source_col = (position % col_count + row_index - half_band) % col_count
        left_side = spread(own_blocks[:, :, left_slot], "col", source_col)
        row_carry = (row_index + offset) // row_count
        slot_shift = (output_phase - offset) // col_count
        rolled = jnp.roll(fetched, -row_carry, axis=1)
        padded = jnp.pad(rolled, ((0, 0), (0, 0), (slot_count, slot_count), (0, 0), (0, 0)))
        right_side = lax.dynamic_slice_in_dim(padded, slot_count + slot_shift, slot_count, axis=2)
        totals = (
            totals[0] + block_product(left_side[0], right_side[2]),
            totals[1] + block_product(left_side[2], right_side[0]),
            totals[2] + block_product(left_side[1], right_side[2]),
            totals[3] + block_product(left_side[2], right_side[1]),
        )
    output_pattern = p1_mask[:, 0][:, :, None, None].astype(jnp.float32)
    commutator = ((totals[0] - totals[1]) * output_pattern).astype(jnp.bfloat16)[:, None]
    response = ((totals[2] + totals[3]) * output_pattern).astype(jnp.bfloat16)[:, None]
    return (commutator, response)


def solution(mesh):
    in_specs = (
        P(None, "row", "col", None, None),
        P(None, "row", "col", None, None),
        P(None, "row", "col", None, None),
        P(None, "row", "col"),
        P(None, "row", "col"),
        P(None, "row", "col"),
    )
    out_specs = (P(None, "row", "col", None, None), P(None, "row", "col", None, None))
    return jax.shard_map(
        per_device, mesh=mesh, in_specs=in_specs, out_specs=out_specs, check_vma=False
    )
```

profile of v0, /device:TPU:1, one launch (start us, length us, event | category | flops | bytes accessed | tf_op | source)
XLA Modules:
  0.0 337.8 jit_solution(11655586247586904348)
XLA Ops:
  10.5 1.1 bitcast_multiply_fusion.2
  11.7 1.3 bitcast_multiply_fusion
  13.0 1.3 pad_maximum_fusion
  14.5 1.2 copy-done.26
  16.5 2.6 select_bitcast_fusion
  20.3 172.3 %all-gather.3.cloned.1.call-done = bf16[3,4,32,128,128]{4,3,1,0,2:T(8,128)(2,1)} async-done(((bf16[3,4,4,128,128]{4,3,1,0,2:T(8,128)(2,1)}), bf16[3,4,32,128,128]{4,3,1,0,2:T(8,128)(2,1)}) %all-gather.3.cloned.1.call-update) | async-done | bytes 12582928 | tf_op jit(solution)/shard_map/all_gather | solution.py:41
  192.6 18.3 %constant_dynamic-slice_fusion = (bf16[3,4,1,4,128,128]{5,4,1,0,3,2:T(8,128)(2,1)}, bf16[3,4,1,4,128,128]{5,4,1,0,3,2:T(8,128)(2,1)}, bf16[3,4,1,4,128,128]{5,4,...) fusion(bf16[3,4,8,4,128,128]{5,4,1,0,3,2:T(8,128)(2,1)} %bitcas, ...), kind=kLoop, calls=%fused_computation.319 | loop fusion | bytes 50331712 | tf_op jit(solution)/shard_map/jit(dynamic_index_in_dim)/dynamic_slice | solution.py:44
  212.4 2.2 fusion.58
  214.6 1.3 fusion.90
  215.9 1.3 fusion.92
  217.2 1.3 fusion.41
  219.0 1.6 copy.108
  220.6 1.6 copy.109
  222.2 1.6 copy.110
  223.8 1.6 copy.111
  225.4 1.6 copy.112
  227.0 1.6 copy.113
  228.6 1.6 copy.114
  230.2 1.6 copy.115
  231.8 1.6 copy.116
  233.4 1.6 copy.117
  235.0 1.6 copy.118
  236.6 1.6 copy.119
  238.2 1.6 copy.120
  239.8 1.2 copy.121
  241.0 2.1 fusion.14
  244.6 1.1 copy-done.38
  247.7 1.1 copy-done.37
  254.0 1.1 copy-done.35
  257.2 1.1 copy-done.34
  260.3 1.1 copy-done.33
  263.4 1.1 copy-done.32
  266.6 1.1 copy-done.31
  272.9 1.1 copy-done.29
  275.7 9.5 %convolution_add_fusion.19 = f32[4,4,128,128]{3,2,1,0:T(8,128)S(1)} fusion(f32[4,4,128,128]{3,2,1,0:T(8,128)S(1)} %convolution_add_fusion.20, bf16[3,4,128,128]{3,2,1,0:T(8,128)(2,1)S(1)} %copy-done.66, s32[]{:T(128)S(6)} %add.921, s32[]{:T(128)S(6)} %select_n.526, bf16[3,4,4,128,128]{3,4,2,1,0:T(8,128)(2,1)S(1)} %fusion.4), kind=kOutput, calls=%fused_computation.119 | convolution fusion | flops 67371008 | bytes 3801096 | tf_op jit(solution)/shard_map/mij,mkjl->mkil/dot_general | solution.py:19
  287.3 1.1 copy-done.27
  291.5 1.3 convolution_add_fusion.1
  292.8 1.4 convolution_add_fusion.16
  294.6 1.6 copy.122
  296.1 2.1 fusion
  299.5 1.1 fusion.24
  300.6 2.0 copy.55
  302.6 1.7 convolution_add_fusion.44
  307.7 1.1 copy-done.7
  310.7 1.1 copy-done.11
  313.6 1.1 copy-done.15
  320.9 1.1 copy-done.25
  323.3 1.2 convolution_add_fusion.59
  (244 shorter events, 55.5 us)
Async XLA Ops:
  8.0 184.6 %all-gather.3.cloned.1.call-start = ((), (), s32[]{:S(2)}) async-start(), calls=%async_computation | async-start | bytes 14155776 | tf_op jit(solution)/shard_map/all_gather | solution.py:41
  14.3 1.4 copy-start.26
  14.3 198.0 %all-reduce.19.cloned.1.call-start = ((), (), s32[]{:S(2)}) async-start(), calls=%async_computation.1 | async-start | bytes 12582912 | tf_op jit(solution)/shard_map/psum | solution.py:11
  212.4 2.2 copy-start.87
  217.2 1.8 copy-start.53
  219.0 1.6 copy-start.52
  220.6 1.6 copy-start.51
  222.2 1.6 copy-start.50
  223.8 1.6 copy-start.49
  225.4 1.6 copy-start.48
  227.0 1.6 copy-start.47
  228.6 1.6 copy-start.46
  230.2 1.6 copy-start.45
  231.8 1.6 copy-start.44
  233.4 1.6 copy-start.43
  235.0 1.6 copy-start.42
  236.6 1.6 copy-start.41
  238.2 1.6 copy-start.40
  240.9 2.1 copy-start.56
  240.9 2.1 copy-start.86
  244.3 1.4 copy-start.38
  247.4 1.4 copy-start.37
  250.5 1.4 copy-start.36
  253.7 1.4 copy-start.35
  256.9 1.4 copy-start.34
  260.0 1.4 copy-start.33
  263.1 1.4 copy-start.32
  266.3 1.4 copy-start.31
  269.4 1.4 copy-start.30
  275.7 9.5 %copy-start.28 = (bf16[3,4,1,4,128,128]{4,5,3,1,0,2:T(8,128)(2,1)S(1)}, bf16[3,4,1,4,128,128]{4,5,3,1,0,2:T(8,128)(2,1)}, u32[]{:S(2)}) copy-start(bf16[3,4,1,4,128,128]{4,5,3,1,0,2:T(8,128)(2,1)} %copy.119) | copy-start | bytes 4718596
  291.1 1.7 copy-start.24
  292.8 1.8 copy-start.39
  296.1 2.1 copy-start.58
  296.1 2.1 copy-start.59
  302.6 1.8 copy-start.1
  302.6 1.8 copy-start.85
  304.5 1.5 copy-start.83
  305.9 1.5 copy-start.81
  307.4 1.5 copy-start.79
  308.9 1.5 copy-start.77
  310.4 1.5 copy-start.75
  311.8 1.5 copy-start.73
  313.3 1.5 copy-start.71
  314.8 1.5 copy-start.69
  316.2 1.5 copy-start.67
  317.7 1.5 copy-start.65
  319.2 1.5 copy-start.63
  320.6 1.5 copy-start.61
  (42 other events, 50.4 us)
Sparse Core Ops, SparseCore 0:
  14.5 178.0 all-gather.2
Sparse Core Ops, SparseCore 1:
  19.2 123.7 all-reduce.18
where the time goes:
time: 345 us; the launch traced here: 338 us
  waiting for transfers between devices  172 us (50%)
  local copies, waits for them, and re-layouts  88 us (26%)
  matrix products  38.2 us (11%)
  other arithmetic  21.3 us (6%)
  between operations  17.8 us (5%)
    all_gather x1, waiting for transfers between devices, per_device(): lax.all_gather(own_blocks[:, :, None], 'row', axis=2, tiled=True)  172 us
    unnamed x194, local copies, waits for them, and re-layouts  69.4 us
    dot_general x64, matrix products, block_product(): jnp.einsum('mij,mkjl->mkil', left_operand, right_operand, preferred_eleme...  38.2 us
    dynamic_slice x1, local copies, waits for them, and re-layouts, per_device(): lax.dynamic_index_in_dim(everything, device, axis=2, keepdims=False)  18.3 us
    concatenate x16, other arithmetic, per_device(): rolled = jnp.roll(fetched, -row_carry, axis=1)  12.1 us
  transfers between devices with their start and end apart: 2, of which 1 were waited for; matrix products, arithmetic and copies ran while one was open for 7% of the time, Pallas kernels for 0%

commit v1 on v0

v1 whole, which is shorter than its diff:
```python
import functools

import jax
import jax.numpy as jnp
import numpy as np
from jax import lax
from jax.experimental import pallas as pl
from jax.experimental.pallas import tpu as pltpu
from jax.sharding import PartitionSpec as P

H, Q, D = 0, 1, 2
AXES = ("row", "col")


class Plan:
    def __init__(self, row_count, col_count, rows_dev, slot_count):
        self.R, self.C, self.M, self.S = row_count, col_count, rows_dev, slot_count
        self.Z, self.Y = row_count // 2, col_count // 2
        self.K = slot_count * col_count
        self.half = self.K // 2
        reach = (self.half + 1) // 2
        self.ring = 2 * reach + 1 <= self.Z
        self.steps = reach if self.ring else self.Z - 1
        self.nb = -(-self.K // self.R)
        self.units = [(0, 0)]
        for step in range(1, self.steps + 1):
            self.units += [(-1, step), (1, step)]

    def pairs(self, target):
        found = []
        for z in range(self.Z):
            for x in range(2):
                for y in range(self.Y):
                    for k in range(2):
                        to = target(z, x, y, k)
                        if to is not None:
                            tz, tx, ty, tk = to
                            found.append(
                                ((2 * z + x) * self.C + 2 * y + k, (2 * tz + tx) * self.C + 2 * ty + tk)
                            )
        return found

    def holds(self, z, way, step):
        return self.ring or 0 <= z + way * step < self.Z

    def flow(self, way, step):
        def target(z, x, y, k):
            to = z - way
            if not self.ring and not (0 <= to < self.Z and self.holds(to, way, step)):
                return None
            return to % self.Z, x, y, k

        return self.pairs(target)

    def table(self):
        R, C, S, M, Y = self.R, self.C, self.S, self.M, self.Y
        out = np.zeros((R, C, len(self.units), 2 + 2 * self.nb * 4), np.int32)
        for r in range(R):
            for c in range(C):
                z, x, y, k = r // 2, r % 2, c // 2, c % 2
                for u, (way, step) in enumerate(self.units):
                    delta = way * step
                    out[r, c, u, 0] = self.holds(z, way, step)
                    out[r, c, u, 1] = ((z + delta) % self.Z % Y - y) % Y
                    for e in range(2):
                        rho = k ^ e
                        base = 2 * delta + k - rho
                        phase = (2 * y + x - 2 * z - rho + self.half) % C
                        first = -((self.half + base) // R)
                        for n in range(self.nb):
                            w = first + n
                            b = base + R * w
                            ok = -self.half <= b < self.half
                            at = 2 + (e * self.nb + n) * 4
                            out[r, c, u, at:at + 4] = (
                                ((b + self.half) // C if ok else 0),
                                w % M,
                                (phase - b) // C,
                                ok,
                            )
        return out


def contract_body(plan, wanted, has_start, tab, a_ref, *refs):
    count = len(wanted)
    unit_refs = refs[:2 * count]
    refs = refs[2 * count:]
    start_ref = None
    if has_start:
        start_ref, refs = refs[0], refs[1:]
    total_ref, held, sem = refs
    e, m = pl.program_id(0), pl.program_id(1)
    first = jnp.logical_and(e == 0, m == 0)
    S, M, nb = plan.S, plan.M, plan.nb
    B = held.shape[-1]

    def copies(u):
        return (
            pltpu.make_async_copy(unit_refs[2 * u], held.at[u, pl.ds(0, 2)], sem.at[u, 0]),
            pltpu.make_async_copy(unit_refs[2 * u + 1], held.at[u, D], sem.at[u, 1]),
        )

    for u, unit in enumerate(wanted):
        @pl.when(jnp.logical_and(first, tab[unit, 0] == 1))
        def _(u=u):
            for copy in copies(u):
                copy.start()

    if has_start:
        total_ref[...] = start_ref[...]
    else:
        total_ref[...] = jnp.zeros_like(total_ref)

    for u, unit in enumerate(wanted):
        @pl.when(tab[unit, 0] == 1)
        def _(u=u, unit=unit):
            @pl.when(first)
            def _():
                for copy in copies(u):
                    copy.wait()

            dy = tab[unit, 1]
            terms = []
            for n in range(nb):
                at = 2 + (e * nb + n) * 4
                terms.append(tuple(tab[unit, at + i] for i in range(4)))

            def left(mat):
                return jnp.concatenate([a_ref[0, dy, mat, 0, slot] for slot, _, _, _ in terms], axis=1)

            def right(mat):
                rows = []
                for _, row_shift, slot_shift, ok in terms:
                    row = lax.rem(m + row_shift, M)
                    cols = []
                    for s in range(S):
                        slot = s + slot_shift
                        inside = jnp.logical_and(ok == 1, jnp.logical_and(slot >= 0, slot < S))
                        block = held[u, mat, row, jnp.clip(slot, 0, S - 1)]
                        cols.append(jnp.where(inside, block, jnp.zeros_like(block)))
                    rows.append(jnp.concatenate(cols, axis=1))
                return jnp.concatenate(rows, axis=0)

            dot = functools.partial(jnp.dot, preferred_element_type=jnp.float32)
            both = dot(jnp.concatenate([left(H), left(D)], axis=0), right(Q))
            mine = left(Q)
            commutator = both[:B] - dot(mine, right(H))
            response = both[B:] + dot(mine, right(D))
            for s in range(S):
                total_ref[0, 0, 0, s] += commutator[:, s * B:(s + 1) * B]
                total_ref[0, 1, 0, s] += response[:, s * B:(s + 1) * B]


def contract(plan, tab, a_units, wanted, unit_arrays, start):
    M, S, Y = plan.M, plan.S, plan.Y
    B = a_units.shape[-1]
    total_block = pl.BlockSpec((1, 2, 1, S, B, B), lambda e, m, tab: (e, 0, m, 0, 0, 0))
    operands = [a_units]
    specs = [pl.BlockSpec((1, Y, 3, 1, S, B, B), lambda e, m, tab: (e, 0, 0, m, 0, 0, 0))]
    for arrays in unit_arrays:
        operands += list(arrays)
        specs += [pl.BlockSpec(memory_space=pl.ANY)] * 2
    if start is not None:
        operands.append(start)
        specs.append(total_block)
    terms = 2 * M * len(wanted) * plan.nb * S * 4
    return pl.pallas_call(
        functools.partial(contract_body, plan, tuple(wanted), start is not None),
        grid_spec=pltpu.PrefetchScalarGridSpec(
            num_scalar_prefetch=1,
            grid=(2, M),
            in_specs=specs,
            out_specs=total_block,
            scratch_shapes=[
                pltpu.VMEM((len(wanted), 3, M, S, B, B), a_units.dtype),
                pltpu.SemaphoreType.DMA((len(wanted), 2)),
            ],
        ),
        out_shape=jax.ShapeDtypeStruct((2, 2, M, S, B, B), jnp.float32),
        compiler_params=pltpu.CompilerParams(vmem_limit_bytes=32 * 2**20),
        cost_estimate=pl.CostEstimate(
            flops=2 * B**3 * terms,
            bytes_accessed=a_units.size * 2 + len(wanted) * 3 * M * S * B * B * 2,
            transcendentals=0,
        ),
    )(tab, *operands)


def per_device(plan, h_blocks, p_blocks, p1_blocks, h_mask, p_mask, p1_mask):
    def kept(values, pattern):
        return values[:, 0] * pattern[:, 0][:, :, None, None].astype(values.dtype)

    def move(value, pairs):
        return lax.ppermute(value, AXES, pairs)

    row, col = lax.axis_index("row"), lax.axis_index("col")
    tab = jnp.asarray(plan.table())[row, col]
    swapped = (row % 2) != (col % 2)

    own_hq = jnp.stack([kept(h_blocks, h_mask), kept(p1_blocks, p1_mask)])
    own_d = kept(p_blocks, p_mask)

    cross = plan.pairs(lambda z, x, y, k: (z, k, y, x))
    sibling = plan.pairs(lambda z, x, y, k: (z, x, y, 1 - k))
    x_swap = plan.pairs(lambda z, x, y, k: (z, 1 - x, y, k))

    got = {(0, 0): (move(own_hq, cross), move(own_d, cross))}
    for step in range(1, plan.steps + 1):
        for way in (-1, 1):
            before = got[(way, step - 1) if step > 1 else (0, 0)]
            pairs = plan.flow(way, step)
            got[(way, step)] = tuple(move(part, pairs) for part in before)

    own = jnp.concatenate([own_hq, own_d[None]])
    across = move(own, x_swap)
    by_x = ([own], [across])
    for dy in range(1, plan.Y):
        pairs = plan.pairs(lambda z, x, y, k: (z, x, (y - dy) % plan.Y, k))
        by_x[0].append(move(own, pairs))
        by_x[1].append(move(across, pairs))
    near, far = jnp.stack(by_x[0]), jnp.stack(by_x[1])
    a_units = jnp.stack([jnp.where(swapped, far, near), jnp.where(swapped, near, far)])

    every = list(range(len(plan.units)))
    early, late = every[:-2], every[-2:]
    total = contract(plan, tab, a_units, early, [got[plan.units[u]] for u in early], None)
    total = contract(plan, tab, a_units, late, [got[plan.units[u]] for u in late], total)

    result = (total[0] + move(total[1], sibling)).astype(jnp.bfloat16)
    result = move(result, cross)
    pattern = p1_mask[:, 0][None, :, :, None, None].astype(result.dtype)
    result = result * pattern
    return result[0][:, None], result[1][:, None]


def solution(mesh):
    blocks = P(None, "row", "col", None, None)
    masks = P(None, "row", "col")

    def run(h_blocks, p_blocks, p1_blocks, h_mask, p_mask, p1_mask):
        plan = Plan(
            mesh.shape["row"], mesh.shape["col"], h_blocks.shape[0], h_blocks.shape[2] // mesh.shape["col"]
        )
        return jax.shard_map(
            functools.partial(per_device, plan),
            mesh=mesh,
            in_specs=(blocks,) * 3 + (masks,) * 3,
            out_specs=(blocks,) * 2,
            check_vma=False,
        )(h_blocks, p_blocks, p1_blocks, h_mask, p_mask, p1_mask)

    return run
```

time: 345 us -> 189 us (0.55); the launches traced: 338 us -> 186 us
  local copies, waits for them, and re-layouts: 88 us -> 4.35 us
  waiting for transfers between devices: 172 us -> 121 us
  matrix products: 38.2 us -> 0 us
  starting transfers between devices: 0.08 us -> 31 us
  between operations: 17.8 us -> 0.97 us
  Pallas kernels: 0 us -> 16.4 us
  other arithmetic: 21.3 us -> 12.3 us
    all_gather x1 -> x0, waiting for transfers between devices: 172 us -> none  [per_device(): lax.all_gather(own_blocks[:, :, None], 'row', axis=2, tiled=True)]
    ppermute x0 -> x19, waiting for transfers between devices: none -> 121 us  [move(): return lax.ppermute(value, AXES, pairs)]
    unnamed x194 -> x20, local copies, waits for them, and re-layouts: 69.4 us -> 3.52 us
    dot_general x64 -> x0, matrix products: 38.2 us -> none  [block_product(): jnp.einsum('mij,mkjl->mkil', left_operand, right_operand, preferred_eleme...]
    ppermute x0 -> x19, starting transfers between devices: none -> 31 us  [move(): return lax.ppermute(value, AXES, pairs)]
    dynamic_slice x1 -> x0, local copies, waits for them, and re-layouts: 18.3 us -> none  [per_device(): lax.dynamic_index_in_dim(everything, device, axis=2, keepdims=False)]
    pallas_call x0 -> x2, Pallas kernels: none -> 16.4 us  [contract(): pl.pallas_call(functools.partial(contract_body, plan, tuple(wanted), star...]
    concatenate x16 -> x0, other arithmetic: 12.1 us -> none  [per_device(): rolled = jnp.roll(fetched, -row_carry, axis=1)]
  transfers between devices with their start and end apart: 2 -> 19, of which waited for: 1 -> 8; matrix products, arithmetic and copies ran while one was open for 7% -> 5% of each run, Pallas kernels for 0% -> 6%
where the time goes in v1:
time: 189 us; the launch traced here: 186 us
  waiting for transfers between devices  121 us (64%)
  starting transfers between devices  31 us (16%)
  Pallas kernels  16.4 us (9%)
  other arithmetic  12.3 us (7%)
  local copies, waits for them, and re-layouts  4.35 us (2%)
    ppermute x19, waiting for transfers between devices, move(): return lax.ppermute(value, AXES, pairs)  121 us
    ppermute x19, starting transfers between devices, move(): return lax.ppermute(value, AXES, pairs)  31 us
    pallas_call x2, Pallas kernels, contract(): pl.pallas_call(functools.partial(contract_body, plan, tuple(wanted), star...  16.4 us
    select_n x1, other arithmetic, per_device(): jnp.where(swapped, far, near)  4.24 us
  transfers between devices with their start and end apart: 19, of which 8 were waited for; matrix products, arithmetic and copies ran while one was open for 5% of the time, Pallas kernels for 6%

profile of v1, /device:TPU:1, one launch (start us, length us, event | category | flops | bytes accessed | tf_op | source)
XLA Modules:
  0.0 186.4 jit_solution(8069218785108187585)
XLA Ops:
  0.6 0.7 convert_element_type.44
  1.3 0.7 convert_element_type.42
  2.0 0.0 copy-start.6
  2.0 1.4 bitcast_multiply_fusion.2
  3.4 0.1 pad_maximum_fusion.4
  3.5 4.5 %collective-permute-start.3 = (bf16[2,4,4,128,128]{4,3,2,1,0:T(8,128)(2,1)S(1)}, bf16[2,4,4,128,128]{4,3,2,1,0:T(8,128)(2,1)S(1)}, u32[]{:S(2)}, u32[]{:S(2)}) collective-permute-start(bf16[2,4,4,128,128]{4,3,2,1,0:T(8,128)(2,1)S(1)} %pad_maximum_fusion.4), channel_id=1, source_target_pairs={{0,0},{1,4},{2,2},{3,6},{4,1},{5,5},{6,3},{7,7},{8,8},{9,12},{10,1... | collective-permute-start | bytes 3145736 | tf_op jit(solution)/shard_map/ppermute | solution.py:194
  8.1 0.1 bitcast_multiply_fusion.1
  8.2 1.9 %fusion.2 = (bf16[1,1,3,4,4,128,128]{6,5,4,3,2,1,0:T(8,128)(2,1)}, bf16[3,4,4,128,128]{4,3,2,1,0:T(8,128)(2,1)}) fusion(bf16[1,4,4,128,128]{4,3,2,1,0:T(8,128)(2,1)S(1)} %bitcast_multiply_fusion.1, bf16[1,4,4,128,128]{4,3,2,1,0:T(8,128)(2,1)S(1)} %get-tuple-element.10, bf16[1,4,4,128,128]{4,3,2,1,0:T(8,128)(2,1)S(1)} %get-tuple-element.11), kind=kLoop, calls=%fused_computation.22 | loop fusion | flops 1572864 | bytes 4718592 | tf_op jit(solution)/shard_map/stack | solution.py:221
  10.2 0.0 collective-permute-start
  10.2 0.1 bitcast_multiply_fusion
  10.3 1.9 %collective-permute-start.7 = (bf16[4,4,128,128]{3,2,1,0:T(8,128)(2,1)S(1)}, bf16[4,4,128,128]{3,2,1,0:T(8,128)(2,1)S(1)}, u32[]{:S(2)}, u32[]{:S(2)}) collective-permute-start(bf16[4,4,128,128]{3,2,1,0:T(8,128)(2,1)S(1)} %bitcast_multiply_fusion), channel_id=1, source_target_pairs={{0,0},{1,4},{2,2},{3,6},{4,1},{5,5},{6,3},{7,7},{8,8},{9,12},{10,1... | collective-permute-start | bytes 1572872 | tf_op jit(solution)/shard_map/ppermute | solution.py:194
  12.2 48.1 %collective-permute-done.7.refs_1_ = bf16[4,4,128,128]{3,2,1,0:T(8,128)(2,1)S(1)} collective-permute-done((bf16[4,4,128,128]{3,2,1,0:T(8,128)(2,1)S(1)}, bf16[4,4,128,128]{3,2,1,0:T(8,128)(2,1)S(1)}, u32[]{:S(2)}, u32[]{:S(2)}) %collective-permute-start.7) | collective-permute-done | bytes 524320 | tf_op jit(solution)/shard_map/ppermute | solution.py:194
  60.2 1.3 collective-permute-start.14
  61.5 0.0 collective-permute-done.3.refs_0_
  61.5 1.3 collective-permute-start.11
  62.8 4.7 %collective-permute-start.4 = (bf16[2,4,4,128,128]{4,3,2,1,0:T(8,128)(2,1)S(1)}, bf16[2,4,4,128,128]{4,3,2,1,0:T(8,128)(2,1)S(1)}, u32[]{:S(2)}, u32[]{:S(2)}) collective-permute-start(bf16[2,4,4,128,128]{4,3,2,1,0:T(8,128)(2,1)S(1)} %collective-permute-done.3.refs_0_), channel_id=1, source_target_pairs={{0,8},{1,9},{2,10},{3,11},{4,12},{5,13},{6,14},{7,15},{8,16},{9,17... | collective-permute-start | bytes 3145736 | tf_op jit(solution)/shard_map/ppermute | solution.py:194
  67.5 4.1 %collective-permute-start.8 = (bf16[4,4,128,128]{3,2,1,0:T(8,128)(2,1)S(1)}, bf16[4,4,128,128]{3,2,1,0:T(8,128)(2,1)}, u32[]{:S(2)}, u32[]{:S(2)}) collective-permute-start(bf16[4,4,128,128]{3,2,1,0:T(8,128)(2,1)S(1)} %collective-permute-done.7.refs_1_), channel_id=1, source_target_pairs={{0,8},{1,9},{2,10},{3,11},{4,12},{5,13},{6,14},{7,15},{8,16},{9,17... | collective-permute-start | bytes 1572872 | tf_op jit(solution)/shard_map/ppermute | solution.py:194
  71.7 0.8 copy-done
  72.5 3.8 %collective-permute-done.14.refs_5_ = bf16[4,4,128,128]{3,2,1,0:T(8,128)(2,1)S(1)} collective-permute-done((bf16[4,4,128,128]{3,2,1,0:T(8,128)(2,1)S(1)}, bf16[4,4,128,128]{3,2,1,0:T(8,128)(2,1)S(1)}, u32[]{:S(2)}, u32[]{:S(2)}) %collective-permute-start.14) | collective-permute-done | bytes 524320 | tf_op jit(solution)/shard_map/ppermute | solution.py:194
  76.2 1.2 collective-permute-start.2
  77.5 0.2 collective-permute-start.1
  77.7 7.1 %collective-permute-done.8.refs_3_ = bf16[4,4,128,128]{3,2,1,0:T(8,128)(2,1)} collective-permute-done((bf16[4,4,128,128]{3,2,1,0:T(8,128)(2,1)S(1)}, bf16[4,4,128,128]{3,2,1,0:T(8,128)(2,1)}, u32[]{:S(2)}, u32[]{:S(2)}) %collective-permute-start.8) | collective-permute-done | bytes 524320 | tf_op jit(solution)/shard_map/ppermute | solution.py:194
  84.8 1.3 collective-permute-start.15
  86.1 0.8 copy-done.2
  86.9 8.1 %collective-permute-done.11.refs_4_ = bf16[2,4,4,128,128]{4,3,2,1,0:T(8,128)(2,1)S(1)} collective-permute-done((bf16[2,4,4,128,128]{4,3,2,1,0:T(8,128)(2,1)S(1)}, bf16[2,4,4,128,128]{4,3,2,1,0:T(8,128)(2,1)S(1)}, u32[]{:S(2)}, u32[]{:S(2)}) %collective-permute-start.11) | collective-permute-done | bytes 1048608 | tf_op jit(solution)/shard_map/ppermute | solution.py:194
  95.0 1.3 collective-permute-start.12
  96.3 1.7 collective-permute-start.5
  98.0 18.5 %collective-permute-done.15.refs_9_ = bf16[4,4,128,128]{3,2,1,0:T(8,128)(2,1)S(1)} collective-permute-done((bf16[4,4,128,128]{3,2,1,0:T(8,128)(2,1)S(1)}, bf16[4,4,128,128]{3,2,1,0:T(8,128)(2,1)S(1)}, u32[]{:S(2)}, u32[]{:S(2)}) %collective-permute-start.15) | collective-permute-done | bytes 524320 | tf_op jit(solution)/shard_map/ppermute | solution.py:194
  116.5 0.8 copy-done.4
  117.3 1.5 collective-permute-start.9
  118.8 0.7 dynamic-slice_bitcast_fusion.tab
  119.5 0.7 collective-permute-start.10
  120.2 1.3 collective-permute-start.16
  121.5 17.5 %collective-permute-done.12.refs_8_ = bf16[2,4,4,128,128]{4,3,2,1,0:T(8,128)(2,1)} collective-permute-done((bf16[2,4,4,128,128]{4,3,2,1,0:T(8,128)(2,1)S(1)}, bf16[2,4,4,128,128]{4,3,2,1,0:T(8,128)(2,1)}, u32[]{:S(2)}, u32[]{:S(2)}) %collective-permute-start.12) | collective-permute-done | bytes 1048608 | tf_op jit(solution)/shard_map/ppermute | solution.py:194
  139.0 1.3 collective-permute-start.13
  140.3 0.7 collective-permute-start.6
  141.0 4.2 %broadcast_select_fusion.1 = (bf16[1,2,3,4,4,128,128]{6,5,4,3,2,1,0:T(8,128)(2,1)S(1)}, bf16[1,2,3,4,4,128,128]{6,5,4,3,2,1,0:T(8,128)(2,1)}) fusion(pred[]{:T(512)S(6)} %ne.15, bf16[1,1,3,4,4,128,128]{6,5,4,3,2,1,0:T(8,128)(2,1)} %bitcast.7, bf16[1,1,3,4,4,128,128]{6,5,4,3,2,1,0:T(8,128)(2,1)} %get-tuple-element.6, ...), kind=kLoop, calls=%fused_computation.4 | loop fusion | flops 6291456 | bytes 12582913 | tf_op jit(solution)/shard_map/jit(_where)/select_n | solution.py:222
  145.3 2.6 %pad_maximum_fusion.a_ref = bf16[2,2,3,4,4,128,128]{6,5,4,3,2,1,0:T(8,128)(2,1)S(1)} fusion(bf16[1,2,3,4,4,128,128]{6,5,4,3,2,1,0:T(8,128)(2,1)} %get-tuple-element.5, bf16[1,2,3,4,4,128,128]{6,5,4,3,2,1,0:T(8,128)(2,1)S(1)} %get-tuple-element.4), kind=kLoop, calls=%fused_computation | loop fusion | flops 3145728 | bytes 12582912 | tf_op jit(solution)/shard_map/stack | solution.py:222
  147.9 11.2 %shard_map.86.refs_4_ = f32[2,2,4,4,128,128]{5,4,3,2,1,0:T(8,128)S(1)} custom-call(s32[7,18]{1,0:T(8,128)S(1)} %dynamic-slice_bitcast_fusion.tab, bf16[2,2,3,4,4,128,128]{6,5,4,3,2,1,0:T(8,128)(2,1)S(1)} %pad_maximum_fusion.a_ref, bf16[2,4,4,128,128]{4,3,2,1,0:T(8,128)(2,1)S(1)} %collective-permute-done.3.refs_0_, bf16[4,4,128,128]{3,2,1,0:T(8,128)(2,1)S(1)} %copy-done.1, ...), custom_call_target="tpu_custom_call" | custom-call | flops 5368709120 | bytes 14155776 | tf_op jit(solution)/shard_map/pallas_call | solution.py:167
  159.2 5.2 %shard_map.87 = f32[2,2,4,4,128,128]{5,4,3,2,1,0:T(8,128)S(1)} custom-call(s32[7,18]{1,0:T(8,128)S(1)} %dynamic-slice_bitcast_fusion.tab, bf16[2,2,3,4,4,128,128]{6,5,4,3,2,1,0:T(8,128)(2,1)S(1)} %pad_maximum_fusion.a_ref, bf16[2,4,4,128,128]{4,3,2,1,0:T(8,128)(2,1)S(1)} %collective-permute-done.6.refs_0_, ...), custom_call_target="tpu_custom_call" | custom-call | flops 2147483648 | bytes 9437184 | tf_op jit(solution)/shard_map/pallas_call | solution.py:167
  164.4 0.1 slice_bitcast_fusion
  164.5 0.1 collective-permute-start.17
  164.6 4.1 %collective-permute-done.17 = f32[2,4,4,128,128]{4,3,2,1,0:T(8,128)S(1)} collective-permute-done((f32[2,4,4,128,128]{4,3,2,1,0:T(8,128)S(1)}, f32[2,4,4,128,128]{4,3,2,1,0:T(8,128)S(1)}, u32[]{:S(2)}, u32[]{:S(2)}) %collective-permute-start.17) | collective-permute-done | bytes 2097184 | tf_op jit(solution)/shard_map/ppermute | solution.py:194
  168.7 0.3 fusion.1
  169.1 1.9 %collective-permute-start.18 = (bf16[2,4,4,128,128]{4,3,2,1,0:T(8,128)(2,1)S(1)}, bf16[2,4,4,128,128]{4,3,2,1,0:T(8,128)(2,1)S(1)}, u32[]{:S(2)}, u32[]{:S(2)}) collective-permute-start(bf16[2,4,4,128,128]{4,3,2,1,0:T(8,128)(2,1)S(1)} %fusion.1), channel_id=1, source_target_pairs={{0,0},{1,4},{2,2},{3,6},{4,1},{5,5},{6,3},{7,7},{8,8},{9,12},{10,1... | collective-permute-start | bytes 3145736 | tf_op jit(solution)/shard_map/ppermute | solution.py:194
  171.0 14.2 %collective-permute-done.18 = bf16[2,4,4,128,128]{4,3,2,1,0:T(8,128)(2,1)S(1)} collective-permute-done((bf16[2,4,4,128,128]{4,3,2,1,0:T(8,128)(2,1)S(1)}, bf16[2,4,4,128,128]{4,3,2,1,0:T(8,128)(2,1)S(1)}, u32[]{:S(2)}, u32[]{:S(2)}) %collective-permute-start.18) | collective-permute-done | bytes 1048608 | tf_op jit(solution)/shard_map/ppermute | solution.py:194
  185.2 0.1 broadcast_multiply_fusion
  185.3 1.1 slice_bitcast_fusion.2
  (26 shorter events, 0.1 us)
Async XLA Ops:
  2.0 6.0 %copy-start.7 = (s32[4,1,4]{2,1,0:T(1,128)S(1)}, s32[4,1,4]{2,1,0:T(1,128)}, u32[]{:S(2)}) copy-start(s32[4,1,4]{2,1,0:T(1,128)} %param.11) | copy-start | bytes 196
  2.0 6.1 %copy-start.6 = (bf16[4,1,4,128,128]{4,3,2,1,0:T(8,128)(2,1)S(1)}, bf16[4,1,4,128,128]{4,3,2,1,0:T(8,128)(2,1)}, u32[]{:S(2)}) copy-start(bf16[4,1,4,128,128]{4,3,2,1,0:T(8,128)(2,1)} %param.8) | copy-start | bytes 1572868
  3.5 58.0 %collective-permute-start.3 = (bf16[2,4,4,128,128]{4,3,2,1,0:T(8,128)(2,1)S(1)}, bf16[2,4,4,128,128]{4,3,2,1,0:T(8,128)(2,1)S(1)}, u32[]{:S(2)}, u32[]{:S(2)}) collective-permute-start(bf16[2,4,4,128,128]{4,3,2,1,0:T(8,128)(2,1)S(1)} %pad_maximum_fusion.4), channel_id=1, source_target_pairs={{0,0},{1,4},{2,2},{3,6},{4,1},{5,5},{6,3},{7,7},{8,8},{9,12},{10,1... | collective-permute-start | bytes 3145736 | tf_op jit(solution)/shard_map/ppermute | solution.py:194
  10.2 67.3 %collective-permute-start = (bf16[3,4,4,128,128]{4,3,2,1,0:T(8,128)(2,1)}, bf16[3,4,4,128,128]{4,3,2,1,0:T(8,128)(2,1)}, u32[]{:S(2)}, u32[]{:S(2)}) collective-permute-start(bf16[3,4,4,128,128]{4,3,2,1,0:T(8,128)(2,1)} %get-tuple-element.7), channel_id=1, source_target_pairs={{0,4},{1,5},{2,6},{3,7},{4,0},{5,1},{6,2},{7,3},{8,12},{9,13},{10,... | collective-permute-start | bytes 4718600 | tf_op jit(solution)/shard_map/ppermute | solution.py:194
  10.3 50.0 %collective-permute-start.7 = (bf16[4,4,128,128]{3,2,1,0:T(8,128)(2,1)S(1)}, bf16[4,4,128,128]{3,2,1,0:T(8,128)(2,1)S(1)}, u32[]{:S(2)}, u32[]{:S(2)}) collective-permute-start(bf16[4,4,128,128]{3,2,1,0:T(8,128)(2,1)S(1)} %bitcast_multiply_fusion), channel_id=1, source_target_pairs={{0,0},{1,4},{2,2},{3,6},{4,1},{5,5},{6,3},{7,7},{8,8},{9,12},{10,1... | collective-permute-start | bytes 1572872 | tf_op jit(solution)/shard_map/ppermute | solution.py:194
  60.2 16.0 %collective-permute-start.14 = (bf16[4,4,128,128]{3,2,1,0:T(8,128)(2,1)S(1)}, bf16[4,4,128,128]{3,2,1,0:T(8,128)(2,1)S(1)}, u32[]{:S(2)}, u32[]{:S(2)}) collective-permute-start(bf16[4,4,128,128]{3,2,1,0:T(8,128)(2,1)S(1)} %collective-permute-done.7.refs_1_), channel_id=1, source_target_pairs={{8,0},{9,1},{10,2},{11,3},{12,4},{13,5},{14,6},{15,7},{16,8},{17,9... | collective-permute-start | bytes 1572872 | tf_op jit(solution)/shard_map/ppermute | solution.py:194
  61.5 33.5 %collective-permute-start.11 = (bf16[2,4,4,128,128]{4,3,2,1,0:T(8,128)(2,1)S(1)}, bf16[2,4,4,128,128]{4,3,2,1,0:T(8,128)(2,1)S(1)}, u32[]{:S(2)}, u32[]{:S(2)}) collective-permute-start(bf16[2,4,4,128,128]{4,3,2,1,0:T(8,128)(2,1)S(1)} %collective-permute-done.3.refs_0_), channel_id=1, source_target_pairs={{8,0},{9,1},{10,2},{11,3},{12,4},{13,5},{14,6},{15,7},{16,8},{17,9... | collective-permute-start | bytes 3145736 | tf_op jit(solution)/shard_map/ppermute | solution.py:194
  62.8 33.5 %collective-permute-start.4 = (bf16[2,4,4,128,128]{4,3,2,1,0:T(8,128)(2,1)S(1)}, bf16[2,4,4,128,128]{4,3,2,1,0:T(8,128)(2,1)S(1)}, u32[]{:S(2)}, u32[]{:S(2)}) collective-permute-start(bf16[2,4,4,128,128]{4,3,2,1,0:T(8,128)(2,1)S(1)} %collective-permute-done.3.refs_0_), channel_id=1, source_target_pairs={{0,8},{1,9},{2,10},{3,11},{4,12},{5,13},{6,14},{7,15},{8,16},{9,17... | collective-permute-start | bytes 3145736 | tf_op jit(solution)/shard_map/ppermute | solution.py:194
  67.5 17.3 %collective-permute-start.8 = (bf16[4,4,128,128]{3,2,1,0:T(8,128)(2,1)S(1)}, bf16[4,4,128,128]{3,2,1,0:T(8,128)(2,1)}, u32[]{:S(2)}, u32[]{:S(2)}) collective-permute-start(bf16[4,4,128,128]{3,2,1,0:T(8,128)(2,1)S(1)} %collective-permute-done.7.refs_1_), channel_id=1, source_target_pairs={{0,8},{1,9},{2,10},{3,11},{4,12},{5,13},{6,14},{7,15},{8,16},{9,17... | collective-permute-start | bytes 1572872 | tf_op jit(solution)/shard_map/ppermute | solution.py:194
  71.7 0.8 copy-start
  76.2 44.0 %collective-permute-start.2 = (bf16[3,4,4,128,128]{4,3,2,1,0:T(8,128)(2,1)}, bf16[3,4,4,128,128]{4,3,2,1,0:T(8,128)(2,1)}, u32[]{:S(2)}, u32[]{:S(2)}) collective-permute-start(bf16[3,4,4,128,128]{4,3,2,1,0:T(8,128)(2,1)} %get-tuple-element.7), channel_id=1, source_target_pairs={{0,2},{1,3},{2,0},{3,1},{4,6},{5,7},{6,4},{7,5},{8,10},{9,11},{10,... | collective-permute-start | bytes 4718600 | tf_op jit(solution)/shard_map/ppermute | solution.py:194
  77.5 63.5 %collective-permute-start.1 = (bf16[3,4,4,128,128]{4,3,2,1,0:T(8,128)(2,1)}, bf16[3,4,4,128,128]{4,3,2,1,0:T(8,128)(2,1)}, u32[]{:S(2)}, u32[]{:S(2)}) collective-permute-start(bf16[3,4,4,128,128]{4,3,2,1,0:T(8,128)(2,1)} %collective-permute-done), channel_id=1, source_target_pairs={{0,2},{1,3},{2,0},{3,1},{4,6},{5,7},{6,4},{7,5},{8,10},{9,11},{10,... | collective-permute-start | bytes 4718600 | tf_op jit(solution)/shard_map/ppermute | solution.py:194
  84.8 31.7 %collective-permute-start.15 = (bf16[4,4,128,128]{3,2,1,0:T(8,128)(2,1)S(1)}, bf16[4,4,128,128]{3,2,1,0:T(8,128)(2,1)S(1)}, u32[]{:S(2)}, u32[]{:S(2)}) collective-permute-start(bf16[4,4,128,128]{3,2,1,0:T(8,128)(2,1)S(1)} %collective-permute-done.14.refs_5_), channel_id=1, source_target_pairs={{8,0},{9,1},{10,2},{11,3},{12,4},{13,5},{14,6},{15,7},{16,8},{17,9... | collective-permute-start | bytes 1572872 | tf_op jit(solution)/shard_map/ppermute | solution.py:194
  86.1 0.8 copy-start.2
  95.0 44.0 %collective-permute-start.12 = (bf16[2,4,4,128,128]{4,3,2,1,0:T(8,128)(2,1)S(1)}, bf16[2,4,4,128,128]{4,3,2,1,0:T(8,128)(2,1)}, u32[]{:S(2)}, u32[]{:S(2)}) collective-permute-start(bf16[2,4,4,128,128]{4,3,2,1,0:T(8,128)(2,1)S(1)} %collective-permute-done.11.refs_4_), channel_id=1, source_target_pairs={{8,0},{9,1},{10,2},{11,3},{12,4},{13,5},{14,6},{15,7},{16,8},{17,9... | collective-permute-start | bytes 3145736 | tf_op jit(solution)/shard_map/ppermute | solution.py:194
  96.3 44.0 %collective-permute-start.5 = (bf16[2,4,4,128,128]{4,3,2,1,0:T(8,128)(2,1)S(1)}, bf16[2,4,4,128,128]{4,3,2,1,0:T(8,128)(2,1)}, u32[]{:S(2)}, u32[]{:S(2)}) collective-permute-start(bf16[2,4,4,128,128]{4,3,2,1,0:T(8,128)(2,1)S(1)} %collective-permute-done.4.refs_2_), channel_id=1, source_target_pairs={{8,16},{9,17},{10,18},{11,19},{12,20},{13,21},{14,22},{15,23},{16,... | collective-permute-start | bytes 3145736 | tf_op jit(solution)/shard_map/ppermute | solution.py:194
  116.5 0.8 copy-start.4
  117.3 2.2 %collective-permute-start.9 = (bf16[4,4,128,128]{3,2,1,0:T(8,128)(2,1)}, bf16[4,4,128,128]{3,2,1,0:T(8,128)(2,1)}, u32[]{:S(2)}, u32[]{:S(2)}) collective-permute-start(bf16[4,4,128,128]{3,2,1,0:T(8,128)(2,1)} %collective-permute-done.8.refs_3_), channel_id=1, source_target_pairs={{8,16},{9,17},{10,18},{11,19},{12,20},{13,21},{14,22},{15,23},{16,... | collective-permute-start | bytes 1572872 | tf_op jit(solution)/shard_map/ppermute | solution.py:194
  119.5 39.6 %collective-permute-start.10 = (bf16[4,4,128,128]{3,2,1,0:T(8,128)(2,1)}, bf16[4,4,128,128]{3,2,1,0:T(8,128)(2,1)S(1)}, u32[]{:S(2)}, u32[]{:S(2)}) collective-permute-start(bf16[4,4,128,128]{3,2,1,0:T(8,128)(2,1)} %collective-permute-done.9.refs_7_), channel_id=1, source_target_pairs={{16,24},{17,25},{18,26},{19,27},{20,28},{21,29},{22,30},{23,31}} | collective-permute-start | bytes 1572872 | tf_op jit(solution)/shard_map/ppermute | solution.py:194
  120.2 38.9 %collective-permute-start.16 = (bf16[4,4,128,128]{3,2,1,0:T(8,128)(2,1)}, bf16[4,4,128,128]{3,2,1,0:T(8,128)(2,1)S(1)}, u32[]{:S(2)}, u32[]{:S(2)}) collective-permute-start(bf16[4,4,128,128]{3,2,1,0:T(8,128)(2,1)} %copy-done.4), channel_id=1, source_target_pairs={{8,0},{9,1},{10,2},{11,3},{12,4},{13,5},{14,6},{15,7}} | collective-permute-start | bytes 1572872 | tf_op jit(solution)/shard_map/ppermute | solution.py:194
  139.0 20.2 %collective-permute-start.13 = (bf16[2,4,4,128,128]{4,3,2,1,0:T(8,128)(2,1)}, bf16[2,4,4,128,128]{4,3,2,1,0:T(8,128)(2,1)S(1)}, u32[]{:S(2)}, u32[]{:S(2)}) collective-permute-start(bf16[2,4,4,128,128]{4,3,2,1,0:T(8,128)(2,1)} %collective-permute-done.12.refs_8_), channel_id=1, source_target_pairs={{8,0},{9,1},{10,2},{11,3},{12,4},{13,5},{14,6},{15,7}} | collective-permute-start | bytes 3145736 | tf_op jit(solution)/shard_map/ppermute | solution.py:194
  140.3 18.9 %collective-permute-start.6 = (bf16[2,4,4,128,128]{4,3,2,1,0:T(8,128)(2,1)}, bf16[2,4,4,128,128]{4,3,2,1,0:T(8,128)(2,1)S(1)}, u32[]{:S(2)}, u32[]{:S(2)}) collective-permute-start(bf16[2,4,4,128,128]{4,3,2,1,0:T(8,128)(2,1)} %collective-permute-done.5.refs_6_), channel_id=1, source_target_pairs={{16,24},{17,25},{18,26},{19,27},{20,28},{21,29},{22,30},{23,31}} | collective-permute-start | bytes 3145736 | tf_op jit(solution)/shard_map/ppermute | solution.py:194
  145.3 2.6 %copy-start.1 = (bf16[4,4,128,128]{3,2,1,0:T(8,128)(2,1)S(1)}, bf16[4,4,128,128]{3,2,1,0:T(8,128)(2,1)}, u32[]{:S(2)}) copy-start(bf16[4,4,128,128]{3,2,1,0:T(8,128)(2,1)} %copy-done) | copy-start | bytes 1572868
  145.3 2.6 %copy-start.3 = (bf16[4,4,128,128]{3,2,1,0:T(8,128)(2,1)S(1)}, bf16[4,4,128,128]{3,2,1,0:T(8,128)(2,1)}, u32[]{:S(2)}) copy-start(bf16[4,4,128,128]{3,2,1,0:T(8,128)(2,1)} %copy-done.2) | copy-start | bytes 1572868
  145.3 2.6 %copy-start.5 = (bf16[4,4,128,128]{3,2,1,0:T(8,128)(2,1)S(1)}, bf16[4,4,128,128]{3,2,1,0:T(8,128)(2,1)}, u32[]{:S(2)}) copy-start(bf16[4,4,128,128]{3,2,1,0:T(8,128)(2,1)} %copy-done.4) | copy-start | bytes 1572868
  164.5 4.2 %collective-permute-start.17 = (f32[2,4,4,128,128]{4,3,2,1,0:T(8,128)S(1)}, f32[2,4,4,128,128]{4,3,2,1,0:T(8,128)S(1)}, u32[]{:S(2)}, u32[]{:S(2)}) collective-permute-start(f32[2,4,4,128,128]{4,3,2,1,0:T(8,128)S(1)} %slice_bitcast_fusion), channel_id=1, source_target_pairs={{0,1},{1,0},{2,3},{3,2},{4,5},{5,4},{6,7},{7,6},{8,9},{9,8},{10,11... | collective-permute-start | bytes 6291464 | tf_op jit(solution)/shard_map/ppermute | solution.py:194
  169.1 16.1 %collective-permute-start.18 = (bf16[2,4,4,128,128]{4,3,2,1,0:T(8,128)(2,1)S(1)}, bf16[2,4,4,128,128]{4,3,2,1,0:T(8,128)(2,1)S(1)}, u32[]{:S(2)}, u32[]{:S(2)}) collective-permute-start(bf16[2,4,4,128,128]{4,3,2,1,0:T(8,128)(2,1)S(1)} %fusion.1), channel_id=1, source_target_pairs={{0,0},{1,4},{2,2},{3,6},{4,1},{5,5},{6,3},{7,7},{8,8},{9,12},{10,1... | collective-permute-start | bytes 3145736 | tf_op jit(solution)/shard_map/ppermute | solution.py:194

commit v2 on v0

v2 whole, which is shorter than its diff:
```python
import functools
import itertools

import jax
import jax.numpy as jnp
import numpy as np
from jax import lax
from jax.experimental import pallas as pl
from jax.experimental.pallas import tpu as pltpu
from jax.sharding import PartitionSpec as P

H, Q, D = 0, 1, 2
AXES = ("row", "col")


class Plan:
    def __init__(self, row_count, col_count, rows_dev, slot_count):
        self.R, self.C, self.M, self.S = row_count, col_count, rows_dev, slot_count
        self.Z, self.Y = row_count // 2, col_count // 2
        self.K = slot_count * col_count
        self.half = self.K // 2
        self.nb = -(-self.K // self.R)
        reach = (self.half + 1) // 2
        Z = self.Z
        ring = 2 * reach + 1 <= Z
        self.quad = Z == 4 and not ring
        if self.quad:
            inward, middle, outward = [(0, 1), (3, 2)], [(1, 2), (2, 1)], [(1, 0), (2, 3)]
            self.hops = [
                ("mid", "own", middle), ("out1", "own", outward), ("in", "own", inward),
                ("mid2", "in", middle), ("out2", "mid", outward), ("out3", "mid2", outward),
            ]
        else:
            self.hops = []
            for step in range(1, (reach if ring else Z - 1) + 1):
                for name, way in (("up", 1), ("down", -1)):
                    ends = [(z, z + way) for z in range(Z)]
                    ends = [(z, to % Z) for z, to in ends if ring or 0 <= to < Z and 0 <= z - way * (step - 1) < Z]
                    self.hops.append((name + str(step), name + str(step - 1) if step > 1 else "own", ends))
        self.origin = {"own": {z: z for z in range(Z)}}
        for name, source, ends in self.hops:
            self.origin[name] = {to: self.origin[source][z] for z, to in ends}
        self.units = list(self.origin)

    def pairs(self, target, planes=None):
        found = []
        for z in range(self.Z) if planes is None else planes:
            for x in range(2):
                for y in range(self.Y):
                    for k in range(2):
                        to = target(z, x, y, k)
                        if to is not None:
                            tz, tx, ty, tk = to
                            found.append(
                                ((2 * z + x) * self.C + 2 * y + k, (2 * tz + tx) * self.C + 2 * ty + tk)
                            )
        return found

    def along_z(self, ends):
        ends = dict(ends)
        return self.pairs(lambda z, x, y, k: (ends[z], x, y, k) if z in ends else None)

    def table(self):
        R, C, M, Y = self.R, self.C, self.M, self.Y
        out = np.zeros((R, C, len(self.units) + 1, 2 + 2 * self.nb * 4), np.int32)
        for r in range(R):
            for c in range(C):
                z, x, y, k = r // 2, r % 2, c // 2, c % 2
                out[r, c, -1, 0] = x != k
                for u, unit in enumerate(self.units):
                    if z not in self.origin[unit]:
                        continue
                    there = self.origin[unit][z]
                    out[r, c, u, 0] = 1
                    out[r, c, u, 1] = (there % Y - y) % Y
                    for e in range(2):
                        rho = k ^ e
                        base = 2 * (there - z) + k - rho
                        phase = (2 * y + x - 2 * z - rho + self.half) % C
                        first = -((self.half + base) // R)
                        for n in range(self.nb):
                            w = first + n
                            b = base + R * w
                            ok = -self.half <= b < self.half
                            at = 2 + (e * self.nb + n) * 4
                            out[r, c, u, at:at + 4] = (
                                ((b + self.half) // C if ok else 0),
                                w % M,
                                (phase - b) // C,
                                ok,
                            )
        return out


def right_side(plan, terms, m, block_at):
    S, M = plan.S, plan.M
    parts = []
    for n, (_, row_shift, slot_shift, ok) in enumerate(terms):
        row = lax.rem(m + row_shift, M)
        cols = []
        for s in range(S):
            slot = s + slot_shift
            inside = jnp.logical_and(ok == 1, jnp.logical_and(slot >= 0, slot < S))
            block = block_at(n, row, jnp.clip(slot, 0, S - 1))
            cols.append(jnp.where(inside, block, jnp.zeros_like(block)))
        parts.append(jnp.concatenate(cols, axis=1))
    return jnp.concatenate(parts, axis=0)


def terms_of(plan, tab, unit, e):
    at = 2 + e * plan.nb * 4
    return [tuple(tab[unit, at + 4 * n + i] for i in range(4)) for n in range(plan.nb)]


def contract_body(plan, wanted, kinds, spans, tab, *refs):
    low, high = (0 if H in kinds else 1), (3 if D in kinds else 2)
    data, refs = refs[:len(spans)], refs[len(spans):]
    total_refs, (held, rows, sem, row_sem) = refs[:2], refs[2:]
    S, M, Y = plan.S, plan.M, plan.Y
    B = held.shape[-1]
    swapped = tab[len(plan.units), 0]
    valid = [tab[unit, 0] == 1 for unit in wanted]
    some = functools.reduce(jnp.logical_or, valid)

    def copies(use, into, into_sem):
        for i, (what, a, b) in enumerate(spans):
            a, b, first = max(a, low), min(b, high), a
            if what == use and a < b:
                yield pltpu.make_async_copy(
                    data[i].at[pl.ds(a - first, b - a)], into.at[pl.ds(a - low, b - a)], into_sem.at[a - low]
                )

    def unit_copies(u):
        return copies(("unit", u), held.at[u], sem.at[u])

    for flip in range(2):
        @pl.when(jnp.logical_and(some, swapped == flip))
        def _(flip=flip):
            for side, dy in itertools.product(range(2), range(Y)):
                into = (side ^ flip, dy)
                for copy in copies(("rows", side, dy), rows.at[into], row_sem.at[into]):
                    copy.start()
    for u in range(len(wanted)):
        @pl.when(valid[u])
        def _(u=u):
            for copy in unit_copies(u):
                copy.start()

    for total_ref in total_refs:
        total_ref[...] = jnp.zeros_like(total_ref)

    for flip in range(2):
        @pl.when(jnp.logical_and(some, swapped == flip))
        def _(flip=flip):
            for side, dy in itertools.product(range(2), range(Y)):
                into = (side ^ flip, dy)
                for copy in copies(("rows", side, dy), rows.at[into], row_sem.at[into]):
                    copy.wait()

    for u, unit in enumerate(wanted):
        @pl.when(valid[u])
        def _(u=u, unit=unit):
            for copy in unit_copies(u):
                copy.wait()
            dy = tab[unit, 1]
            for e in range(2):
                terms = terms_of(plan, tab, unit, e)

                @pl.loop(0, M, unroll=True)
                def _(m, e=e, terms=terms):
                    def left(mat):
                        return jnp.concatenate([rows[e, dy, mat - low, m, slot] for slot, _, _, _ in terms], axis=1)

                    def right(mat):
                        return right_side(plan, terms, m, lambda n, row, slot: held[u, mat - low, row, slot])

                    dot = functools.partial(jnp.dot, preferred_element_type=jnp.float32)
                    both = dot(jnp.concatenate([left(kind) for kind in kinds], axis=0), right(Q))
                    mine = left(Q)
                    for i, kind in enumerate(kinds):
                        there, back = both[i * B:(i + 1) * B], dot(mine, right(kind))
                        sums = there - back if kind == H else there + back
                        for s in range(S):
                            total_refs[e][i, m, s] += sums[:, s * B:(s + 1) * B]


def contract(plan, tab, near, far, wanted, kinds, got):
    M, S, Y = plan.M, plan.S, plan.Y
    operands, spans = [], []
    for u, unit in enumerate(wanted):
        for array, first in got[unit]:
            operands.append(array)
            spans.append((("unit", u), first, first + array.shape[0]))
    for side, lists in enumerate((near, far)):
        for dy, pieces in enumerate(lists):
            for array, first in pieces:
                operands.append(array)
                spans.append((("rows", side, dy), first, first + array.shape[0]))
    B, kind_of = operands[0].shape[-1], operands[0].dtype
    mats = 1 + len(kinds)
    specs = [pl.BlockSpec(memory_space=pl.ANY)] * len(operands)
    whole = pl.BlockSpec(memory_space=pltpu.VMEM)
    terms = 2 * M * min(len(wanted), plan.Z) * plan.nb * S * 2 * len(kinds)
    return pl.pallas_call(
        functools.partial(
            contract_body, plan, tuple(plan.units.index(unit) for unit in wanted), kinds, tuple(spans)
        ),
        in_specs=[pl.BlockSpec(memory_space=pltpu.SMEM)] + specs,
        out_specs=[whole] * 2,
        scratch_shapes=[
            pltpu.VMEM((len(wanted), mats, M, S, B, B), kind_of),
            pltpu.VMEM((2, Y, mats, M, S, B, B), kind_of),
            pltpu.SemaphoreType.DMA((len(wanted), mats)),
            pltpu.SemaphoreType.DMA((2, Y, mats)),
        ],
        out_shape=[jax.ShapeDtypeStruct((len(kinds), M, S, B, B), jnp.float32)] * 2,
        compiler_params=pltpu.CompilerParams(vmem_limit_bytes=58 * 2**20),
        cost_estimate=pl.CostEstimate(
            flops=6 * B**3 * terms,
            bytes_accessed=len(spans) * M * S * B * B * 2,
            transcendentals=0,
        ),
    )(tab, *operands)


def find(pieces, mat):
    for ref, first in pieces:
        if first <= mat < first + ref.shape[0]:
            return ref, mat - first


def last_body(plan, kind, firsts, tab, kept, given, *refs):
    data, (kept_out, given_out, rows, held, sem) = refs[:-5], refs[-5:]
    S, M, Y, nb = plan.S, plan.M, plan.Y, plan.nb
    B = held.shape[-1]
    unit = len(plan.units) - 1
    valid = tab[unit, 0] == 1
    swapped = tab[unit + 1, 0]
    terms = [terms_of(plan, tab, unit, e) for e in range(2)]
    totals = kept_out, given_out
    places = {}
    for at, (name, first) in enumerate(firsts):
        places.setdefault(name, []).append((data[at], first))

    def base_copies():
        for i, ref in enumerate((kept, given)):
            yield pltpu.make_async_copy(ref.at[kind // 2], totals[i], sem.at[0, i, 0])

    def unit_copies():
        for i, mat in enumerate((kind, Q)):
            ref, index = find(places["unit"], mat)
            yield pltpu.make_async_copy(ref.at[index], held.at[i], sem.at[0, i, 1])

    def row_copies(e, pieces):
        for i, mat in enumerate((kind, Q)):
            ref, index = find(pieces, mat)
            for n in range(nb):
                yield pltpu.make_async_copy(ref.at[index, :, terms[e][n][0]], rows.at[e, i, n], sem.at[1 + e, i, n])

    def fetch(verb):
        @pl.when(valid)
        def _():
            for copy in unit_copies():
                verb(copy)

        for flip, dy in itertools.product(range(2), range(Y)):
            @pl.when(jnp.logical_and(valid, jnp.logical_and(swapped == flip, tab[unit, 1] == dy)))
            def _(flip=flip, dy=dy):
                for side in range(2):
                    for copy in row_copies(side ^ flip, places["rows", side, dy]):
                        verb(copy)

        for copy in base_copies():
            verb(copy)

    fetch(lambda copy: copy.start())
    fetch(lambda copy: copy.wait())

    @pl.when(valid)
    def _():
        for e in (1, 0):
            @pl.loop(0, M, unroll=True)
            def _(m, e=e):
                def left(i):
                    return jnp.concatenate([rows[e, i, n, m] for n in range(nb)], axis=1)

                def right(i):
                    return right_side(plan, terms[e], m, lambda n, row, slot: held[i, row, slot])

                dot = functools.partial(jnp.dot, preferred_element_type=jnp.float32)
                there, back = dot(left(0), right(1)), dot(left(1), right(0))
                more = there - back if kind == H else there + back
                for s in range(S):
                    totals[e][m, s] += more[:, s * B:(s + 1) * B]


def last(plan, tab, kind, kept, given, near, far, unit):
    M, S, Y, nb = plan.M, plan.S, plan.Y, plan.nb
    lists = [("unit", unit)]
    lists += [(("rows", side, dy), pieces) for side, sides in enumerate((near, far)) for dy, pieces in enumerate(sides)]
    firsts = tuple((name, first) for name, pieces in lists for _, first in pieces)
    operands = [array for _, pieces in lists for array, _ in pieces]
    B = kept.shape[-1]
    return pl.pallas_call(
        functools.partial(last_body, plan, kind, firsts),
        in_specs=[pl.BlockSpec(memory_space=pltpu.SMEM)] + [pl.BlockSpec(memory_space=pl.ANY)] * (2 + len(operands)),
        out_specs=[pl.BlockSpec(memory_space=pltpu.VMEM)] * 2,
        scratch_shapes=[
            pltpu.VMEM((2, 2, nb, M, B, B), operands[0].dtype),
            pltpu.VMEM((2, M, S, B, B), operands[0].dtype),
            pltpu.SemaphoreType.DMA((3, 2, max(nb, 2))),
        ],
        out_shape=[jax.ShapeDtypeStruct((M, S, B, B), jnp.float32)] * 2,
        compiler_params=pltpu.CompilerParams(vmem_limit_bytes=58 * 2**20),
        cost_estimate=pl.CostEstimate(flops=4 * 10**10, bytes_accessed=8 * 2**20, transcendentals=0),
    )(tab, kept, given, *operands)


def keep_body(*refs):
    count = len(refs) // 2
    masks, values, out = refs[:count], refs[count:-1], refs[-1]
    m = pl.program_id(0)
    for i, value in enumerate(values):
        for s in range(value.shape[2]):
            block = value[0, 0, s]
            out[i, 0, s] = jnp.where(masks[i][m, 0, s] != 0, block, jnp.zeros_like(block))


def keep(values, masks):
    M, _, S, B, _ = values[0].shape
    return pl.pallas_call(
        keep_body,
        grid=(M,),
        in_specs=[pl.BlockSpec(memory_space=pltpu.SMEM)] * len(masks)
        + [pl.BlockSpec((1, 1, S, B, B), lambda m: (m, 0, 0, 0, 0))] * len(values),
        out_specs=pl.BlockSpec((len(values), 1, S, B, B), lambda m: (0, m, 0, 0, 0)),
        out_shape=jax.ShapeDtypeStruct((len(values), M, S, B, B), values[0].dtype),
    )(*masks, *values)


def tick_body(token, out):
    out[...] = token[...]


def tick(token, *done, cost=2 * 10**10):
    token = lax.optimization_barrier((token, *done))[0]
    return pl.pallas_call(
        tick_body,
        out_shape=jax.ShapeDtypeStruct(token.shape, token.dtype),
        cost_estimate=pl.CostEstimate(flops=cost, bytes_accessed=0, transcendentals=0),
    )(token)


def move(value, pairs):
    return lax.ppermute(value, AXES, pairs)


def after(value, *others):
    return lax.optimization_barrier((value, *others))[0]


def per_device(plan, h_blocks, p_blocks, p1_blocks, h_mask, p_mask, p1_mask):
    row, col = lax.axis_index("row"), lax.axis_index("col")
    tab = jnp.asarray(plan.table())[row, col]
    mine = keep((h_blocks, p1_blocks, p_blocks), (h_mask, p1_mask, p_mask))
    pattern = p1_mask[:, 0][:, :, None, None].astype(jnp.bfloat16)

    cross = plan.pairs(lambda z, x, y, k: (z, k, y, x))
    sibling = plan.pairs(lambda z, x, y, k: (z, x, y, 1 - k))
    x_swap = plan.pairs(lambda z, x, y, k: (z, 1 - x, y, k))
    x_pairs = plan.pairs(lambda z, x, y, k: (z, 1 - x, y, k) if x == k else (z, x, y, 1 - k))
    y_pairs = [plan.pairs(lambda z, x, y, k: (z, x, (y - dy) % plan.Y, k)) for dy in range(1, plan.Y)]

    unit = move(mine, cross)
    hops = {name: (source, plan.along_z(ends)) for name, source, ends in plan.hops}
    if not plan.quad:
        got = {"own": unit}
        for name, (source, pairs) in hops.items():
            got[name] = move(got[source], pairs)
        across = move(unit, x_pairs)
        near = [[(mine, 0)]] + [[(move(mine, pairs), 0)] for pairs in y_pairs]
        far = [[(across, 0)]] + [[(move(across, pairs), 0)] for pairs in y_pairs]
        got = {name: [(value, 0)] for name, value in got.items()}
        kept, given = contract(plan, tab, near, far, plan.units, (H, D), got)
        results = move((kept + move(given, sibling)).astype(jnp.bfloat16), cross)
        return tuple((result * pattern)[:, None] for result in results)

    token = jnp.zeros((8, 128), jnp.float32)
    flight = [unit]
    got = {"own": {Q: unit[1:], H: unit[:1]}}

    def along(names, part):
        for name in names:
            source, pairs = hops[name]
            got.setdefault(name, {})[part] = sent(got[source][part], pairs)

    def sent(value, pairs):
        result = move(after(value, token), pairs)
        group.append(result)
        return result

    def closed():
        return tick(token, *flight), group, []

    group = []
    along(("mid", "out1", "in"), Q)
    token, flight, group = closed()
    along(("mid", "out1", "in"), H)
    beside = [sent(mine, pairs) for pairs in y_pairs]
    across = sent(unit, x_pairs)
    token, flight, group = closed()
    along(("mid2", "out2"), Q)
    token, flight, group = closed()
    along(("mid2", "out2"), H)
    far_qd = [sent(across[1:], pairs) for pairs in y_pairs]
    far_h = [sent(value[:1], x_swap) for value in beside]
    token, flight, group = closed()
    along(("out3",), Q)
    token, flight, group = closed()
    along(("out3",), H)

    near = [[(mine, H)]] + [[(value, H)] for value in beside]
    far = [[(across, H)]] + [[(a, H), (b, Q)] for a, b in zip(far_h, far_qd)]
    early = ["own", "in", "mid", "out1", "mid2", "out2"]
    pieces = {name: [(parts[H], H), (parts[Q], Q)] for name, parts in got.items()}
    kept, given = contract(plan, after(tab, token), near, far, early, (H, D), pieces)
    own, lent = last(plan, tab, D, kept, given, near, far, pieces["out3"][1:])
    response = own, move(lent, sibling)
    own, lent = last(plan, after(tab, own), H, kept, given, near, far, pieces["out3"])
    commutator = own, move(lent, sibling)
    results = [move((own + lent).astype(jnp.bfloat16), cross) for own, lent in (response, commutator)]
    response, commutator = [(result * pattern)[:, None] for result in results]
    return commutator, response


def solution(mesh):
    blocks = P(None, "row", "col", None, None)
    masks = P(None, "row", "col")

    def run(h_blocks, p_blocks, p1_blocks, h_mask, p_mask, p1_mask):
        plan = Plan(
            mesh.shape["row"], mesh.shape["col"], h_blocks.shape[0], h_blocks.shape[2] // mesh.shape["col"]
        )
        return jax.shard_map(
            functools.partial(per_device, plan),
            mesh=mesh,
            in_specs=(blocks,) * 3 + (masks,) * 3,
            out_specs=(blocks,) * 2,
            check_vma=False,
        )(h_blocks, p_blocks, p1_blocks, h_mask, p_mask, p1_mask)

    return run
```

time: 345 us -> 153 us (0.44); the launches traced: 338 us -> 153 us
  waiting for transfers between devices: 172 us -> 81.5 us
  local copies, waits for them, and re-layouts: 88 us -> 3.4 us
  starting transfers between devices: 0.08 us -> 38.3 us
  matrix products: 38.2 us -> 0 us
  Pallas kernels: 0 us -> 25.8 us
  other arithmetic: 21.3 us -> 2.57 us
  between operations: 17.8 us -> 1.02 us
    all_gather x1 -> x0, waiting for transfers between devices: 172 us -> none  [per_device(): lax.all_gather(own_blocks[:, :, None], 'row', axis=2, tiled=True)]
    ppermute x0 -> x21, waiting for transfers between devices: none -> 81.5 us  [move(): return lax.ppermute(value, AXES, pairs)]
    unnamed x194 -> x37, local copies, waits for them, and re-layouts: 69.4 us -> 1.87 us
    ppermute x0 -> x21, starting transfers between devices: none -> 38.3 us  [move(): return lax.ppermute(value, AXES, pairs)]
    dot_general x64 -> x0, matrix products: 38.2 us -> none  [block_product(): jnp.einsum('mij,mkjl->mkil', left_operand, right_operand, preferred_eleme...]
    pallas_call x0 -> x4, Pallas kernels: none -> 25.8 us  [the longest x1 11.3 us: contract(): pl.pallas_call(functools.partial(contract_body, plan, tuple((plan.units.i...]
    dynamic_slice x1 -> x0, local copies, waits for them, and re-layouts: 18.3 us -> none  [per_device(): lax.dynamic_index_in_dim(everything, device, axis=2, keepdims=False)]
    concatenate x16 -> x0, other arithmetic: 12.1 us -> none  [per_device(): rolled = jnp.roll(fetched, -row_carry, axis=1)]
  transfers between devices with their start and end apart: 2 -> 21, of which waited for: 1 -> 15; matrix products, arithmetic and copies ran while one was open for 7% -> 2% of each run, Pallas kernels for 0% -> 11%
where the time goes in v2:
time: 153 us
  waiting for transfers between devices  81.5 us (53%)
  starting transfers between devices  38.3 us (25%)
  Pallas kernels  25.8 us (17%)
  local copies, waits for them, and re-layouts  3.4 us (2%)
  other arithmetic  2.57 us (2%)
    ppermute x21, waiting for transfers between devices, move(): return lax.ppermute(value, AXES, pairs)  81.5 us
    ppermute x21, starting transfers between devices, move(): return lax.ppermute(value, AXES, pairs)  38.3 us
    pallas_call x1, Pallas kernels, contract(): pl.pallas_call(functools.partial(contract_body, plan, tuple((plan.units.i...  11.3 us
    pallas_call x2, Pallas kernels, last(): pl.pallas_call(functools.partial(last_body, plan, kind, firsts), in_specs...  10.6 us
    pallas_call x1, Pallas kernels, keep(): pl.pallas_call(keep_body, grid=(M,), in_specs=[pl.BlockSpec(memory_space=...  3.83 us
  transfers between devices with their start and end apart: 21, of which 15 were waited for; matrix products, arithmetic and copies ran while one was open for 2% of the time, Pallas kernels for 11%

profile of v2, /device:TPU:1, one launch (start us, length us, event | category | flops | bytes accessed | tf_op | source)
XLA Modules:
  0.0 152.6 jit_solution(14060354799060045060)
XLA Ops:
  0.6 3.8 %shard_map.86.refs_12_.refs_1_.refs_2_ = bf16[3,4,4,128,128]{4,3,2,1,0:T(8,128)(2,1)} custom-call(s32[4,1,4]{2,1,0:T(1,128)} %refs_0_.1, s32[4,1,4]{2,1,0:T(1,128)} %refs_1_.1, s32[4,1,4]{2,1,0:T(1,128)} %refs_2_.1, bf16[4,1,4,128,128]{4,3,2,1,0:T(8,128)(2,1)} %refs_3_.1, bf16[4,1,4,128,128]{4,3,2,1,0:T(8,128)(2,1)} %refs_4_.1, ...), custom_call_target="tpu_custom_call" | custom-call | tf_op jit(solution)/shard_map/pallas_call | solution.py:331
  4.5 4.5 %collective-permute-start = (bf16[3,4,4,128,128]{4,3,2,1,0:T(8,128)(2,1)}, bf16[3,4,4,128,128]{4,3,2,1,0:T(8,128)(2,1)S(1)}, u32[]{:S(2)}, u32[]{:S(2)}) collective-permute-start(bf16[3,4,4,128,128]{4,3,2,1,0:T(8,128)(2,1)} %shard_map.86.refs_12_.refs_1_.refs_2_), channel_id=1, source_target_pairs={{0,0},{1,4},{2,2},{3,6},{4,1},{5,5},{6,3},{7,7},{8,8},{9,12},{10,1... | collective-permute-start | bytes 4718600 | tf_op jit(solution)/shard_map/ppermute | solution.py:355
  9.0 1.3 dynamic-slice_bitcast_fusion.tab
  10.3 17.4 %collective-permute-done = bf16[3,4,4,128,128]{4,3,2,1,0:T(8,128)(2,1)S(1)} collective-permute-done((bf16[3,4,4,128,128]{4,3,2,1,0:T(8,128)(2,1)}, bf16[3,4,4,128,128]{4,3,2,1,0:T(8,128)(2,1)S(1)}, u32[]{:S(2)}, u32[]{:S(2)}) %collective-permute-start) | collective-permute-done | bytes 1572896 | tf_op jit(solution)/shard_map/ppermute | solution.py:355
  27.7 0.1 slice.16.refs_1_
  27.7 3.2 %collective-permute-start.3 = (bf16[2,4,4,128,128]{4,3,2,1,0:T(8,128)(2,1)S(1)}, bf16[2,4,4,128,128]{4,3,2,1,0:T(8,128)(2,1)S(1)}, u32[]{:S(2)}, u32[]{:S(2)}) collective-permute-start(bf16[2,4,4,128,128]{4,3,2,1,0:T(8,128)(2,1)S(1)} %slice.16.refs_1_), channel_id=1, source_target_pairs={{0,8},{1,9},{2,10},{3,11},{4,12},{5,13},{6,14},{7,15},{24,16},{25,... | collective-permute-start | bytes 3145736 | tf_op jit(solution)/shard_map/ppermute | solution.py:355
  30.9 1.3 collective-permute-start.2
  32.2 0.7 collective-permute-start.1
  33.0 0.0 copy-start.4
  33.0 7.5 %collective-permute-start.6 = (bf16[1,4,4,128,128]{4,3,2,1,0:T(8,128)(2,1)S(1)}, bf16[1,4,4,128,128]{4,3,2,1,0:T(8,128)(2,1)S(1)}, u32[]{:S(2)}, u32[]{:S(2)}) collective-permute-start(bf16[1,4,4,128,128]{4,3,2,1,0:T(8,128)(2,1)S(1)} %slice.17.refs_0_), channel_id=1, source_target_pairs={{0,8},{1,9},{2,10},{3,11},{4,12},{5,13},{6,14},{7,15},{24,16},{25,... | collective-permute-start | bytes 1572872 | tf_op jit(solution)/shard_map/ppermute | solution.py:355
  40.5 1.3 collective-permute-start.5
  41.8 0.8 collective-permute-done.3.refs_3_
  42.6 0.7 collective-permute-start.4
  43.3 3.5 %collective-permute-done.2.refs_7_ = bf16[2,4,4,128,128]{4,3,2,1,0:T(8,128)(2,1)} collective-permute-done((bf16[2,4,4,128,128]{4,3,2,1,0:T(8,128)(2,1)S(1)}, bf16[2,4,4,128,128]{4,3,2,1,0:T(8,128)(2,1)}, u32[]{:S(2)}, u32[]{:S(2)}) %collective-permute-start.2) | collective-permute-done | bytes 1048608 | tf_op jit(solution)/shard_map/ppermute | solution.py:355
  46.8 1.2 collective-permute-start.7
  48.0 0.2 collective-permute-done.6.refs_2_
  48.2 1.6 %collective-permute-start.9 = (bf16[2,4,4,128,128]{4,3,2,1,0:T(8,128)(2,1)S(1)}, bf16[2,4,4,128,128]{4,3,2,1,0:T(8,128)(2,1)}, u32[]{:S(2)}, u32[]{:S(2)}) collective-permute-start(bf16[2,4,4,128,128]{4,3,2,1,0:T(8,128)(2,1)S(1)} %collective-permute-done.3.refs_3_), channel_id=1, source_target_pairs={{8,16},{9,17},{10,18},{11,19},{12,20},{13,21},{14,22},{15,23},{16,... | collective-permute-start | bytes 3145736 | tf_op jit(solution)/shard_map/ppermute | solution.py:355
  49.8 2.3 %collective-permute-done.5.refs_6_ = bf16[1,4,4,128,128]{4,3,2,1,0:T(8,128)(2,1)} collective-permute-done((bf16[1,4,4,128,128]{4,3,2,1,0:T(8,128)(2,1)S(1)}, bf16[1,4,4,128,128]{4,3,2,1,0:T(8,128)(2,1)}, u32[]{:S(2)}, u32[]{:S(2)}) %collective-permute-start.5) | collective-permute-done | bytes 524320 | tf_op jit(solution)/shard_map/ppermute | solution.py:355
  52.2 1.3 collective-permute-start.10
  53.5 13.3 %collective-permute-done.7.refs_13_.refs_2_.refs_3_ = bf16[3,4,4,128,128]{4,3,2,1,0:T(8,128)(2,1)S(1)} collective-permute-done((bf16[3,4,4,128,128]{4,3,2,1,0:T(8,128)(2,1)S(1)}, bf16[3,4,4,128,128]{4,3,2,1,0:T(8,128)(2,1)S(1)}, u32[]{:S(2)}, u32[]{:S(2)}) %collective-permute-start.7) | collective-permute-done | bytes 1572896 | tf_op jit(solution)/shard_map/ppermute | solution.py:355
  66.8 0.8 collective-permute-done.8.refs_14_.refs_3_.refs_4_
  67.6 1.4 collective-permute-start.11
  69.1 1.3 collective-permute-start.12
  70.4 0.1 collective-permute-start.14
  70.4 0.1 slice.18
  70.6 0.8 collective-permute-start.13
  71.4 4.2 %collective-permute-done.10.refs_11_ = bf16[2,4,4,128,128]{4,3,2,1,0:T(8,128)(2,1)S(1)} collective-permute-done((bf16[2,4,4,128,128]{4,3,2,1,0:T(8,128)(2,1)S(1)}, bf16[2,4,4,128,128]{4,3,2,1,0:T(8,128)(2,1)S(1)}, u32[]{:S(2)}, u32[]{:S(2)}) %collective-permute-start.10) | collective-permute-done | bytes 1048608 | tf_op jit(solution)/shard_map/ppermute | solution.py:355
  75.6 1.3 collective-permute-start.15
  76.9 11.0 %collective-permute-done.12.refs_10_ = bf16[1,4,4,128,128]{4,3,2,1,0:T(8,128)(2,1)S(1)} collective-permute-done((bf16[1,4,4,128,128]{4,3,2,1,0:T(8,128)(2,1)S(1)}, bf16[1,4,4,128,128]{4,3,2,1,0:T(8,128)(2,1)S(1)}, u32[]{:S(2)}, u32[]{:S(2)}) %collective-permute-start.12) | collective-permute-done | bytes 524320 | tf_op jit(solution)/shard_map/ppermute | solution.py:355
  87.9 3.2 %collective-permute-done.13.refs_16_.refs_5_.refs_6_ = bf16[2,4,4,128,128]{4,3,2,1,0:T(8,128)(2,1)S(1)} collective-permute-done((bf16[2,4,4,128,128]{4,3,2,1,0:T(8,128)(2,1)S(1)}, bf16[2,4,4,128,128]{4,3,2,1,0:T(8,128)(2,1)S(1)}, u32[]{:S(2)}, u32[]{:S(2)}) %collective-permute-start.13) | collective-permute-done | bytes 1048608 | tf_op jit(solution)/shard_map/ppermute | solution.py:355
  91.1 1.3 collective-permute-start.16
  92.5 11.3 %shard_map.87 = (f32[2,4,4,128,128]{4,3,2,1,0:T(8,128)}, f32[2,4,4,128,128]{4,3,2,1,0:T(8,128)}) custom-call(s32[8,18]{1,0:T(8,128)} %dynamic-slice_bitcast_fusion.tab, bf16[1,4,4,128,128]{4,3,2,1,0:T(8,128)(2,1)} %copy-done.4, bf16[2,4,4,128,128]{4,3,2,1,0:T(8,128)(2,1)} %copy-done.1, bf16[1,4,4,128,128]{4,3,2,1,0:T(8,128)(2,1)} %copy-done.13, ...), custom_call_target="tpu_custom_call" | custom-call | flops 12884901888 | bytes 8912896 | tf_op jit(solution)/shard_map/pallas_call | solution.py:204
  103.8 6.5 %collective-permute-done.15.refs_0_.refs_1_ = bf16[2,4,4,128,128]{4,3,2,1,0:T(8,128)(2,1)S(1)} collective-permute-done((bf16[2,4,4,128,128]{4,3,2,1,0:T(8,128)(2,1)}, bf16[2,4,4,128,128]{4,3,2,1,0:T(8,128)(2,1)S(1)}, u32[]{:S(2)}, u32[]{:S(2)}) %collective-permute-start.15) | collective-permute-done | bytes 1048608 | tf_op jit(solution)/shard_map/ppermute | solution.py:355
  110.3 1.0 copy-done.11
  111.3 5.3 %shard_map.88 = (f32[4,4,128,128]{3,2,1,0:T(8,128)}, f32[4,4,128,128]{3,2,1,0:T(8,128)}) custom-call(s32[8,18]{1,0:T(8,128)} %dynamic-slice_bitcast_fusion.tab, f32[2,4,4,128,128]{4,3,2,1,0:T(8,128)} %get-tuple-element.43.kept, f32[2,4,4,128,128]{4,3,2,1,0:T(8,128)} %get-tuple-element.44.given, bf16[2,4,4,128,128]{4,3,2,1,0:T(8,128)(2,1)} %copy-done.11, ...), custom_call_target="tpu_custom_call" | custom-call | flops 40000000000 | bytes 8388608 | tf_op jit(solution)/shard_map/pallas_call | solution.py:304
  116.7 4.9 %collective-permute-done.16.refs_0_ = bf16[1,4,4,128,128]{4,3,2,1,0:T(8,128)(2,1)S(1)} collective-permute-done((bf16[1,4,4,128,128]{4,3,2,1,0:T(8,128)(2,1)}, bf16[1,4,4,128,128]{4,3,2,1,0:T(8,128)(2,1)S(1)}, u32[]{:S(2)}, u32[]{:S(2)}) %collective-permute-start.16) | collective-permute-done | bytes 524320 | tf_op jit(solution)/shard_map/ppermute | solution.py:355
  121.6 0.8 copy-done.17
  122.3 5.3 %shard_map.89 = (f32[4,4,128,128]{3,2,1,0:T(8,128)}, f32[4,4,128,128]{3,2,1,0:T(8,128)}) custom-call(s32[8,18]{1,0:T(8,128)} %dynamic-slice_bitcast_fusion.tab, f32[2,4,4,128,128]{4,3,2,1,0:T(8,128)} %get-tuple-element.43.kept, f32[2,4,4,128,128]{4,3,2,1,0:T(8,128)} %get-tuple-element.44.given, bf16[1,4,4,128,128]{4,3,2,1,0:T(8,128)(2,1)} %copy-done.17, ...), custom_call_target="tpu_custom_call" | custom-call | flops 40000000000 | bytes 8388608 | tf_op jit(solution)/shard_map/pallas_call | solution.py:304
  127.7 3.2 %collective-permute-start.17 = (f32[4,4,128,128]{3,2,1,0:T(8,128)}, f32[4,4,128,128]{3,2,1,0:T(8,128)S(1)}, u32[]{:S(2)}, u32[]{:S(2)}) collective-permute-start(f32[4,4,128,128]{3,2,1,0:T(8,128)} %get-tuple-element.50), channel_id=1, source_target_pairs={{0,1},{1,0},{2,3},{3,2},{4,5},{5,4},{6,7},{7,6},{8,9},{9,8},{10,11... | collective-permute-start | bytes 3145736 | tf_op jit(solution)/shard_map/ppermute | solution.py:355
  130.9 0.1 collective-permute-start.19
  130.9 3.0 %collective-permute-done.17 = f32[4,4,128,128]{3,2,1,0:T(8,128)S(1)} collective-permute-done((f32[4,4,128,128]{3,2,1,0:T(8,128)}, f32[4,4,128,128]{3,2,1,0:T(8,128)S(1)}, u32[]{:S(2)}, u32[]{:S(2)}) %collective-permute-start.17) | collective-permute-done | bytes 1048608 | tf_op jit(solution)/shard_map/ppermute | solution.py:355
  134.0 1.3 add_convert_fusion.1
  135.3 3.6 %collective-permute-start.18 = (bf16[4,4,128,128]{3,2,1,0:T(8,128)(2,1)S(1)}, bf16[4,4,128,128]{3,2,1,0:T(8,128)(2,1)S(1)}, u32[]{:S(2)}, u32[]{:S(2)}) collective-permute-start(bf16[4,4,128,128]{3,2,1,0:T(8,128)(2,1)S(1)} %add_convert_fusion.1), channel_id=1, source_target_pairs={{0,0},{1,4},{2,2},{3,6},{4,1},{5,5},{6,3},{7,7},{8,8},{9,12},{10,1... | collective-permute-start | bytes 1572872 | tf_op jit(solution)/shard_map/ppermute | solution.py:355
  139.0 0.1 add_convert_fusion
  139.1 2.0 %collective-permute-start.20 = (bf16[4,4,128,128]{3,2,1,0:T(8,128)(2,1)S(1)}, bf16[4,4,128,128]{3,2,1,0:T(8,128)(2,1)S(1)}, u32[]{:S(2)}, u32[]{:S(2)}) collective-permute-start(bf16[4,4,128,128]{3,2,1,0:T(8,128)(2,1)S(1)} %add_convert_fusion), channel_id=1, source_target_pairs={{0,0},{1,4},{2,2},{3,6},{4,1},{5,5},{6,3},{7,7},{8,8},{9,12},{10,1... | collective-permute-start | bytes 1572872 | tf_op jit(solution)/shard_map/ppermute | solution.py:355
  141.1 4.7 %collective-permute-done.18 = bf16[4,4,128,128]{3,2,1,0:T(8,128)(2,1)S(1)} collective-permute-done((bf16[4,4,128,128]{3,2,1,0:T(8,128)(2,1)S(1)}, bf16[4,4,128,128]{3,2,1,0:T(8,128)(2,1)S(1)}, u32[]{:S(2)}, u32[]{:S(2)}) %collective-permute-start.18) | collective-permute-done | bytes 524320 | tf_op jit(solution)/shard_map/ppermute | solution.py:355
  145.8 5.6 %collective-permute-done.20 = bf16[4,4,128,128]{3,2,1,0:T(8,128)(2,1)S(1)} collective-permute-done((bf16[4,4,128,128]{3,2,1,0:T(8,128)(2,1)S(1)}, bf16[4,4,128,128]{3,2,1,0:T(8,128)(2,1)S(1)}, u32[]{:S(2)}, u32[]{:S(2)}) %collective-permute-start.20) | collective-permute-done | bytes 524320 | tf_op jit(solution)/shard_map/ppermute | solution.py:355
  151.4 1.1 multiply_bitcast_fusion
  (44 shorter events, 0.2 us)
Async XLA Ops:
  4.5 23.2 %collective-permute-start = (bf16[3,4,4,128,128]{4,3,2,1,0:T(8,128)(2,1)}, bf16[3,4,4,128,128]{4,3,2,1,0:T(8,128)(2,1)S(1)}, u32[]{:S(2)}, u32[]{:S(2)}) collective-permute-start(bf16[3,4,4,128,128]{4,3,2,1,0:T(8,128)(2,1)} %shard_map.86.refs_12_.refs_1_.refs_2_), channel_id=1, source_target_pairs={{0,0},{1,4},{2,2},{3,6},{4,1},{5,5},{6,3},{7,7},{8,8},{9,12},{10,1... | collective-permute-start | bytes 4718600 | tf_op jit(solution)/shard_map/ppermute | solution.py:355
  10.3 36.5 %copy-start = (bf16[3,4,4,128,128]{4,3,2,1,0:T(8,128)(2,1)S(1)}, bf16[3,4,4,128,128]{4,3,2,1,0:T(8,128)(2,1)}, u32[]{:S(2)}) copy-start(bf16[3,4,4,128,128]{4,3,2,1,0:T(8,128)(2,1)} %shard_map.86.refs_12_.refs_1_.refs_2_) | copy-start | bytes 4718596
  27.7 42.8 %copy-start.1 = (bf16[2,4,4,128,128]{4,3,2,1,0:T(8,128)(2,1)}, bf16[2,4,4,128,128]{4,3,2,1,0:T(8,128)(2,1)S(1)}, u32[]{:S(2)}) copy-start(bf16[2,4,4,128,128]{4,3,2,1,0:T(8,128)(2,1)S(1)} %slice.16.refs_1_) | copy-start | bytes 3145732
  27.7 14.8 %collective-permute-start.3 = (bf16[2,4,4,128,128]{4,3,2,1,0:T(8,128)(2,1)S(1)}, bf16[2,4,4,128,128]{4,3,2,1,0:T(8,128)(2,1)S(1)}, u32[]{:S(2)}, u32[]{:S(2)}) collective-permute-start(bf16[2,4,4,128,128]{4,3,2,1,0:T(8,128)(2,1)S(1)} %slice.16.refs_1_), channel_id=1, source_target_pairs={{0,8},{1,9},{2,10},{3,11},{4,12},{5,13},{6,14},{7,15},{24,16},{25,... | collective-permute-start | bytes 3145736 | tf_op jit(solution)/shard_map/ppermute | solution.py:355
  30.9 15.8 %collective-permute-start.2 = (bf16[2,4,4,128,128]{4,3,2,1,0:T(8,128)(2,1)S(1)}, bf16[2,4,4,128,128]{4,3,2,1,0:T(8,128)(2,1)}, u32[]{:S(2)}, u32[]{:S(2)}) collective-permute-start(bf16[2,4,4,128,128]{4,3,2,1,0:T(8,128)(2,1)S(1)} %slice.16.refs_1_), channel_id=1, source_target_pairs={{8,0},{9,1},{10,2},{11,3},{12,4},{13,5},{14,6},{15,7},{16,24},{17,... | collective-permute-start | bytes 3145736 | tf_op jit(solution)/shard_map/ppermute | solution.py:355
  32.2 15.8 %collective-permute-start.1 = (bf16[2,4,4,128,128]{4,3,2,1,0:T(8,128)(2,1)S(1)}, bf16[2,4,4,128,128]{4,3,2,1,0:T(8,128)(2,1)S(1)}, u32[]{:S(2)}, u32[]{:S(2)}) collective-permute-start(bf16[2,4,4,128,128]{4,3,2,1,0:T(8,128)(2,1)S(1)} %slice.16.refs_1_), channel_id=1, source_target_pairs={{8,16},{9,17},{10,18},{11,19},{12,20},{13,21},{14,22},{15,23},{16,... | collective-permute-start | bytes 3145736 | tf_op jit(solution)/shard_map/ppermute | solution.py:355
  33.0 37.3 %copy-start.4 = (bf16[1,4,4,128,128]{4,3,2,1,0:T(8,128)(2,1)}, bf16[1,4,4,128,128]{4,3,2,1,0:T(8,128)(2,1)S(1)}, u32[]{:S(2)}) copy-start(bf16[1,4,4,128,128]{4,3,2,1,0:T(8,128)(2,1)S(1)} %slice.17.refs_0_) | copy-start | bytes 1572868
  33.0 15.2 %collective-permute-start.6 = (bf16[1,4,4,128,128]{4,3,2,1,0:T(8,128)(2,1)S(1)}, bf16[1,4,4,128,128]{4,3,2,1,0:T(8,128)(2,1)S(1)}, u32[]{:S(2)}, u32[]{:S(2)}) collective-permute-start(bf16[1,4,4,128,128]{4,3,2,1,0:T(8,128)(2,1)S(1)} %slice.17.refs_0_), channel_id=1, source_target_pairs={{0,8},{1,9},{2,10},{3,11},{4,12},{5,13},{6,14},{7,15},{24,16},{25,... | collective-permute-start | bytes 1572872 | tf_op jit(solution)/shard_map/ppermute | solution.py:355
  40.5 11.7 %collective-permute-start.5 = (bf16[1,4,4,128,128]{4,3,2,1,0:T(8,128)(2,1)S(1)}, bf16[1,4,4,128,128]{4,3,2,1,0:T(8,128)(2,1)}, u32[]{:S(2)}, u32[]{:S(2)}) collective-permute-start(bf16[1,4,4,128,128]{4,3,2,1,0:T(8,128)(2,1)S(1)} %slice.17.refs_0_), channel_id=1, source_target_pairs={{8,0},{9,1},{10,2},{11,3},{12,4},{13,5},{14,6},{15,7},{16,24},{17,... | collective-permute-start | bytes 1572872 | tf_op jit(solution)/shard_map/ppermute | solution.py:355
  42.6 48.5 %copy-start.7 = (bf16[2,4,4,128,128]{4,3,2,1,0:T(8,128)(2,1)}, bf16[2,4,4,128,128]{4,3,2,1,0:T(8,128)(2,1)S(1)}, u32[]{:S(2)}) copy-start(bf16[2,4,4,128,128]{4,3,2,1,0:T(8,128)(2,1)S(1)} %collective-permute-done.3.refs_3_) | copy-start | bytes 3145732
  42.6 10.9 %collective-permute-start.4 = (bf16[1,4,4,128,128]{4,3,2,1,0:T(8,128)(2,1)S(1)}, bf16[1,4,4,128,128]{4,3,2,1,0:T(8,128)(2,1)S(1)}, u32[]{:S(2)}, u32[]{:S(2)}) collective-permute-start(bf16[1,4,4,128,128]{4,3,2,1,0:T(8,128)(2,1)S(1)} %slice.17.refs_0_), channel_id=1, source_target_pairs={{8,16},{9,17},{10,18},{11,19},{12,20},{13,21},{14,22},{15,23},{16,... | collective-permute-start | bytes 1572872 | tf_op jit(solution)/shard_map/ppermute | solution.py:355
  46.8 20.0 %collective-permute-start.7 = (bf16[3,4,4,128,128]{4,3,2,1,0:T(8,128)(2,1)S(1)}, bf16[3,4,4,128,128]{4,3,2,1,0:T(8,128)(2,1)S(1)}, u32[]{:S(2)}, u32[]{:S(2)}) collective-permute-start(bf16[3,4,4,128,128]{4,3,2,1,0:T(8,128)(2,1)S(1)} %copy-done), channel_id=1, source_target_pairs={{0,2},{1,3},{2,0},{3,1},{4,6},{5,7},{6,4},{7,5},{8,10},{9,11},{10,... | collective-permute-start | bytes 4718600 | tf_op jit(solution)/shard_map/ppermute | solution.py:355
  48.0 43.1 %copy-start.8 = (bf16[2,4,4,128,128]{4,3,2,1,0:T(8,128)(2,1)}, bf16[2,4,4,128,128]{4,3,2,1,0:T(8,128)(2,1)S(1)}, u32[]{:S(2)}) copy-start(bf16[2,4,4,128,128]{4,3,2,1,0:T(8,128)(2,1)S(1)} %collective-permute-done.1.refs_5_) | copy-start | bytes 3145732
  48.0 19.6 %collective-permute-start.8 = (bf16[3,4,4,128,128]{4,3,2,1,0:T(8,128)(2,1)S(1)}, bf16[3,4,4,128,128]{4,3,2,1,0:T(8,128)(2,1)S(1)}, u32[]{:S(2)}, u32[]{:S(2)}) collective-permute-start(bf16[3,4,4,128,128]{4,3,2,1,0:T(8,128)(2,1)S(1)} %collective-permute-done), channel_id=1, source_target_pairs={{0,4},{1,0},{2,6},{3,2},{4,5},{5,1},{6,7},{7,3},{8,12},{9,8},{10,1... | collective-permute-start | bytes 4718600 | tf_op jit(solution)/shard_map/ppermute | solution.py:355
  48.2 42.9 %copy-start.13 = (bf16[1,4,4,128,128]{4,3,2,1,0:T(8,128)(2,1)}, bf16[1,4,4,128,128]{4,3,2,1,0:T(8,128)(2,1)S(1)}, u32[]{:S(2)}) copy-start(bf16[1,4,4,128,128]{4,3,2,1,0:T(8,128)(2,1)S(1)} %collective-permute-done.6.refs_2_) | copy-start | bytes 1572868
  48.2 22.4 %collective-permute-start.9 = (bf16[2,4,4,128,128]{4,3,2,1,0:T(8,128)(2,1)S(1)}, bf16[2,4,4,128,128]{4,3,2,1,0:T(8,128)(2,1)}, u32[]{:S(2)}, u32[]{:S(2)}) collective-permute-start(bf16[2,4,4,128,128]{4,3,2,1,0:T(8,128)(2,1)S(1)} %collective-permute-done.3.refs_3_), channel_id=1, source_target_pairs={{8,16},{9,17},{10,18},{11,19},{12,20},{13,21},{14,22},{15,23},{16,... | collective-permute-start | bytes 3145736 | tf_op jit(solution)/shard_map/ppermute | solution.py:355
  52.2 23.4 %collective-permute-start.10 = (bf16[2,4,4,128,128]{4,3,2,1,0:T(8,128)(2,1)S(1)}, bf16[2,4,4,128,128]{4,3,2,1,0:T(8,128)(2,1)S(1)}, u32[]{:S(2)}, u32[]{:S(2)}) collective-permute-start(bf16[2,4,4,128,128]{4,3,2,1,0:T(8,128)(2,1)S(1)} %collective-permute-done.1.refs_5_), channel_id=1, source_target_pairs={{8,0},{9,1},{10,2},{11,3},{12,4},{13,5},{14,6},{15,7},{16,24},{17,... | collective-permute-start | bytes 3145736 | tf_op jit(solution)/shard_map/ppermute | solution.py:355
  53.5 37.6 %copy-start.14 = (bf16[1,4,4,128,128]{4,3,2,1,0:T(8,128)(2,1)}, bf16[1,4,4,128,128]{4,3,2,1,0:T(8,128)(2,1)S(1)}, u32[]{:S(2)}) copy-start(bf16[1,4,4,128,128]{4,3,2,1,0:T(8,128)(2,1)S(1)} %collective-permute-done.4.refs_4_) | copy-start | bytes 1572868
  66.7 3.6 %copy-start.5 = (bf16[3,4,4,128,128]{4,3,2,1,0:T(8,128)(2,1)}, bf16[3,4,4,128,128]{4,3,2,1,0:T(8,128)(2,1)S(1)}, u32[]{:S(2)}) copy-start(bf16[3,4,4,128,128]{4,3,2,1,0:T(8,128)(2,1)S(1)} %collective-permute-done.7.refs_13_.refs_2_.refs_3_) | copy-start | bytes 4718596
  67.6 24.9 %copy-start.3 = (bf16[3,4,4,128,128]{4,3,2,1,0:T(8,128)(2,1)}, bf16[3,4,4,128,128]{4,3,2,1,0:T(8,128)(2,1)S(1)}, u32[]{:S(2)}) copy-start(bf16[3,4,4,128,128]{4,3,2,1,0:T(8,128)(2,1)S(1)} %collective-permute-done.8.refs_14_.refs_3_.refs_4_) | copy-start | bytes 4718596
  67.6 9.3 %collective-permute-start.11 = (bf16[1,4,4,128,128]{4,3,2,1,0:T(8,128)(2,1)S(1)}, bf16[1,4,4,128,128]{4,3,2,1,0:T(8,128)(2,1)}, u32[]{:S(2)}, u32[]{:S(2)}) collective-permute-start(bf16[1,4,4,128,128]{4,3,2,1,0:T(8,128)(2,1)S(1)} %collective-permute-done.6.refs_2_), channel_id=1, source_target_pairs={{8,16},{9,17},{10,18},{11,19},{12,20},{13,21},{14,22},{15,23},{16,... | collective-permute-start | bytes 1572872 | tf_op jit(solution)/shard_map/ppermute | solution.py:355
  69.1 18.8 %collective-permute-start.12 = (bf16[1,4,4,128,128]{4,3,2,1,0:T(8,128)(2,1)S(1)}, bf16[1,4,4,128,128]{4,3,2,1,0:T(8,128)(2,1)S(1)}, u32[]{:S(2)}, u32[]{:S(2)}) collective-permute-start(bf16[1,4,4,128,128]{4,3,2,1,0:T(8,128)(2,1)S(1)} %collective-permute-done.4.refs_4_), channel_id=1, source_target_pairs={{8,0},{9,1},{10,2},{11,3},{12,4},{13,5},{14,6},{15,7},{16,24},{17,... | collective-permute-start | bytes 1572872 | tf_op jit(solution)/shard_map/ppermute | solution.py:355
  70.4 17.5 %collective-permute-start.14 = (bf16[1,4,4,128,128]{4,3,2,1,0:T(8,128)(2,1)S(1)}, bf16[1,4,4,128,128]{4,3,2,1,0:T(8,128)(2,1)S(1)}, u32[]{:S(2)}, u32[]{:S(2)}) collective-permute-start(bf16[1,4,4,128,128]{4,3,2,1,0:T(8,128)(2,1)S(1)} %slice.19), channel_id=1, source_target_pairs={{0,4},{1,5},{2,6},{3,7},{4,0},{5,1},{6,2},{7,3},{8,12},{9,13},{10,... | collective-permute-start | bytes 1572872 | tf_op jit(solution)/shard_map/ppermute | solution.py:355
  70.6 20.5 %collective-permute-start.13 = (bf16[2,4,4,128,128]{4,3,2,1,0:T(8,128)(2,1)S(1)}, bf16[2,4,4,128,128]{4,3,2,1,0:T(8,128)(2,1)S(1)}, u32[]{:S(2)}, u32[]{:S(2)}) collective-permute-start(bf16[2,4,4,128,128]{4,3,2,1,0:T(8,128)(2,1)S(1)} %slice.18), channel_id=1, source_target_pairs={{0,2},{1,3},{2,0},{3,1},{4,6},{5,7},{6,4},{7,5},{8,10},{9,11},{10,... | collective-permute-start | bytes 3145736 | tf_op jit(solution)/shard_map/ppermute | solution.py:355
  75.6 15.5 %copy-start.9 = (bf16[2,4,4,128,128]{4,3,2,1,0:T(8,128)(2,1)}, bf16[2,4,4,128,128]{4,3,2,1,0:T(8,128)(2,1)S(1)}, u32[]{:S(2)}) copy-start(bf16[2,4,4,128,128]{4,3,2,1,0:T(8,128)(2,1)S(1)} %collective-permute-done.10.refs_11_) | copy-start | bytes 3145732
  75.6 34.7 %collective-permute-start.15 = (bf16[2,4,4,128,128]{4,3,2,1,0:T(8,128)(2,1)}, bf16[2,4,4,128,128]{4,3,2,1,0:T(8,128)(2,1)S(1)}, u32[]{:S(2)}, u32[]{:S(2)}) collective-permute-start(bf16[2,4,4,128,128]{4,3,2,1,0:T(8,128)(2,1)} %collective-permute-done.9.refs_9_), channel_id=1, source_target_pairs={{8,0},{9,1},{10,2},{11,3},{12,4},{13,5},{14,6},{15,7},{16,24},{17,... | collective-permute-start | bytes 3145736 | tf_op jit(solution)/shard_map/ppermute | solution.py:355
  87.8 3.3 %copy-start.16 = (bf16[1,4,4,128,128]{4,3,2,1,0:T(8,128)(2,1)}, bf16[1,4,4,128,128]{4,3,2,1,0:T(8,128)(2,1)S(1)}, u32[]{:S(2)}) copy-start(bf16[1,4,4,128,128]{4,3,2,1,0:T(8,128)(2,1)S(1)} %collective-permute-done.12.refs_10_) | copy-start | bytes 1572868
  87.8 4.6 %copy-start.15 = (bf16[1,4,4,128,128]{4,3,2,1,0:T(8,128)(2,1)}, bf16[1,4,4,128,128]{4,3,2,1,0:T(8,128)(2,1)S(1)}, u32[]{:S(2)}) copy-start(bf16[1,4,4,128,128]{4,3,2,1,0:T(8,128)(2,1)S(1)} %collective-permute-done.14.refs_15_.refs_4_.refs_5_) | copy-start | bytes 1572868
  91.1 1.3 copy-start.10
  91.1 30.4 %collective-permute-start.16 = (bf16[1,4,4,128,128]{4,3,2,1,0:T(8,128)(2,1)}, bf16[1,4,4,128,128]{4,3,2,1,0:T(8,128)(2,1)S(1)}, u32[]{:S(2)}, u32[]{:S(2)}) collective-permute-start(bf16[1,4,4,128,128]{4,3,2,1,0:T(8,128)(2,1)} %collective-permute-done.11.refs_8_), channel_id=1, source_target_pairs={{8,0},{9,1},{10,2},{11,3},{12,4},{13,5},{14,6},{15,7},{16,24},{17,... | collective-permute-start | bytes 1572872 | tf_op jit(solution)/shard_map/ppermute | solution.py:355
  110.3 1.0 copy-start.11
  116.7 14.2 %copy-start.12 = (f32[4,4,128,128]{3,2,1,0:T(8,128)S(1)}, f32[4,4,128,128]{3,2,1,0:T(8,128)}, u32[]{:S(2)}) copy-start(f32[4,4,128,128]{3,2,1,0:T(8,128)} %get-tuple-element.51) | copy-start | bytes 3145732
  121.5 0.8 copy-start.17
  127.7 11.3 %copy-start.2 = (f32[4,4,128,128]{3,2,1,0:T(8,128)S(1)}, f32[4,4,128,128]{3,2,1,0:T(8,128)}, u32[]{:S(2)}) copy-start(f32[4,4,128,128]{3,2,1,0:T(8,128)} %get-tuple-element.46) | copy-start | bytes 3145732
  127.7 6.3 %collective-permute-start.17 = (f32[4,4,128,128]{3,2,1,0:T(8,128)}, f32[4,4,128,128]{3,2,1,0:T(8,128)S(1)}, u32[]{:S(2)}, u32[]{:S(2)}) collective-permute-start(f32[4,4,128,128]{3,2,1,0:T(8,128)} %get-tuple-element.50), channel_id=1, source_target_pairs={{0,1},{1,0},{2,3},{3,2},{4,5},{5,4},{6,7},{7,6},{8,9},{9,8},{10,11... | collective-permute-start | bytes 3145736 | tf_op jit(solution)/shard_map/ppermute | solution.py:355
  130.9 8.1 %collective-permute-start.19 = (f32[4,4,128,128]{3,2,1,0:T(8,128)S(1)}, f32[4,4,128,128]{3,2,1,0:T(8,128)S(1)}, u32[]{:S(2)}, u32[]{:S(2)}) collective-permute-start(f32[4,4,128,128]{3,2,1,0:T(8,128)S(1)} %copy-done.12), channel_id=1, source_target_pairs={{0,1},{1,0},{2,3},{3,2},{4,5},{5,4},{6,7},{7,6},{8,9},{9,8},{10,11... | collective-permute-start | bytes 3145736 | tf_op jit(solution)/shard_map/ppermute | solution.py:355
  135.3 5.7 %copy-start.6 = (s32[4,1,4]{2,1,0:T(1,128)S(1)}, s32[4,1,4]{2,1,0:T(1,128)}, u32[]{:S(2)}) copy-start(s32[4,1,4]{2,1,0:T(1,128)} %refs_1_.1) | copy-start | bytes 196
  135.3 10.5 %collective-permute-start.18 = (bf16[4,4,128,128]{3,2,1,0:T(8,128)(2,1)S(1)}, bf16[4,4,128,128]{3,2,1,0:T(8,128)(2,1)S(1)}, u32[]{:S(2)}, u32[]{:S(2)}) collective-permute-start(bf16[4,4,128,128]{3,2,1,0:T(8,128)(2,1)S(1)} %add_convert_fusion.1), channel_id=1, source_target_pairs={{0,0},{1,4},{2,2},{3,6},{4,1},{5,5},{6,3},{7,7},{8,8},{9,12},{10,1... | collective-permute-start | bytes 1572872 | tf_op jit(solution)/shard_map/ppermute | solution.py:355
  139.1 12.4 %collective-permute-start.20 = (bf16[4,4,128,128]{3,2,1,0:T(8,128)(2,1)S(1)}, bf16[4,4,128,128]{3,2,1,0:T(8,128)(2,1)S(1)}, u32[]{:S(2)}, u32[]{:S(2)}) collective-permute-start(bf16[4,4,128,128]{3,2,1,0:T(8,128)(2,1)S(1)} %add_convert_fusion), channel_id=1, source_target_pairs={{0,0},{1,4},{2,2},{3,6},{4,1},{5,5},{6,3},{7,7},{8,8},{9,12},{10,1... | collective-permute-start | bytes 1572872 | tf_op jit(solution)/shard_map/ppermute | solution.py:355

commit v3 on v2

--- a/solution.py
+++ b/solution.py
@@ -214,7 +214,7 @@
             pltpu.SemaphoreType.DMA((2, Y, mats)),
         ],
         out_shape=[jax.ShapeDtypeStruct((len(kinds), M, S, B, B), jnp.float32)] * 2,
-        compiler_params=pltpu.CompilerParams(vmem_limit_bytes=58 * 2**20),
+        compiler_params=pltpu.CompilerParams(vmem_limit_bytes=30 * 2**20),
         cost_estimate=pl.CostEstimate(
             flops=6 * B**3 * terms,
             bytes_accessed=len(spans) * M * S * B * B * 2,
@@ -229,7 +229,7 @@
             return ref, mat - first
 
 
-def last_body(plan, kind, firsts, tab, kept, given, *refs):
+def last_body(plan, products, firsts, tab, kept, given, *refs):
     data, (kept_out, given_out, rows, held, sem) = refs[:-5], refs[-5:]
     S, M, Y, nb = plan.S, plan.M, plan.Y, plan.nb
     B = held.shape[-1]
@@ -244,15 +244,16 @@
 
     def base_copies():
         for i, ref in enumerate((kept, given)):
-            yield pltpu.make_async_copy(ref.at[kind // 2], totals[i], sem.at[0, i, 0])
+            source = ref.at[1 if products[0][2] == D else 0] if len(ref.shape) == 5 else ref
+            yield pltpu.make_async_copy(source, totals[i], sem.at[0, i, 0])
 
     def unit_copies():
-        for i, mat in enumerate((kind, Q)):
+        for i, (_, mat, _) in enumerate(products):
             ref, index = find(places["unit"], mat)
             yield pltpu.make_async_copy(ref.at[index], held.at[i], sem.at[0, i, 1])
 
     def row_copies(e, pieces):
-        for i, mat in enumerate((kind, Q)):
+        for i, (mat, _, _) in enumerate(products):
             ref, index = find(pieces, mat)
             for n in range(nb):
                 yield pltpu.make_async_copy(ref.at[index, :, terms[e][n][0]], rows.at[e, i, n], sem.at[1 + e, i, n])
@@ -281,20 +282,17 @@
         for e in (1, 0):
             @pl.loop(0, M, unroll=True)
             def _(m, e=e):
-                def left(i):
-                    return jnp.concatenate([rows[e, i, n, m] for n in range(nb)], axis=1)
-
-                def right(i):
-                    return right_side(plan, terms[e], m, lambda n, row, slot: held[i, row, slot])
-
-                dot = functools.partial(jnp.dot, preferred_element_type=jnp.float32)
-                there, back = dot(left(0), right(1)), dot(left(1), right(0))
-                more = there - back if kind == H else there + back
+                more = 0
+                for i, (_, _, kind) in enumerate(products):
+                    left = jnp.concatenate([rows[e, i, n, m] for n in range(nb)], axis=1)
+                    right = right_side(plan, terms[e], m, lambda n, row, slot: held[i, row, slot])
+                    part = jnp.dot(left, right, preferred_element_type=jnp.float32)
+                    more = more - part if kind == -1 else more + part
                 for s in range(S):
                     totals[e][m, s] += more[:, s * B:(s + 1) * B]
 
 
-def last(plan, tab, kind, kept, given, near, far, unit):
+def last(plan, tab, products, kept, given, near, far, unit):
     M, S, Y, nb = plan.M, plan.S, plan.Y, plan.nb
     lists = [("unit", unit)]
     lists += [(("rows", side, dy), pieces) for side, sides in enumerate((near, far)) for dy, pieces in enumerate(sides)]
@@ -302,17 +300,17 @@
     operands = [array for _, pieces in lists for array, _ in pieces]
     B = kept.shape[-1]
     return pl.pallas_call(
-        functools.partial(last_body, plan, kind, firsts),
+        functools.partial(last_body, plan, products, firsts),
         in_specs=[pl.BlockSpec(memory_space=pltpu.SMEM)] + [pl.BlockSpec(memory_space=pl.ANY)] * (2 + len(operands)),
         out_specs=[pl.BlockSpec(memory_space=pltpu.VMEM)] * 2,
         scratch_shapes=[
-            pltpu.VMEM((2, 2, nb, M, B, B), operands[0].dtype),
-            pltpu.VMEM((2, M, S, B, B), operands[0].dtype),
+            pltpu.VMEM((2, len(products), nb, M, B, B), operands[0].dtype),
+            pltpu.VMEM((len(products), M, S, B, B), operands[0].dtype),
             pltpu.SemaphoreType.DMA((3, 2, max(nb, 2))),
         ],
         out_shape=[jax.ShapeDtypeStruct((M, S, B, B), jnp.float32)] * 2,
-        compiler_params=pltpu.CompilerParams(vmem_limit_bytes=58 * 2**20),
-        cost_estimate=pl.CostEstimate(flops=4 * 10**10, bytes_accessed=8 * 2**20, transcendentals=0),
+        compiler_params=pltpu.CompilerParams(vmem_limit_bytes=30 * 2**20),
+        cost_estimate=pl.CostEstimate(flops=2 * 10**10, bytes_accessed=8 * 2**20, transcendentals=0),
     )(tab, kept, given, *operands)
 
 
@@ -424,13 +422,18 @@
     early = ["own", "in", "mid", "out1", "mid2", "out2"]
     pieces = {name: [(parts[H], H), (parts[Q], Q)] for name, parts in got.items()}
     kept, given = contract(plan, after(tab, token), near, far, early, (H, D), pieces)
-    own, lent = last(plan, tab, D, kept, given, near, far, pieces["out3"][1:])
-    response = own, move(lent, sibling)
-    own, lent = last(plan, after(tab, own), H, kept, given, near, far, pieces["out3"])
-    commutator = own, move(lent, sibling)
-    results = [move((own + lent).astype(jnp.bfloat16), cross) for own, lent in (response, commutator)]
-    response, commutator = [(result * pattern)[:, None] for result in results]
-    return commutator, response
+    barrier = lax.optimization_barrier
+    out_qd, out_h = pieces["out3"][1:], pieces["out3"][:1]
+    own, lent = last(plan, tab, ((D, Q, D), (Q, D, D)), kept, given, near, far, out_qd)
+    lent = move(lent, sibling)
+    own, kept = barrier((own, kept))
+    kept, given = last(plan, tab, ((H, Q, H),), kept, given, near, far, out_qd)
+    lent, kept = barrier((lent, kept))
+    response, given = barrier(((own + lent).astype(jnp.bfloat16), given))
+    response = move(response, cross)
+    own, lent = last(plan, tab, ((Q, H, -1),), kept, given, near, far, out_h)
+    commutator = move((own + move(lent, sibling)).astype(jnp.bfloat16), cross)
+    return (commutator * pattern)[:, None], (response * pattern)[:, None]
 
 
 def solution(mesh):

time: 153 us -> 144 us (0.941)
  Pallas kernels: 25.8 us -> 16.7 us
  starting transfers between devices: 38.3 us -> 42 us
  local copies, waits for them, and re-layouts: 3.4 us -> 0.95 us
    pallas_call x2 -> x3, Pallas kernels: 10.6 us -> 5.84 us  [last(): pl.pallas_call(functools.partial(last_body, plan, products, firsts), in_s...]
    pallas_call x1, Pallas kernels: 11.3 us -> 7.05 us  [contract(): pl.pallas_call(functools.partial(contract_body, plan, tuple((plan.units.i...]
    ppermute x21, starting transfers between devices: 38.3 us -> 42 us  [move(): return lax.ppermute(value, AXES, pairs)]
    unnamed x37 -> x5, local copies, waits for them, and re-layouts: 1.87 us -> 0.01 us
  transfers between devices with their start and end apart: 21 -> 21, of which waited for: 15 -> 14; matrix products, arithmetic and copies ran while one was open for 2% -> 1% of each run, Pallas kernels for 11% -> 8%
where the time goes in v3:
time: 144 us
  waiting for transfers between devices  81.6 us (57%)
  starting transfers between devices  42 us (29%)
  Pallas kernels  16.7 us (12%)
    ppermute x21, waiting for transfers between devices, move(): return lax.ppermute(value, AXES, pairs)  81.6 us
    ppermute x21, starting transfers between devices, move(): return lax.ppermute(value, AXES, pairs)  42 us
    pallas_call x1, Pallas kernels, contract(): pl.pallas_call(functools.partial(contract_body, plan, tuple((plan.units.i...  7.05 us
    pallas_call x3, Pallas kernels, last(): pl.pallas_call(functools.partial(last_body, plan, products, firsts), in_s...  5.84 us
    pallas_call x1, Pallas kernels, keep(): pl.pallas_call(keep_body, grid=(M,), in_specs=[pl.BlockSpec(memory_space=...  3.83 us
  transfers between devices with their start and end apart: 21, of which 14 were waited for; matrix products, arithmetic and copies ran while one was open for 1% of the time, Pallas kernels for 8%

profile of v3, /device:TPU:1, one launch (start us, length us, event | category | flops | bytes accessed | tf_op | source)
XLA Modules:
  0.0 143.5 jit_solution(3807236094765845206)
XLA Ops:
  0.6 3.8 %shard_map.86.refs_12_.refs_1_ = bf16[3,4,4,128,128]{4,3,2,1,0:T(8,128)(2,1)} custom-call(s32[4,1,4]{2,1,0:T(1,128)} %refs_0_.1, s32[4,1,4]{2,1,0:T(1,128)} %refs_1_.1, s32[4,1,4]{2,1,0:T(1,128)} %refs_2_.1, bf16[4,1,4,128,128]{4,3,2,1,0:T(8,128)(2,1)} %refs_3_.1, bf16[4,1,4,128,128]{4,3,2,1,0:T(8,128)(2,1)} %refs_4_.1, bf16[4,1,4,128,128]{4,3,2,1,0:T(8,128)(2,1)} %refs_5_.1), custom_call_target="tpu_custom_call" | custom-call | tf_op jit(solution)/shard_map/pallas_call | solution.py:329
  4.5 4.5 %collective-permute-start = (bf16[3,4,4,128,128]{4,3,2,1,0:T(8,128)(2,1)}, bf16[3,4,4,128,128]{4,3,2,1,0:T(8,128)(2,1)S(1)}, u32[]{:S(2)}, u32[]{:S(2)}) collective-permute-start(bf16[3,4,4,128,128]{4,3,2,1,0:T(8,128)(2,1)} %shard_map.86.refs_12_.refs_1_), channel_id=1, source_target_pairs={{0,0},{1,4},{2,2},{3,6},{4,1},{5,5},{6,3},{7,7},{8,8},{9,12},{10,1... | collective-permute-start | bytes 4718600 | tf_op jit(solution)/shard_map/ppermute | solution.py:353
  9.0 0.7 dynamic-slice_bitcast_fusion.tab
  9.7 17.9 %collective-permute-done = bf16[3,4,4,128,128]{4,3,2,1,0:T(8,128)(2,1)S(1)} collective-permute-done((bf16[3,4,4,128,128]{4,3,2,1,0:T(8,128)(2,1)}, bf16[3,4,4,128,128]{4,3,2,1,0:T(8,128)(2,1)S(1)}, u32[]{:S(2)}, u32[]{:S(2)}) %collective-permute-start) | collective-permute-done | bytes 1572896 | tf_op jit(solution)/shard_map/ppermute | solution.py:353
  27.6 0.1 slice.16.refs_1_
  27.6 3.3 %collective-permute-start.3 = (bf16[2,4,4,128,128]{4,3,2,1,0:T(8,128)(2,1)S(1)}, bf16[2,4,4,128,128]{4,3,2,1,0:T(8,128)(2,1)S(1)}, u32[]{:S(2)}, u32[]{:S(2)}) collective-permute-start(bf16[2,4,4,128,128]{4,3,2,1,0:T(8,128)(2,1)S(1)} %slice.16.refs_1_), channel_id=1, source_target_pairs={{0,8},{1,9},{2,10},{3,11},{4,12},{5,13},{6,14},{7,15},{24,16},{25,... | collective-permute-start | bytes 3145736 | tf_op jit(solution)/shard_map/ppermute | solution.py:353
  30.9 1.3 collective-permute-start.2
  32.2 0.7 collective-permute-start.1
  33.0 6.6 %collective-permute-start.6 = (bf16[1,4,4,128,128]{4,3,2,1,0:T(8,128)(2,1)S(1)}, bf16[1,4,4,128,128]{4,3,2,1,0:T(8,128)(2,1)S(1)}, u32[]{:S(2)}, u32[]{:S(2)}) collective-permute-start(bf16[1,4,4,128,128]{4,3,2,1,0:T(8,128)(2,1)S(1)} %slice.17.refs_0_), channel_id=1, source_target_pairs={{0,8},{1,9},{2,10},{3,11},{4,12},{5,13},{6,14},{7,15},{24,16},{25,... | collective-permute-start | bytes 1572872 | tf_op jit(solution)/shard_map/ppermute | solution.py:353
  39.5 1.3 collective-permute-start.5
  40.9 1.7 %collective-permute-done.3.refs_3_ = bf16[2,4,4,128,128]{4,3,2,1,0:T(8,128)(2,1)S(1)} collective-permute-done((bf16[2,4,4,128,128]{4,3,2,1,0:T(8,128)(2,1)S(1)}, bf16[2,4,4,128,128]{4,3,2,1,0:T(8,128)(2,1)S(1)}, u32[]{:S(2)}, u32[]{:S(2)}) %collective-permute-start.3) | collective-permute-done | bytes 1048608 | tf_op jit(solution)/shard_map/ppermute | solution.py:353
  42.6 0.7 collective-permute-start.4
  43.3 3.5 %collective-permute-done.2.refs_7_ = bf16[2,4,4,128,128]{4,3,2,1,0:T(8,128)(2,1)S(1)} collective-permute-done((bf16[2,4,4,128,128]{4,3,2,1,0:T(8,128)(2,1)S(1)}, bf16[2,4,4,128,128]{4,3,2,1,0:T(8,128)(2,1)S(1)}, u32[]{:S(2)}, u32[]{:S(2)}) %collective-permute-start.2) | collective-permute-done | bytes 1048608 | tf_op jit(solution)/shard_map/ppermute | solution.py:353
  46.7 1.2 collective-permute-start.7
  48.0 0.0 collective-permute-done.1.refs_5_
  48.0 0.2 collective-permute-done.6.refs_2_
  48.2 0.7 collective-permute-start.9
  48.9 3.2 %collective-permute-done.5.refs_6_ = bf16[1,4,4,128,128]{4,3,2,1,0:T(8,128)(2,1)S(1)} collective-permute-done((bf16[1,4,4,128,128]{4,3,2,1,0:T(8,128)(2,1)S(1)}, bf16[1,4,4,128,128]{4,3,2,1,0:T(8,128)(2,1)S(1)}, u32[]{:S(2)}, u32[]{:S(2)}) %collective-permute-start.5) | collective-permute-done | bytes 524320 | tf_op jit(solution)/shard_map/ppermute | solution.py:353
  52.1 1.3 collective-permute-start.10
  53.4 12.9 %collective-permute-done.7.refs_13_.refs_2_ = bf16[3,4,4,128,128]{4,3,2,1,0:T(8,128)(2,1)S(1)} collective-permute-done((bf16[3,4,4,128,128]{4,3,2,1,0:T(8,128)(2,1)S(1)}, bf16[3,4,4,128,128]{4,3,2,1,0:T(8,128)(2,1)S(1)}, u32[]{:S(2)}, u32[]{:S(2)}) %collective-permute-start.7) | collective-permute-done | bytes 1572896 | tf_op jit(solution)/shard_map/ppermute | solution.py:353
  66.3 1.2 collective-permute-done.8.refs_14_.refs_3_
  67.6 0.7 collective-permute-start.11
  68.3 1.3 collective-permute-start.12
  69.6 0.1 collective-permute-start.14
  69.7 0.1 slice.18
  69.8 0.3 collective-permute-start.13
  70.1 6.0 %collective-permute-done.10.refs_11_ = bf16[2,4,4,128,128]{4,3,2,1,0:T(8,128)(2,1)S(1)} collective-permute-done((bf16[2,4,4,128,128]{4,3,2,1,0:T(8,128)(2,1)S(1)}, bf16[2,4,4,128,128]{4,3,2,1,0:T(8,128)(2,1)S(1)}, u32[]{:S(2)}, u32[]{:S(2)}) %collective-permute-start.10) | collective-permute-done | bytes 1048608 | tf_op jit(solution)/shard_map/ppermute | solution.py:353
  76.1 1.3 collective-permute-start.15
  77.4 9.9 %collective-permute-done.12.refs_10_ = bf16[1,4,4,128,128]{4,3,2,1,0:T(8,128)(2,1)S(1)} collective-permute-done((bf16[1,4,4,128,128]{4,3,2,1,0:T(8,128)(2,1)S(1)}, bf16[1,4,4,128,128]{4,3,2,1,0:T(8,128)(2,1)S(1)}, u32[]{:S(2)}, u32[]{:S(2)}) %collective-permute-start.12) | collective-permute-done | bytes 524320 | tf_op jit(solution)/shard_map/ppermute | solution.py:353
  87.3 3.1 %collective-permute-done.13.refs_16_.refs_5_ = bf16[2,4,4,128,128]{4,3,2,1,0:T(8,128)(2,1)S(1)} collective-permute-done((bf16[2,4,4,128,128]{4,3,2,1,0:T(8,128)(2,1)S(1)}, bf16[2,4,4,128,128]{4,3,2,1,0:T(8,128)(2,1)S(1)}, u32[]{:S(2)}, u32[]{:S(2)}) %collective-permute-start.13) | collective-permute-done | bytes 1048608 | tf_op jit(solution)/shard_map/ppermute | solution.py:353
  90.4 1.3 collective-permute-start.17
  91.7 7.0 %shard_map.87 = (f32[2,4,4,128,128]{4,3,2,1,0:T(8,128)S(1)}, f32[2,4,4,128,128]{4,3,2,1,0:T(8,128)S(1)}) custom-call(s32[8,18]{1,0:T(8,128)S(1)} %dynamic-slice_bitcast_fusion.tab, bf16[1,4,4,128,128]{4,3,2,1,0:T(8,128)(2,1)S(1)} %slice.17.refs_0_, bf16[2,4,4,128,128]{4,3,2,1,0:T(8,128)(2,1)S(1)} %slice.16.refs_1_, ...), custom_call_target="tpu_custom_call" | custom-call | flops 12884901888 | bytes 8912896 | tf_op jit(solution)/shard_map/pallas_call | solution.py:204
  98.8 11.0 %collective-permute-done.15.refs_0_ = bf16[2,4,4,128,128]{4,3,2,1,0:T(8,128)(2,1)S(1)} collective-permute-done((bf16[2,4,4,128,128]{4,3,2,1,0:T(8,128)(2,1)S(1)}, bf16[2,4,4,128,128]{4,3,2,1,0:T(8,128)(2,1)S(1)}, u32[]{:S(2)}, u32[]{:S(2)}) %collective-permute-start.15) | collective-permute-done | bytes 1048608 | tf_op jit(solution)/shard_map/ppermute | solution.py:353
  109.8 2.3 %shard_map.88 = (f32[4,4,128,128]{3,2,1,0:T(8,128)S(1)}, f32[4,4,128,128]{3,2,1,0:T(8,128)S(1)}) custom-call(s32[8,18]{1,0:T(8,128)S(1)} %dynamic-slice_bitcast_fusion.tab, f32[2,4,4,128,128]{4,3,2,1,0:T(8,128)S(1)} %get-tuple-element.55.kept, f32[2,4,4,128,128]{4,3,2,1,0:T(8,128)S(1)} %get-tuple-element.51.given, ...), custom_call_target="tpu_custom_call" | custom-call | flops 20000000000 | bytes 8388608 | tf_op jit(solution)/shard_map/pallas_call | solution.py:302
  112.1 6.5 %collective-permute-start.16 = (f32[4,4,128,128]{3,2,1,0:T(8,128)S(1)}, f32[4,4,128,128]{3,2,1,0:T(8,128)S(1)}, u32[]{:S(2)}, u32[]{:S(2)}) collective-permute-start(f32[4,4,128,128]{3,2,1,0:T(8,128)S(1)} %get-tuple-element.53), channel_id=1, source_target_pairs={{0,1},{1,0},{2,3},{3,2},{4,5},{5,4},{6,7},{7,6},{8,9},{9,8},{10,11... | collective-permute-start | bytes 3145736 | tf_op jit(solution)/shard_map/ppermute | solution.py:353
  118.7 1.8 %shard_map.89 = (f32[4,4,128,128]{3,2,1,0:T(8,128)S(1)}, f32[4,4,128,128]{3,2,1,0:T(8,128)S(1)}) custom-call(s32[8,18]{1,0:T(8,128)S(1)} %dynamic-slice_bitcast_fusion.tab, f32[2,4,4,128,128]{4,3,2,1,0:T(8,128)S(1)} %get-tuple-element.55.kept, f32[2,4,4,128,128]{4,3,2,1,0:T(8,128)S(1)} %get-tuple-element.51.given, ...), custom_call_target="tpu_custom_call" | custom-call | flops 20000000000 | bytes 8388608 | tf_op jit(solution)/shard_map/pallas_call | solution.py:302
  120.4 0.5 collective-permute-done.16
  120.9 0.1 add_convert_fusion.1
  121.1 1.8 %shard_map.90 = (f32[4,4,128,128]{3,2,1,0:T(8,128)S(1)}, f32[4,4,128,128]{3,2,1,0:T(8,128)S(1)}) custom-call(s32[8,18]{1,0:T(8,128)S(1)} %dynamic-slice_bitcast_fusion.tab, f32[4,4,128,128]{3,2,1,0:T(8,128)S(1)} %get-tuple-element.57.kept, f32[4,4,128,128]{3,2,1,0:T(8,128)S(1)} %get-tuple-element.61.given, ...), custom_call_target="tpu_custom_call" | custom-call | flops 20000000000 | bytes 8388608 | tf_op jit(solution)/shard_map/pallas_call | solution.py:302
  122.9 0.0 copy-start.1
  122.9 3.4 %collective-permute-start.18 = (f32[4,4,128,128]{3,2,1,0:T(8,128)S(1)}, f32[4,4,128,128]{3,2,1,0:T(8,128)S(1)}, u32[]{:S(2)}, u32[]{:S(2)}) collective-permute-start(f32[4,4,128,128]{3,2,1,0:T(8,128)S(1)} %get-tuple-element.64), channel_id=1, source_target_pairs={{0,1},{1,0},{2,3},{3,2},{4,5},{5,4},{6,7},{7,6},{8,9},{9,8},{10,11... | collective-permute-start | bytes 3145736 | tf_op jit(solution)/shard_map/ppermute | solution.py:353
  126.3 2.2 %collective-permute-start.20 = (bf16[4,4,128,128]{3,2,1,0:T(8,128)(2,1)S(1)}, bf16[4,4,128,128]{3,2,1,0:T(8,128)(2,1)S(1)}, u32[]{:S(2)}, u32[]{:S(2)}) collective-permute-start(bf16[4,4,128,128]{3,2,1,0:T(8,128)(2,1)S(1)} %add_convert_fusion.1), channel_id=1, source_target_pairs={{0,0},{1,4},{2,2},{3,6},{4,1},{5,5},{6,3},{7,7},{8,8},{9,12},{10,1... | collective-permute-start | bytes 1572872 | tf_op jit(solution)/shard_map/ppermute | solution.py:353
  128.6 0.0 collective-permute-done.18
  128.6 0.1 add_convert_fusion
  128.7 3.3 %collective-permute-start.19 = (bf16[4,4,128,128]{3,2,1,0:T(8,128)(2,1)S(1)}, bf16[4,4,128,128]{3,2,1,0:T(8,128)(2,1)S(1)}, u32[]{:S(2)}, u32[]{:S(2)}) collective-permute-start(bf16[4,4,128,128]{3,2,1,0:T(8,128)(2,1)S(1)} %add_convert_fusion), channel_id=1, source_target_pairs={{0,0},{1,4},{2,2},{3,6},{4,1},{5,5},{6,3},{7,7},{8,8},{9,12},{10,1... | collective-permute-start | bytes 1572872 | tf_op jit(solution)/shard_map/ppermute | solution.py:353
  132.0 4.8 %collective-permute-done.20 = bf16[4,4,128,128]{3,2,1,0:T(8,128)(2,1)S(1)} collective-permute-done((bf16[4,4,128,128]{3,2,1,0:T(8,128)(2,1)S(1)}, bf16[4,4,128,128]{3,2,1,0:T(8,128)(2,1)S(1)}, u32[]{:S(2)}, u32[]{:S(2)}) %collective-permute-start.20) | collective-permute-done | bytes 524320 | tf_op jit(solution)/shard_map/ppermute | solution.py:353
  136.8 5.6 %collective-permute-done.19 = bf16[4,4,128,128]{3,2,1,0:T(8,128)(2,1)S(1)} collective-permute-done((bf16[4,4,128,128]{3,2,1,0:T(8,128)(2,1)S(1)}, bf16[4,4,128,128]{3,2,1,0:T(8,128)(2,1)S(1)}, u32[]{:S(2)}, u32[]{:S(2)}) %collective-permute-start.19) | collective-permute-done | bytes 524320 | tf_op jit(solution)/shard_map/ppermute | solution.py:353
  142.4 1.1 multiply_bitcast_fusion
  (13 shorter events, 0.1 us)
Async XLA Ops:
  4.5 23.1 %collective-permute-start = (bf16[3,4,4,128,128]{4,3,2,1,0:T(8,128)(2,1)}, bf16[3,4,4,128,128]{4,3,2,1,0:T(8,128)(2,1)S(1)}, u32[]{:S(2)}, u32[]{:S(2)}) collective-permute-start(bf16[3,4,4,128,128]{4,3,2,1,0:T(8,128)(2,1)} %shard_map.86.refs_12_.refs_1_), channel_id=1, source_target_pairs={{0,0},{1,4},{2,2},{3,6},{4,1},{5,5},{6,3},{7,7},{8,8},{9,12},{10,1... | collective-permute-start | bytes 4718600 | tf_op jit(solution)/shard_map/ppermute | solution.py:353
  9.7 37.1 %copy-start = (bf16[3,4,4,128,128]{4,3,2,1,0:T(8,128)(2,1)S(1)}, bf16[3,4,4,128,128]{4,3,2,1,0:T(8,128)(2,1)}, u32[]{:S(2)}) copy-start(bf16[3,4,4,128,128]{4,3,2,1,0:T(8,128)(2,1)} %shard_map.86.refs_12_.refs_1_) | copy-start | bytes 4718596
  27.6 14.9 %collective-permute-start.3 = (bf16[2,4,4,128,128]{4,3,2,1,0:T(8,128)(2,1)S(1)}, bf16[2,4,4,128,128]{4,3,2,1,0:T(8,128)(2,1)S(1)}, u32[]{:S(2)}, u32[]{:S(2)}) collective-permute-start(bf16[2,4,4,128,128]{4,3,2,1,0:T(8,128)(2,1)S(1)} %slice.16.refs_1_), channel_id=1, source_target_pairs={{0,8},{1,9},{2,10},{3,11},{4,12},{5,13},{6,14},{7,15},{24,16},{25,... | collective-permute-start | bytes 3145736 | tf_op jit(solution)/shard_map/ppermute | solution.py:353
  30.9 15.8 %collective-permute-start.2 = (bf16[2,4,4,128,128]{4,3,2,1,0:T(8,128)(2,1)S(1)}, bf16[2,4,4,128,128]{4,3,2,1,0:T(8,128)(2,1)S(1)}, u32[]{:S(2)}, u32[]{:S(2)}) collective-permute-start(bf16[2,4,4,128,128]{4,3,2,1,0:T(8,128)(2,1)S(1)} %slice.16.refs_1_), channel_id=1, source_target_pairs={{8,0},{9,1},{10,2},{11,3},{12,4},{13,5},{14,6},{15,7},{16,24},{17,... | collective-permute-start | bytes 3145736 | tf_op jit(solution)/shard_map/ppermute | solution.py:353
  32.2 15.8 %collective-permute-start.1 = (bf16[2,4,4,128,128]{4,3,2,1,0:T(8,128)(2,1)S(1)}, bf16[2,4,4,128,128]{4,3,2,1,0:T(8,128)(2,1)S(1)}, u32[]{:S(2)}, u32[]{:S(2)}) collective-permute-start(bf16[2,4,4,128,128]{4,3,2,1,0:T(8,128)(2,1)S(1)} %slice.16.refs_1_), channel_id=1, source_target_pairs={{8,16},{9,17},{10,18},{11,19},{12,20},{13,21},{14,22},{15,23},{16,... | collective-permute-start | bytes 3145736 | tf_op jit(solution)/shard_map/ppermute | solution.py:353
  33.0 15.2 %collective-permute-start.6 = (bf16[1,4,4,128,128]{4,3,2,1,0:T(8,128)(2,1)S(1)}, bf16[1,4,4,128,128]{4,3,2,1,0:T(8,128)(2,1)S(1)}, u32[]{:S(2)}, u32[]{:S(2)}) collective-permute-start(bf16[1,4,4,128,128]{4,3,2,1,0:T(8,128)(2,1)S(1)} %slice.17.refs_0_), channel_id=1, source_target_pairs={{0,8},{1,9},{2,10},{3,11},{4,12},{5,13},{6,14},{7,15},{24,16},{25,... | collective-permute-start | bytes 1572872 | tf_op jit(solution)/shard_map/ppermute | solution.py:353
  39.5 12.5 %collective-permute-start.5 = (bf16[1,4,4,128,128]{4,3,2,1,0:T(8,128)(2,1)S(1)}, bf16[1,4,4,128,128]{4,3,2,1,0:T(8,128)(2,1)S(1)}, u32[]{:S(2)}, u32[]{:S(2)}) collective-permute-start(bf16[1,4,4,128,128]{4,3,2,1,0:T(8,128)(2,1)S(1)} %slice.17.refs_0_), channel_id=1, source_target_pairs={{8,0},{9,1},{10,2},{11,3},{12,4},{13,5},{14,6},{15,7},{16,24},{17,... | collective-permute-start | bytes 1572872 | tf_op jit(solution)/shard_map/ppermute | solution.py:353
  42.6 10.8 %collective-permute-start.4 = (bf16[1,4,4,128,128]{4,3,2,1,0:T(8,128)(2,1)S(1)}, bf16[1,4,4,128,128]{4,3,2,1,0:T(8,128)(2,1)S(1)}, u32[]{:S(2)}, u32[]{:S(2)}) collective-permute-start(bf16[1,4,4,128,128]{4,3,2,1,0:T(8,128)(2,1)S(1)} %slice.17.refs_0_), channel_id=1, source_target_pairs={{8,16},{9,17},{10,18},{11,19},{12,20},{13,21},{14,22},{15,23},{16,... | collective-permute-start | bytes 1572872 | tf_op jit(solution)/shard_map/ppermute | solution.py:353
  46.7 19.6 %collective-permute-start.7 = (bf16[3,4,4,128,128]{4,3,2,1,0:T(8,128)(2,1)S(1)}, bf16[3,4,4,128,128]{4,3,2,1,0:T(8,128)(2,1)S(1)}, u32[]{:S(2)}, u32[]{:S(2)}) collective-permute-start(bf16[3,4,4,128,128]{4,3,2,1,0:T(8,128)(2,1)S(1)} %copy-done), channel_id=1, source_target_pairs={{0,2},{1,3},{2,0},{3,1},{4,6},{5,7},{6,4},{7,5},{8,10},{9,11},{10,... | collective-permute-start | bytes 4718600 | tf_op jit(solution)/shard_map/ppermute | solution.py:353
  48.0 19.6 %collective-permute-start.8 = (bf16[3,4,4,128,128]{4,3,2,1,0:T(8,128)(2,1)S(1)}, bf16[3,4,4,128,128]{4,3,2,1,0:T(8,128)(2,1)S(1)}, u32[]{:S(2)}, u32[]{:S(2)}) collective-permute-start(bf16[3,4,4,128,128]{4,3,2,1,0:T(8,128)(2,1)S(1)} %collective-permute-done), channel_id=1, source_target_pairs={{0,4},{1,0},{2,6},{3,2},{4,5},{5,1},{6,7},{7,3},{8,12},{9,8},{10,1... | collective-permute-start | bytes 4718600 | tf_op jit(solution)/shard_map/ppermute | solution.py:353
  48.2 21.6 %collective-permute-start.9 = (bf16[2,4,4,128,128]{4,3,2,1,0:T(8,128)(2,1)S(1)}, bf16[2,4,4,128,128]{4,3,2,1,0:T(8,128)(2,1)S(1)}, u32[]{:S(2)}, u32[]{:S(2)}) collective-permute-start(bf16[2,4,4,128,128]{4,3,2,1,0:T(8,128)(2,1)S(1)} %collective-permute-done.3.refs_3_), channel_id=1, source_target_pairs={{8,16},{9,17},{10,18},{11,19},{12,20},{13,21},{14,22},{15,23},{16,... | collective-permute-start | bytes 3145736 | tf_op jit(solution)/shard_map/ppermute | solution.py:353
  52.1 24.0 %collective-permute-start.10 = (bf16[2,4,4,128,128]{4,3,2,1,0:T(8,128)(2,1)S(1)}, bf16[2,4,4,128,128]{4,3,2,1,0:T(8,128)(2,1)S(1)}, u32[]{:S(2)}, u32[]{:S(2)}) collective-permute-start(bf16[2,4,4,128,128]{4,3,2,1,0:T(8,128)(2,1)S(1)} %collective-permute-done.1.refs_5_), channel_id=1, source_target_pairs={{8,0},{9,1},{10,2},{11,3},{12,4},{13,5},{14,6},{15,7},{16,24},{17,... | collective-permute-start | bytes 3145736 | tf_op jit(solution)/shard_map/ppermute | solution.py:353
  67.6 9.8 %collective-permute-start.11 = (bf16[1,4,4,128,128]{4,3,2,1,0:T(8,128)(2,1)S(1)}, bf16[1,4,4,128,128]{4,3,2,1,0:T(8,128)(2,1)S(1)}, u32[]{:S(2)}, u32[]{:S(2)}) collective-permute-start(bf16[1,4,4,128,128]{4,3,2,1,0:T(8,128)(2,1)S(1)} %collective-permute-done.6.refs_2_), channel_id=1, source_target_pairs={{8,16},{9,17},{10,18},{11,19},{12,20},{13,21},{14,22},{15,23},{16,... | collective-permute-start | bytes 1572872 | tf_op jit(solution)/shard_map/ppermute | solution.py:353
  68.3 19.0 %collective-permute-start.12 = (bf16[1,4,4,128,128]{4,3,2,1,0:T(8,128)(2,1)S(1)}, bf16[1,4,4,128,128]{4,3,2,1,0:T(8,128)(2,1)S(1)}, u32[]{:S(2)}, u32[]{:S(2)}) collective-permute-start(bf16[1,4,4,128,128]{4,3,2,1,0:T(8,128)(2,1)S(1)} %collective-permute-done.4.refs_4_), channel_id=1, source_target_pairs={{8,0},{9,1},{10,2},{11,3},{12,4},{13,5},{14,6},{15,7},{16,24},{17,... | collective-permute-start | bytes 1572872 | tf_op jit(solution)/shard_map/ppermute | solution.py:353
  69.6 17.7 %collective-permute-start.14 = (bf16[1,4,4,128,128]{4,3,2,1,0:T(8,128)(2,1)S(1)}, bf16[1,4,4,128,128]{4,3,2,1,0:T(8,128)(2,1)S(1)}, u32[]{:S(2)}, u32[]{:S(2)}) collective-permute-start(bf16[1,4,4,128,128]{4,3,2,1,0:T(8,128)(2,1)S(1)} %slice.19), channel_id=1, source_target_pairs={{0,4},{1,5},{2,6},{3,7},{4,0},{5,1},{6,2},{7,3},{8,12},{9,13},{10,... | collective-permute-start | bytes 1572872 | tf_op jit(solution)/shard_map/ppermute | solution.py:353
  69.8 20.6 %collective-permute-start.13 = (bf16[2,4,4,128,128]{4,3,2,1,0:T(8,128)(2,1)S(1)}, bf16[2,4,4,128,128]{4,3,2,1,0:T(8,128)(2,1)S(1)}, u32[]{:S(2)}, u32[]{:S(2)}) collective-permute-start(bf16[2,4,4,128,128]{4,3,2,1,0:T(8,128)(2,1)S(1)} %slice.18), channel_id=1, source_target_pairs={{0,2},{1,3},{2,0},{3,1},{4,6},{5,7},{6,4},{7,5},{8,10},{9,11},{10,... | collective-permute-start | bytes 3145736 | tf_op jit(solution)/shard_map/ppermute | solution.py:353
  76.1 33.7 %collective-permute-start.15 = (bf16[2,4,4,128,128]{4,3,2,1,0:T(8,128)(2,1)S(1)}, bf16[2,4,4,128,128]{4,3,2,1,0:T(8,128)(2,1)S(1)}, u32[]{:S(2)}, u32[]{:S(2)}) collective-permute-start(bf16[2,4,4,128,128]{4,3,2,1,0:T(8,128)(2,1)S(1)} %collective-permute-done.9.refs_9_), channel_id=1, source_target_pairs={{8,0},{9,1},{10,2},{11,3},{12,4},{13,5},{14,6},{15,7},{16,24},{17,... | collective-permute-start | bytes 3145736 | tf_op jit(solution)/shard_map/ppermute | solution.py:353
  90.4 30.7 %collective-permute-start.17 = (bf16[1,4,4,128,128]{4,3,2,1,0:T(8,128)(2,1)S(1)}, bf16[1,4,4,128,128]{4,3,2,1,0:T(8,128)(2,1)S(1)}, u32[]{:S(2)}, u32[]{:S(2)}) collective-permute-start(bf16[1,4,4,128,128]{4,3,2,1,0:T(8,128)(2,1)S(1)} %collective-permute-done.11.refs_8_), channel_id=1, source_target_pairs={{8,0},{9,1},{10,2},{11,3},{12,4},{13,5},{14,6},{15,7},{16,24},{17,... | collective-permute-start | bytes 1572872 | tf_op jit(solution)/shard_map/ppermute | solution.py:353
  112.1 8.8 %collective-permute-start.16 = (f32[4,4,128,128]{3,2,1,0:T(8,128)S(1)}, f32[4,4,128,128]{3,2,1,0:T(8,128)S(1)}, u32[]{:S(2)}, u32[]{:S(2)}) collective-permute-start(f32[4,4,128,128]{3,2,1,0:T(8,128)S(1)} %get-tuple-element.53), channel_id=1, source_target_pairs={{0,1},{1,0},{2,3},{3,2},{4,5},{5,4},{6,7},{7,6},{8,9},{9,8},{10,11... | collective-permute-start | bytes 3145736 | tf_op jit(solution)/shard_map/ppermute | solution.py:353
  122.9 9.2 %copy-start.1 = (s32[4,1,4]{2,1,0:T(1,128)S(1)}, s32[4,1,4]{2,1,0:T(1,128)}, u32[]{:S(2)}) copy-start(s32[4,1,4]{2,1,0:T(1,128)} %refs_1_.1) | copy-start | bytes 196
  122.9 5.7 %collective-permute-start.18 = (f32[4,4,128,128]{3,2,1,0:T(8,128)S(1)}, f32[4,4,128,128]{3,2,1,0:T(8,128)S(1)}, u32[]{:S(2)}, u32[]{:S(2)}) collective-permute-start(f32[4,4,128,128]{3,2,1,0:T(8,128)S(1)} %get-tuple-element.64), channel_id=1, source_target_pairs={{0,1},{1,0},{2,3},{3,2},{4,5},{5,4},{6,7},{7,6},{8,9},{9,8},{10,11... | collective-permute-start | bytes 3145736 | tf_op jit(solution)/shard_map/ppermute | solution.py:353
  126.3 10.5 %collective-permute-start.20 = (bf16[4,4,128,128]{3,2,1,0:T(8,128)(2,1)S(1)}, bf16[4,4,128,128]{3,2,1,0:T(8,128)(2,1)S(1)}, u32[]{:S(2)}, u32[]{:S(2)}) collective-permute-start(bf16[4,4,128,128]{3,2,1,0:T(8,128)(2,1)S(1)} %add_convert_fusion.1), channel_id=1, source_target_pairs={{0,0},{1,4},{2,2},{3,6},{4,1},{5,5},{6,3},{7,7},{8,8},{9,12},{10,1... | collective-permute-start | bytes 1572872 | tf_op jit(solution)/shard_map/ppermute | solution.py:353
  128.7 13.7 %collective-permute-start.19 = (bf16[4,4,128,128]{3,2,1,0:T(8,128)(2,1)S(1)}, bf16[4,4,128,128]{3,2,1,0:T(8,128)(2,1)S(1)}, u32[]{:S(2)}, u32[]{:S(2)}) collective-permute-start(bf16[4,4,128,128]{3,2,1,0:T(8,128)(2,1)S(1)} %add_convert_fusion), channel_id=1, source_target_pairs={{0,0},{1,4},{2,2},{3,6},{4,1},{5,5},{6,3},{7,7},{8,8},{9,12},{10,1... | collective-permute-start | bytes 1572872 | tf_op jit(solution)/shard_map/ppermute | solution.py:353

commit v4 on v3

--- a/solution.py
+++ b/solution.py
@@ -405,17 +405,17 @@
     token, flight, group = closed()
     along(("mid", "out1", "in"), H)
     beside = [sent(mine, pairs) for pairs in y_pairs]
-    across = sent(unit, x_pairs)
     token, flight, group = closed()
     along(("mid2", "out2"), Q)
+    across = sent(unit, x_pairs)
     token, flight, group = closed()
     along(("mid2", "out2"), H)
     far_qd = [sent(across[1:], pairs) for pairs in y_pairs]
     far_h = [sent(value[:1], x_swap) for value in beside]
     token, flight, group = closed()
     along(("out3",), Q)
+    along(("out3",), H)
     token, flight, group = closed()
-    along(("out3",), H)
 
     near = [[(mine, H)]] + [[(value, H)] for value in beside]
     far = [[(across, H)]] + [[(a, H), (b, Q)] for a, b in zip(far_h, far_qd)]

time: 144 us -> 141 us (0.979)
  starting transfers between devices: 42 us -> 32 us
  waiting for transfers between devices: 81.6 us -> 89 us
    ppermute x21, starting transfers between devices: 42 us -> 32 us  [move(): return lax.ppermute(value, AXES, pairs)]
    ppermute x21, waiting for transfers between devices: 81.6 us -> 89 us  [move(): return lax.ppermute(value, AXES, pairs)]
  transfers between devices with their start and end apart: 21 -> 21, of which waited for: 14 -> 12; matrix products, arithmetic and copies ran while one was open for 1% -> 1% of each run, Pallas kernels for 8% -> 8%
where the time goes in v4:
time: 141 us
  waiting for transfers between devices  89 us (63%)
  starting transfers between devices  32 us (23%)
  Pallas kernels  16.4 us (12%)
    ppermute x21, waiting for transfers between devices, move(): return lax.ppermute(value, AXES, pairs)  89 us
    ppermute x21, starting transfers between devices, move(): return lax.ppermute(value, AXES, pairs)  32 us
    pallas_call x1, Pallas kernels, contract(): pl.pallas_call(functools.partial(contract_body, plan, tuple((plan.units.i...  6.75 us
    pallas_call x3, Pallas kernels, last(): pl.pallas_call(functools.partial(last_body, plan, products, firsts), in_s...  5.84 us
    pallas_call x1, Pallas kernels, keep(): pl.pallas_call(keep_body, grid=(M,), in_specs=[pl.BlockSpec(memory_space=...  3.83 us
  transfers between devices with their start and end apart: 21, of which 12 were waited for; matrix products, arithmetic and copies ran while one was open for 1% of the time, Pallas kernels for 8%

profile of v4, /device:TPU:1, one launch (start us, length us, event | category | flops | bytes accessed | tf_op | source)
XLA Modules:
  0.0 140.6 jit_solution(13754579457056165667)
XLA Ops:
  0.6 3.8 %shard_map.86.refs_12_.refs_1_ = bf16[3,4,4,128,128]{4,3,2,1,0:T(8,128)(2,1)} custom-call(s32[4,1,4]{2,1,0:T(1,128)} %refs_0_.1, s32[4,1,4]{2,1,0:T(1,128)} %refs_1_.1, s32[4,1,4]{2,1,0:T(1,128)} %refs_2_.1, bf16[4,1,4,128,128]{4,3,2,1,0:T(8,128)(2,1)} %refs_3_.1, bf16[4,1,4,128,128]{4,3,2,1,0:T(8,128)(2,1)} %refs_4_.1, bf16[4,1,4,128,128]{4,3,2,1,0:T(8,128)(2,1)} %refs_5_.1), custom_call_target="tpu_custom_call" | custom-call | tf_op jit(solution)/shard_map/pallas_call | solution.py:329
  4.5 4.5 %collective-permute-start = (bf16[3,4,4,128,128]{4,3,2,1,0:T(8,128)(2,1)}, bf16[3,4,4,128,128]{4,3,2,1,0:T(8,128)(2,1)S(1)}, u32[]{:S(2)}, u32[]{:S(2)}) collective-permute-start(bf16[3,4,4,128,128]{4,3,2,1,0:T(8,128)(2,1)} %shard_map.86.refs_12_.refs_1_), channel_id=1, source_target_pairs={{0,0},{1,4},{2,2},{3,6},{4,1},{5,5},{6,3},{7,7},{8,8},{9,12},{10,1... | collective-permute-start | bytes 4718600 | tf_op jit(solution)/shard_map/ppermute | solution.py:353
  9.0 0.7 dynamic-slice_bitcast_fusion.tab
  9.7 17.9 %collective-permute-done = bf16[3,4,4,128,128]{4,3,2,1,0:T(8,128)(2,1)S(1)} collective-permute-done((bf16[3,4,4,128,128]{4,3,2,1,0:T(8,128)(2,1)}, bf16[3,4,4,128,128]{4,3,2,1,0:T(8,128)(2,1)S(1)}, u32[]{:S(2)}, u32[]{:S(2)}) %collective-permute-start) | collective-permute-done | bytes 1572896 | tf_op jit(solution)/shard_map/ppermute | solution.py:353
  27.6 0.1 slice.17.refs_1_
  27.6 3.3 %collective-permute-start.2 = (bf16[2,4,4,128,128]{4,3,2,1,0:T(8,128)(2,1)S(1)}, bf16[2,4,4,128,128]{4,3,2,1,0:T(8,128)(2,1)S(1)}, u32[]{:S(2)}, u32[]{:S(2)}) collective-permute-start(bf16[2,4,4,128,128]{4,3,2,1,0:T(8,128)(2,1)S(1)} %slice.17.refs_1_), channel_id=1, source_target_pairs={{0,8},{1,9},{2,10},{3,11},{4,12},{5,13},{6,14},{7,15},{24,16},{25,... | collective-permute-start | bytes 3145736 | tf_op jit(solution)/shard_map/ppermute | solution.py:353
  30.9 0.7 collective-permute-start.4
  31.6 1.3 collective-permute-start.6
  33.0 4.1 %collective-permute-start.1 = (bf16[1,4,4,128,128]{4,3,2,1,0:T(8,128)(2,1)S(1)}, bf16[1,4,4,128,128]{4,3,2,1,0:T(8,128)(2,1)S(1)}, u32[]{:S(2)}, u32[]{:S(2)}) collective-permute-start(bf16[1,4,4,128,128]{4,3,2,1,0:T(8,128)(2,1)S(1)} %slice.16.refs_0_), channel_id=1, source_target_pairs={{0,8},{1,9},{2,10},{3,11},{4,12},{5,13},{6,14},{7,15},{24,16},{25,... | collective-permute-start | bytes 1572872 | tf_op jit(solution)/shard_map/ppermute | solution.py:353
  37.1 0.7 collective-permute-start.3
  37.8 4.8 %collective-permute-done.2.refs_3_ = bf16[2,4,4,128,128]{4,3,2,1,0:T(8,128)(2,1)S(1)} collective-permute-done((bf16[2,4,4,128,128]{4,3,2,1,0:T(8,128)(2,1)S(1)}, bf16[2,4,4,128,128]{4,3,2,1,0:T(8,128)(2,1)S(1)}, u32[]{:S(2)}, u32[]{:S(2)}) %collective-permute-start.2) | collective-permute-done | bytes 1048608 | tf_op jit(solution)/shard_map/ppermute | solution.py:353
  42.6 1.3 collective-permute-start.5
  43.9 1.3 collective-permute-start.7
  45.2 13.4 %collective-permute-done.6.refs_7_ = bf16[2,4,4,128,128]{4,3,2,1,0:T(8,128)(2,1)S(1)} collective-permute-done((bf16[2,4,4,128,128]{4,3,2,1,0:T(8,128)(2,1)S(1)}, bf16[2,4,4,128,128]{4,3,2,1,0:T(8,128)(2,1)S(1)}, u32[]{:S(2)}, u32[]{:S(2)}) %collective-permute-start.6) | collective-permute-done | bytes 1048608 | tf_op jit(solution)/shard_map/ppermute | solution.py:353
  58.6 0.7 collective-permute-start.9
  59.3 1.3 collective-permute-start.11
  60.6 0.0 collective-permute-done.3.refs_4_
  60.7 0.0 collective-permute-start.12
  60.7 3.3 %collective-permute-done.5.refs_6_ = bf16[1,4,4,128,128]{4,3,2,1,0:T(8,128)(2,1)S(1)} collective-permute-done((bf16[1,4,4,128,128]{4,3,2,1,0:T(8,128)(2,1)S(1)}, bf16[1,4,4,128,128]{4,3,2,1,0:T(8,128)(2,1)S(1)}, u32[]{:S(2)}, u32[]{:S(2)}) %collective-permute-start.5) | collective-permute-done | bytes 524320 | tf_op jit(solution)/shard_map/ppermute | solution.py:353
  64.0 0.0 collective-permute-done.7.refs_13_.refs_2_
  64.0 0.7 collective-permute-start.8
  64.7 1.3 collective-permute-start.10
  66.0 14.1 %collective-permute-done.12.refs_14_.refs_3_ = bf16[3,4,4,128,128]{4,3,2,1,0:T(8,128)(2,1)S(1)} collective-permute-done((bf16[3,4,4,128,128]{4,3,2,1,0:T(8,128)(2,1)S(1)}, bf16[3,4,4,128,128]{4,3,2,1,0:T(8,128)(2,1)S(1)}, u32[]{:S(2)}, u32[]{:S(2)}) %collective-permute-start.12) | collective-permute-done | bytes 1572896 | tf_op jit(solution)/shard_map/ppermute | solution.py:353
  80.1 0.0 collective-permute-start.13
  80.1 0.1 slice.19
  80.2 0.0 collective-permute-done.9.refs_9_
  80.2 0.7 collective-permute-start.14
  80.9 1.3 collective-permute-start.15
  82.2 1.3 collective-permute-start.17
  83.5 5.0 %collective-permute-done.10.refs_10_ = bf16[1,4,4,128,128]{4,3,2,1,0:T(8,128)(2,1)S(1)} collective-permute-done((bf16[1,4,4,128,128]{4,3,2,1,0:T(8,128)(2,1)S(1)}, bf16[1,4,4,128,128]{4,3,2,1,0:T(8,128)(2,1)S(1)}, u32[]{:S(2)}, u32[]{:S(2)}) %collective-permute-start.10) | collective-permute-done | bytes 524320 | tf_op jit(solution)/shard_map/ppermute | solution.py:353
  88.5 4.4 %collective-permute-done.13.refs_15_.refs_4_ = bf16[1,4,4,128,128]{4,3,2,1,0:T(8,128)(2,1)S(1)} collective-permute-done((bf16[1,4,4,128,128]{4,3,2,1,0:T(8,128)(2,1)S(1)}, bf16[1,4,4,128,128]{4,3,2,1,0:T(8,128)(2,1)S(1)}, u32[]{:S(2)}, u32[]{:S(2)}) %collective-permute-start.13) | collective-permute-done | bytes 524320 | tf_op jit(solution)/shard_map/ppermute | solution.py:353
  93.0 11.5 %collective-permute-done.14.refs_16_.refs_5_ = bf16[2,4,4,128,128]{4,3,2,1,0:T(8,128)(2,1)S(1)} collective-permute-done((bf16[2,4,4,128,128]{4,3,2,1,0:T(8,128)(2,1)S(1)}, bf16[2,4,4,128,128]{4,3,2,1,0:T(8,128)(2,1)S(1)}, u32[]{:S(2)}, u32[]{:S(2)}) %collective-permute-start.14) | collective-permute-done | bytes 1048608 | tf_op jit(solution)/shard_map/ppermute | solution.py:353
  104.5 6.7 %shard_map.87 = (f32[2,4,4,128,128]{4,3,2,1,0:T(8,128)S(1)}, f32[2,4,4,128,128]{4,3,2,1,0:T(8,128)S(1)}) custom-call(s32[8,18]{1,0:T(8,128)S(1)} %dynamic-slice_bitcast_fusion.tab, bf16[1,4,4,128,128]{4,3,2,1,0:T(8,128)(2,1)S(1)} %slice.16.refs_0_, bf16[2,4,4,128,128]{4,3,2,1,0:T(8,128)(2,1)S(1)} %slice.17.refs_1_, ...), custom_call_target="tpu_custom_call" | custom-call | flops 12884901888 | bytes 8912896 | tf_op jit(solution)/shard_map/pallas_call | solution.py:204
  111.2 2.3 %shard_map.88 = (f32[4,4,128,128]{3,2,1,0:T(8,128)S(1)}, f32[4,4,128,128]{3,2,1,0:T(8,128)S(1)}) custom-call(s32[8,18]{1,0:T(8,128)S(1)} %dynamic-slice_bitcast_fusion.tab, f32[2,4,4,128,128]{4,3,2,1,0:T(8,128)S(1)} %get-tuple-element.51.kept, f32[2,4,4,128,128]{4,3,2,1,0:T(8,128)S(1)} %get-tuple-element.46.given, ...), custom_call_target="tpu_custom_call" | custom-call | flops 20000000000 | bytes 8388608 | tf_op jit(solution)/shard_map/pallas_call | solution.py:302
  113.6 1.4 %collective-permute-start.16 = (f32[4,4,128,128]{3,2,1,0:T(8,128)S(1)}, f32[4,4,128,128]{3,2,1,0:T(8,128)S(1)}, u32[]{:S(2)}, u32[]{:S(2)}) collective-permute-start(f32[4,4,128,128]{3,2,1,0:T(8,128)S(1)} %get-tuple-element.49), channel_id=1, source_target_pairs={{0,1},{1,0},{2,3},{3,2},{4,5},{5,4},{6,7},{7,6},{8,9},{9,8},{10,11... | collective-permute-start | bytes 3145736 | tf_op jit(solution)/shard_map/ppermute | solution.py:353
  115.0 1.8 %shard_map.89 = (f32[4,4,128,128]{3,2,1,0:T(8,128)S(1)}, f32[4,4,128,128]{3,2,1,0:T(8,128)S(1)}) custom-call(s32[8,18]{1,0:T(8,128)S(1)} %dynamic-slice_bitcast_fusion.tab, f32[2,4,4,128,128]{4,3,2,1,0:T(8,128)S(1)} %get-tuple-element.51.kept, f32[2,4,4,128,128]{4,3,2,1,0:T(8,128)S(1)} %get-tuple-element.46.given, ...), custom_call_target="tpu_custom_call" | custom-call | flops 20000000000 | bytes 8388608 | tf_op jit(solution)/shard_map/pallas_call | solution.py:302
  116.8 0.5 collective-permute-done.16
  117.3 0.1 add_convert_fusion.1
  117.4 4.0 %collective-permute-done.17.refs_0_ = bf16[1,4,4,128,128]{4,3,2,1,0:T(8,128)(2,1)S(1)} collective-permute-done((bf16[1,4,4,128,128]{4,3,2,1,0:T(8,128)(2,1)S(1)}, bf16[1,4,4,128,128]{4,3,2,1,0:T(8,128)(2,1)S(1)}, u32[]{:S(2)}, u32[]{:S(2)}) %collective-permute-start.17) | collective-permute-done | bytes 524320 | tf_op jit(solution)/shard_map/ppermute | solution.py:353
  121.4 1.8 %shard_map.90 = (f32[4,4,128,128]{3,2,1,0:T(8,128)S(1)}, f32[4,4,128,128]{3,2,1,0:T(8,128)S(1)}) custom-call(s32[8,18]{1,0:T(8,128)S(1)} %dynamic-slice_bitcast_fusion.tab, f32[4,4,128,128]{3,2,1,0:T(8,128)S(1)} %get-tuple-element.53.kept, f32[4,4,128,128]{3,2,1,0:T(8,128)S(1)} %get-tuple-element.57.given, ...), custom_call_target="tpu_custom_call" | custom-call | flops 20000000000 | bytes 8388608 | tf_op jit(solution)/shard_map/pallas_call | solution.py:302
  123.2 0.0 copy-start.1
  123.2 0.2 collective-permute-start.18
  123.4 3.3 %collective-permute-start.20 = (bf16[4,4,128,128]{3,2,1,0:T(8,128)(2,1)S(1)}, bf16[4,4,128,128]{3,2,1,0:T(8,128)(2,1)S(1)}, u32[]{:S(2)}, u32[]{:S(2)}) collective-permute-start(bf16[4,4,128,128]{3,2,1,0:T(8,128)(2,1)S(1)} %add_convert_fusion.1), channel_id=1, source_target_pairs={{0,0},{1,4},{2,2},{3,6},{4,1},{5,5},{6,3},{7,7},{8,8},{9,12},{10,1... | collective-permute-start | bytes 1572872 | tf_op jit(solution)/shard_map/ppermute | solution.py:353
  126.7 0.1 add_convert_fusion
  126.8 2.6 %collective-permute-start.19 = (bf16[4,4,128,128]{3,2,1,0:T(8,128)(2,1)S(1)}, bf16[4,4,128,128]{3,2,1,0:T(8,128)(2,1)S(1)}, u32[]{:S(2)}, u32[]{:S(2)}) collective-permute-start(bf16[4,4,128,128]{3,2,1,0:T(8,128)(2,1)S(1)} %add_convert_fusion), channel_id=1, source_target_pairs={{0,0},{1,4},{2,2},{3,6},{4,1},{5,5},{6,3},{7,7},{8,8},{9,12},{10,1... | collective-permute-start | bytes 1572872 | tf_op jit(solution)/shard_map/ppermute | solution.py:353
  129.5 4.4 %collective-permute-done.20 = bf16[4,4,128,128]{3,2,1,0:T(8,128)(2,1)S(1)} collective-permute-done((bf16[4,4,128,128]{3,2,1,0:T(8,128)(2,1)S(1)}, bf16[4,4,128,128]{3,2,1,0:T(8,128)(2,1)S(1)}, u32[]{:S(2)}, u32[]{:S(2)}) %collective-permute-start.20) | collective-permute-done | bytes 524320 | tf_op jit(solution)/shard_map/ppermute | solution.py:353
  133.9 5.6 %collective-permute-done.19 = bf16[4,4,128,128]{3,2,1,0:T(8,128)(2,1)S(1)} collective-permute-done((bf16[4,4,128,128]{3,2,1,0:T(8,128)(2,1)S(1)}, bf16[4,4,128,128]{3,2,1,0:T(8,128)(2,1)S(1)}, u32[]{:S(2)}, u32[]{:S(2)}) %collective-permute-start.19) | collective-permute-done | bytes 524320 | tf_op jit(solution)/shard_map/ppermute | solution.py:353
  139.5 1.1 multiply_bitcast_fusion
  (13 shorter events, 0.1 us)
Async XLA Ops:
  4.5 23.1 %collective-permute-start = (bf16[3,4,4,128,128]{4,3,2,1,0:T(8,128)(2,1)}, bf16[3,4,4,128,128]{4,3,2,1,0:T(8,128)(2,1)S(1)}, u32[]{:S(2)}, u32[]{:S(2)}) collective-permute-start(bf16[3,4,4,128,128]{4,3,2,1,0:T(8,128)(2,1)} %shard_map.86.refs_12_.refs_1_), channel_id=1, source_target_pairs={{0,0},{1,4},{2,2},{3,6},{4,1},{5,5},{6,3},{7,7},{8,8},{9,12},{10,1... | collective-permute-start | bytes 4718600 | tf_op jit(solution)/shard_map/ppermute | solution.py:353
  9.7 34.2 %copy-start = (bf16[3,4,4,128,128]{4,3,2,1,0:T(8,128)(2,1)S(1)}, bf16[3,4,4,128,128]{4,3,2,1,0:T(8,128)(2,1)}, u32[]{:S(2)}) copy-start(bf16[3,4,4,128,128]{4,3,2,1,0:T(8,128)(2,1)} %shard_map.86.refs_12_.refs_1_) | copy-start | bytes 4718596
  27.6 14.9 %collective-permute-start.2 = (bf16[2,4,4,128,128]{4,3,2,1,0:T(8,128)(2,1)S(1)}, bf16[2,4,4,128,128]{4,3,2,1,0:T(8,128)(2,1)S(1)}, u32[]{:S(2)}, u32[]{:S(2)}) collective-permute-start(bf16[2,4,4,128,128]{4,3,2,1,0:T(8,128)(2,1)S(1)} %slice.17.refs_1_), channel_id=1, source_target_pairs={{0,8},{1,9},{2,10},{3,11},{4,12},{5,13},{6,14},{7,15},{24,16},{25,... | collective-permute-start | bytes 3145736 | tf_op jit(solution)/shard_map/ppermute | solution.py:353
  30.9 13.0 %collective-permute-start.4 = (bf16[2,4,4,128,128]{4,3,2,1,0:T(8,128)(2,1)S(1)}, bf16[2,4,4,128,128]{4,3,2,1,0:T(8,128)(2,1)S(1)}, u32[]{:S(2)}, u32[]{:S(2)}) collective-permute-start(bf16[2,4,4,128,128]{4,3,2,1,0:T(8,128)(2,1)S(1)} %slice.17.refs_1_), channel_id=1, source_target_pairs={{8,16},{9,17},{10,18},{11,19},{12,20},{13,21},{14,22},{15,23},{16,... | collective-permute-start | bytes 3145736 | tf_op jit(solution)/shard_map/ppermute | solution.py:353
  31.6 27.0 %collective-permute-start.6 = (bf16[2,4,4,128,128]{4,3,2,1,0:T(8,128)(2,1)S(1)}, bf16[2,4,4,128,128]{4,3,2,1,0:T(8,128)(2,1)S(1)}, u32[]{:S(2)}, u32[]{:S(2)}) collective-permute-start(bf16[2,4,4,128,128]{4,3,2,1,0:T(8,128)(2,1)S(1)} %slice.17.refs_1_), channel_id=1, source_target_pairs={{8,0},{9,1},{10,2},{11,3},{12,4},{13,5},{14,6},{15,7},{16,24},{17,... | collective-permute-start | bytes 3145736 | tf_op jit(solution)/shard_map/ppermute | solution.py:353
  33.0 26.3 %collective-permute-start.1 = (bf16[1,4,4,128,128]{4,3,2,1,0:T(8,128)(2,1)S(1)}, bf16[1,4,4,128,128]{4,3,2,1,0:T(8,128)(2,1)S(1)}, u32[]{:S(2)}, u32[]{:S(2)}) collective-permute-start(bf16[1,4,4,128,128]{4,3,2,1,0:T(8,128)(2,1)S(1)} %slice.16.refs_0_), channel_id=1, source_target_pairs={{0,8},{1,9},{2,10},{3,11},{4,12},{5,13},{6,14},{7,15},{24,16},{25,... | collective-permute-start | bytes 1572872 | tf_op jit(solution)/shard_map/ppermute | solution.py:353
  37.1 23.6 %collective-permute-start.3 = (bf16[1,4,4,128,128]{4,3,2,1,0:T(8,128)(2,1)S(1)}, bf16[1,4,4,128,128]{4,3,2,1,0:T(8,128)(2,1)S(1)}, u32[]{:S(2)}, u32[]{:S(2)}) collective-permute-start(bf16[1,4,4,128,128]{4,3,2,1,0:T(8,128)(2,1)S(1)} %slice.16.refs_0_), channel_id=1, source_target_pairs={{8,16},{9,17},{10,18},{11,19},{12,20},{13,21},{14,22},{15,23},{16,... | collective-permute-start | bytes 1572872 | tf_op jit(solution)/shard_map/ppermute | solution.py:353
  42.6 21.4 %collective-permute-start.5 = (bf16[1,4,4,128,128]{4,3,2,1,0:T(8,128)(2,1)S(1)}, bf16[1,4,4,128,128]{4,3,2,1,0:T(8,128)(2,1)S(1)}, u32[]{:S(2)}, u32[]{:S(2)}) collective-permute-start(bf16[1,4,4,128,128]{4,3,2,1,0:T(8,128)(2,1)S(1)} %slice.16.refs_0_), channel_id=1, source_target_pairs={{8,0},{9,1},{10,2},{11,3},{12,4},{13,5},{14,6},{15,7},{16,24},{17,... | collective-permute-start | bytes 1572872 | tf_op jit(solution)/shard_map/ppermute | solution.py:353
  43.9 20.1 %collective-permute-start.7 = (bf16[3,4,4,128,128]{4,3,2,1,0:T(8,128)(2,1)S(1)}, bf16[3,4,4,128,128]{4,3,2,1,0:T(8,128)(2,1)S(1)}, u32[]{:S(2)}, u32[]{:S(2)}) collective-permute-start(bf16[3,4,4,128,128]{4,3,2,1,0:T(8,128)(2,1)S(1)} %copy-done), channel_id=1, source_target_pairs={{0,2},{1,3},{2,0},{3,1},{4,6},{5,7},{6,4},{7,5},{8,10},{9,11},{10,... | collective-permute-start | bytes 4718600 | tf_op jit(solution)/shard_map/ppermute | solution.py:353
  58.6 21.6 %collective-permute-start.9 = (bf16[2,4,4,128,128]{4,3,2,1,0:T(8,128)(2,1)S(1)}, bf16[2,4,4,128,128]{4,3,2,1,0:T(8,128)(2,1)S(1)}, u32[]{:S(2)}, u32[]{:S(2)}) collective-permute-start(bf16[2,4,4,128,128]{4,3,2,1,0:T(8,128)(2,1)S(1)} %collective-permute-done.2.refs_3_), channel_id=1, source_target_pairs={{8,16},{9,17},{10,18},{11,19},{12,20},{13,21},{14,22},{15,23},{16,... | collective-permute-start | bytes 3145736 | tf_op jit(solution)/shard_map/ppermute | solution.py:353
  59.3 21.6 %collective-permute-start.11 = (bf16[2,4,4,128,128]{4,3,2,1,0:T(8,128)(2,1)S(1)}, bf16[2,4,4,128,128]{4,3,2,1,0:T(8,128)(2,1)S(1)}, u32[]{:S(2)}, u32[]{:S(2)}) collective-permute-start(bf16[2,4,4,128,128]{4,3,2,1,0:T(8,128)(2,1)S(1)} %collective-permute-done.4.refs_5_), channel_id=1, source_target_pairs={{8,0},{9,1},{10,2},{11,3},{12,4},{13,5},{14,6},{15,7},{16,24},{17,... | collective-permute-start | bytes 3145736 | tf_op jit(solution)/shard_map/ppermute | solution.py:353
  60.7 19.4 %collective-permute-start.12 = (bf16[3,4,4,128,128]{4,3,2,1,0:T(8,128)(2,1)S(1)}, bf16[3,4,4,128,128]{4,3,2,1,0:T(8,128)(2,1)S(1)}, u32[]{:S(2)}, u32[]{:S(2)}) collective-permute-start(bf16[3,4,4,128,128]{4,3,2,1,0:T(8,128)(2,1)S(1)} %collective-permute-done), channel_id=1, source_target_pairs={{0,4},{1,0},{2,6},{3,2},{4,5},{5,1},{6,7},{7,3},{8,12},{9,8},{10,1... | collective-permute-start | bytes 4718600 | tf_op jit(solution)/shard_map/ppermute | solution.py:353
  64.0 18.2 %collective-permute-start.8 = (bf16[1,4,4,128,128]{4,3,2,1,0:T(8,128)(2,1)S(1)}, bf16[1,4,4,128,128]{4,3,2,1,0:T(8,128)(2,1)S(1)}, u32[]{:S(2)}, u32[]{:S(2)}) collective-permute-start(bf16[1,4,4,128,128]{4,3,2,1,0:T(8,128)(2,1)S(1)} %collective-permute-done.1.refs_2_), channel_id=1, source_target_pairs={{8,16},{9,17},{10,18},{11,19},{12,20},{13,21},{14,22},{15,23},{16,... | collective-permute-start | bytes 1572872 | tf_op jit(solution)/shard_map/ppermute | solution.py:353
  64.7 23.9 %collective-permute-start.10 = (bf16[1,4,4,128,128]{4,3,2,1,0:T(8,128)(2,1)S(1)}, bf16[1,4,4,128,128]{4,3,2,1,0:T(8,128)(2,1)S(1)}, u32[]{:S(2)}, u32[]{:S(2)}) collective-permute-start(bf16[1,4,4,128,128]{4,3,2,1,0:T(8,128)(2,1)S(1)} %collective-permute-done.3.refs_4_), channel_id=1, source_target_pairs={{8,0},{9,1},{10,2},{11,3},{12,4},{13,5},{14,6},{15,7},{16,24},{17,... | collective-permute-start | bytes 1572872 | tf_op jit(solution)/shard_map/ppermute | solution.py:353
  80.1 12.9 %collective-permute-start.13 = (bf16[1,4,4,128,128]{4,3,2,1,0:T(8,128)(2,1)S(1)}, bf16[1,4,4,128,128]{4,3,2,1,0:T(8,128)(2,1)S(1)}, u32[]{:S(2)}, u32[]{:S(2)}) collective-permute-start(bf16[1,4,4,128,128]{4,3,2,1,0:T(8,128)(2,1)S(1)} %slice.18), channel_id=1, source_target_pairs={{0,4},{1,5},{2,6},{3,7},{4,0},{5,1},{6,2},{7,3},{8,12},{9,13},{10,... | collective-permute-start | bytes 1572872 | tf_op jit(solution)/shard_map/ppermute | solution.py:353
  80.2 24.3 %collective-permute-start.14 = (bf16[2,4,4,128,128]{4,3,2,1,0:T(8,128)(2,1)S(1)}, bf16[2,4,4,128,128]{4,3,2,1,0:T(8,128)(2,1)S(1)}, u32[]{:S(2)}, u32[]{:S(2)}) collective-permute-start(bf16[2,4,4,128,128]{4,3,2,1,0:T(8,128)(2,1)S(1)} %slice.19), channel_id=1, source_target_pairs={{0,2},{1,3},{2,0},{3,1},{4,6},{5,7},{6,4},{7,5},{8,10},{9,11},{10,... | collective-permute-start | bytes 3145736 | tf_op jit(solution)/shard_map/ppermute | solution.py:353
  80.9 30.3 %collective-permute-start.15 = (bf16[2,4,4,128,128]{4,3,2,1,0:T(8,128)(2,1)S(1)}, bf16[2,4,4,128,128]{4,3,2,1,0:T(8,128)(2,1)S(1)}, u32[]{:S(2)}, u32[]{:S(2)}) collective-permute-start(bf16[2,4,4,128,128]{4,3,2,1,0:T(8,128)(2,1)S(1)} %collective-permute-done.9.refs_9_), channel_id=1, source_target_pairs={{8,0},{9,1},{10,2},{11,3},{12,4},{13,5},{14,6},{15,7},{16,24},{17,... | collective-permute-start | bytes 3145736 | tf_op jit(solution)/shard_map/ppermute | solution.py:353
  82.2 39.2 %collective-permute-start.17 = (bf16[1,4,4,128,128]{4,3,2,1,0:T(8,128)(2,1)S(1)}, bf16[1,4,4,128,128]{4,3,2,1,0:T(8,128)(2,1)S(1)}, u32[]{:S(2)}, u32[]{:S(2)}) collective-permute-start(bf16[1,4,4,128,128]{4,3,2,1,0:T(8,128)(2,1)S(1)} %collective-permute-done.8.refs_8_), channel_id=1, source_target_pairs={{8,0},{9,1},{10,2},{11,3},{12,4},{13,5},{14,6},{15,7},{16,24},{17,... | collective-permute-start | bytes 1572872 | tf_op jit(solution)/shard_map/ppermute | solution.py:353
  113.6 3.7 %collective-permute-start.16 = (f32[4,4,128,128]{3,2,1,0:T(8,128)S(1)}, f32[4,4,128,128]{3,2,1,0:T(8,128)S(1)}, u32[]{:S(2)}, u32[]{:S(2)}) collective-permute-start(f32[4,4,128,128]{3,2,1,0:T(8,128)S(1)} %get-tuple-element.49), channel_id=1, source_target_pairs={{0,1},{1,0},{2,3},{3,2},{4,5},{5,4},{6,7},{7,6},{8,9},{9,8},{10,11... | collective-permute-start | bytes 3145736 | tf_op jit(solution)/shard_map/ppermute | solution.py:353
  123.2 6.3 %copy-start.1 = (s32[4,1,4]{2,1,0:T(1,128)S(1)}, s32[4,1,4]{2,1,0:T(1,128)}, u32[]{:S(2)}) copy-start(s32[4,1,4]{2,1,0:T(1,128)} %refs_1_.1) | copy-start | bytes 196
  123.2 3.5 %collective-permute-start.18 = (f32[4,4,128,128]{3,2,1,0:T(8,128)S(1)}, f32[4,4,128,128]{3,2,1,0:T(8,128)S(1)}, u32[]{:S(2)}, u32[]{:S(2)}) collective-permute-start(f32[4,4,128,128]{3,2,1,0:T(8,128)S(1)} %get-tuple-element.60), channel_id=1, source_target_pairs={{0,1},{1,0},{2,3},{3,2},{4,5},{5,4},{6,7},{7,6},{8,9},{9,8},{10,11... | collective-permute-start | bytes 3145736 | tf_op jit(solution)/shard_map/ppermute | solution.py:353
  123.4 10.5 %collective-permute-start.20 = (bf16[4,4,128,128]{3,2,1,0:T(8,128)(2,1)S(1)}, bf16[4,4,128,128]{3,2,1,0:T(8,128)(2,1)S(1)}, u32[]{:S(2)}, u32[]{:S(2)}) collective-permute-start(bf16[4,4,128,128]{3,2,1,0:T(8,128)(2,1)S(1)} %add_convert_fusion.1), channel_id=1, source_target_pairs={{0,0},{1,4},{2,2},{3,6},{4,1},{5,5},{6,3},{7,7},{8,8},{9,12},{10,1... | collective-permute-start | bytes 1572872 | tf_op jit(solution)/shard_map/ppermute | solution.py:353
  126.8 12.7 %collective-permute-start.19 = (bf16[4,4,128,128]{3,2,1,0:T(8,128)(2,1)S(1)}, bf16[4,4,128,128]{3,2,1,0:T(8,128)(2,1)S(1)}, u32[]{:S(2)}, u32[]{:S(2)}) collective-permute-start(bf16[4,4,128,128]{3,2,1,0:T(8,128)(2,1)S(1)} %add_convert_fusion), channel_id=1, source_target_pairs={{0,0},{1,4},{2,2},{3,6},{4,1},{5,5},{6,3},{7,7},{8,8},{9,12},{10,1... | collective-permute-start | bytes 1572872 | tf_op jit(solution)/shard_map/ppermute | solution.py:353

commit v5 on v4

--- a/solution.py
+++ b/solution.py
@@ -410,15 +410,15 @@
     across = sent(unit, x_pairs)
     token, flight, group = closed()
     along(("mid2", "out2"), H)
-    far_qd = [sent(across[1:], pairs) for pairs in y_pairs]
-    far_h = [sent(value[:1], x_swap) for value in beside]
+    far_hq = [sent(across[:2], pairs) for pairs in y_pairs]
+    far_d = [sent(value[2:], x_swap) for value in beside]
     token, flight, group = closed()
     along(("out3",), Q)
     along(("out3",), H)
     token, flight, group = closed()
 
     near = [[(mine, H)]] + [[(value, H)] for value in beside]
-    far = [[(across, H)]] + [[(a, H), (b, Q)] for a, b in zip(far_h, far_qd)]
+    far = [[(across, H)]] + [[(a, H), (b, D)] for a, b in zip(far_hq, far_d)]
     early = ["own", "in", "mid", "out1", "mid2", "out2"]
     pieces = {name: [(parts[H], H), (parts[Q], Q)] for name, parts in got.items()}
     kept, given = contract(plan, after(tab, token), near, far, early, (H, D), pieces)

time: 141 us -> 141 us (level)
  no operation moved by 1% of the time
where the time goes in v5:
time: 141 us
  waiting for transfers between devices  88.9 us (63%)
  starting transfers between devices  32 us (23%)
  Pallas kernels  16.4 us (12%)
    ppermute x21, waiting for transfers between devices, move(): return lax.ppermute(value, AXES, pairs)  88.9 us
    ppermute x21, starting transfers between devices, move(): return lax.ppermute(value, AXES, pairs)  32 us
    pallas_call x1, Pallas kernels, contract(): pl.pallas_call(functools.partial(contract_body, plan, tuple((plan.units.i...  6.75 us
    pallas_call x3, Pallas kernels, last(): pl.pallas_call(functools.partial(last_body, plan, products, firsts), in_s...  5.85 us
    pallas_call x1, Pallas kernels, keep(): pl.pallas_call(keep_body, grid=(M,), in_specs=[pl.BlockSpec(memory_space=...  3.83 us
  transfers between devices with their start and end apart: 21, of which 12 were waited for; matrix products, arithmetic and copies ran while one was open for 1% of the time, Pallas kernels for 8%

profile of v5, /device:TPU:1, one launch (start us, length us, event | category | flops | bytes accessed | tf_op | source)
XLA Modules:
  0.0 140.6 jit_solution(9700824701099563931)
XLA Ops:
  0.6 3.8 %shard_map.86.refs_12_.refs_1_ = bf16[3,4,4,128,128]{4,3,2,1,0:T(8,128)(2,1)} custom-call(s32[4,1,4]{2,1,0:T(1,128)} %refs_0_.1, s32[4,1,4]{2,1,0:T(1,128)} %refs_1_.1, s32[4,1,4]{2,1,0:T(1,128)} %refs_2_.1, bf16[4,1,4,128,128]{4,3,2,1,0:T(8,128)(2,1)} %refs_3_.1, bf16[4,1,4,128,128]{4,3,2,1,0:T(8,128)(2,1)} %refs_4_.1, bf16[4,1,4,128,128]{4,3,2,1,0:T(8,128)(2,1)} %refs_5_.1), custom_call_target="tpu_custom_call" | custom-call | tf_op jit(solution)/shard_map/pallas_call | solution.py:329
  4.5 4.5 %collective-permute-start = (bf16[3,4,4,128,128]{4,3,2,1,0:T(8,128)(2,1)}, bf16[3,4,4,128,128]{4,3,2,1,0:T(8,128)(2,1)S(1)}, u32[]{:S(2)}, u32[]{:S(2)}) collective-permute-start(bf16[3,4,4,128,128]{4,3,2,1,0:T(8,128)(2,1)} %shard_map.86.refs_12_.refs_1_), channel_id=1, source_target_pairs={{0,0},{1,4},{2,2},{3,6},{4,1},{5,5},{6,3},{7,7},{8,8},{9,12},{10,1... | collective-permute-start | bytes 4718600 | tf_op jit(solution)/shard_map/ppermute | solution.py:353
  9.0 0.7 dynamic-slice_bitcast_fusion.tab
  9.7 17.9 %collective-permute-done = bf16[3,4,4,128,128]{4,3,2,1,0:T(8,128)(2,1)S(1)} collective-permute-done((bf16[3,4,4,128,128]{4,3,2,1,0:T(8,128)(2,1)}, bf16[3,4,4,128,128]{4,3,2,1,0:T(8,128)(2,1)S(1)}, u32[]{:S(2)}, u32[]{:S(2)}) %collective-permute-start) | collective-permute-done | bytes 1572896 | tf_op jit(solution)/shard_map/ppermute | solution.py:353
  27.6 0.1 slice.17.refs_1_
  27.6 3.3 %collective-permute-start.2 = (bf16[2,4,4,128,128]{4,3,2,1,0:T(8,128)(2,1)S(1)}, bf16[2,4,4,128,128]{4,3,2,1,0:T(8,128)(2,1)S(1)}, u32[]{:S(2)}, u32[]{:S(2)}) collective-permute-start(bf16[2,4,4,128,128]{4,3,2,1,0:T(8,128)(2,1)S(1)} %slice.17.refs_1_), channel_id=1, source_target_pairs={{0,8},{1,9},{2,10},{3,11},{4,12},{5,13},{6,14},{7,15},{24,16},{25,... | collective-permute-start | bytes 3145736 | tf_op jit(solution)/shard_map/ppermute | solution.py:353
  30.9 0.7 collective-permute-start.4
  31.6 1.3 collective-permute-start.6
  33.0 4.1 %collective-permute-start.1 = (bf16[1,4,4,128,128]{4,3,2,1,0:T(8,128)(2,1)S(1)}, bf16[1,4,4,128,128]{4,3,2,1,0:T(8,128)(2,1)S(1)}, u32[]{:S(2)}, u32[]{:S(2)}) collective-permute-start(bf16[1,4,4,128,128]{4,3,2,1,0:T(8,128)(2,1)S(1)} %slice.16.refs_0_), channel_id=1, source_target_pairs={{0,8},{1,9},{2,10},{3,11},{4,12},{5,13},{6,14},{7,15},{24,16},{25,... | collective-permute-start | bytes 1572872 | tf_op jit(solution)/shard_map/ppermute | solution.py:353
  37.1 0.7 collective-permute-start.3
  37.8 4.8 %collective-permute-done.2.refs_3_ = bf16[2,4,4,128,128]{4,3,2,1,0:T(8,128)(2,1)S(1)} collective-permute-done((bf16[2,4,4,128,128]{4,3,2,1,0:T(8,128)(2,1)S(1)}, bf16[2,4,4,128,128]{4,3,2,1,0:T(8,128)(2,1)S(1)}, u32[]{:S(2)}, u32[]{:S(2)}) %collective-permute-start.2) | collective-permute-done | bytes 1048608 | tf_op jit(solution)/shard_map/ppermute | solution.py:353
  42.6 1.3 collective-permute-start.5
  43.9 1.3 collective-permute-start.7
  45.2 13.4 %collective-permute-done.6.refs_7_ = bf16[2,4,4,128,128]{4,3,2,1,0:T(8,128)(2,1)S(1)} collective-permute-done((bf16[2,4,4,128,128]{4,3,2,1,0:T(8,128)(2,1)S(1)}, bf16[2,4,4,128,128]{4,3,2,1,0:T(8,128)(2,1)S(1)}, u32[]{:S(2)}, u32[]{:S(2)}) %collective-permute-start.6) | collective-permute-done | bytes 1048608 | tf_op jit(solution)/shard_map/ppermute | solution.py:353
  58.6 0.7 collective-permute-start.9
  59.3 1.3 collective-permute-start.11
  60.6 0.0 collective-permute-done.3.refs_4_
  60.7 0.0 collective-permute-start.12
  60.7 3.3 %collective-permute-done.5.refs_6_ = bf16[1,4,4,128,128]{4,3,2,1,0:T(8,128)(2,1)S(1)} collective-permute-done((bf16[1,4,4,128,128]{4,3,2,1,0:T(8,128)(2,1)S(1)}, bf16[1,4,4,128,128]{4,3,2,1,0:T(8,128)(2,1)S(1)}, u32[]{:S(2)}, u32[]{:S(2)}) %collective-permute-start.5) | collective-permute-done | bytes 524320 | tf_op jit(solution)/shard_map/ppermute | solution.py:353
  64.0 0.0 collective-permute-done.7.refs_13_.refs_2_
  64.0 0.7 collective-permute-start.8
  64.7 1.3 collective-permute-start.10
  66.0 14.1 %collective-permute-done.12.refs_14_.refs_3_ = bf16[3,4,4,128,128]{4,3,2,1,0:T(8,128)(2,1)S(1)} collective-permute-done((bf16[3,4,4,128,128]{4,3,2,1,0:T(8,128)(2,1)S(1)}, bf16[3,4,4,128,128]{4,3,2,1,0:T(8,128)(2,1)S(1)}, u32[]{:S(2)}, u32[]{:S(2)}) %collective-permute-start.12) | collective-permute-done | bytes 1572896 | tf_op jit(solution)/shard_map/ppermute | solution.py:353
  80.1 0.0 collective-permute-start.14
  80.1 0.1 slice.18
  80.2 0.0 collective-permute-done.9.refs_9_
  80.2 0.7 collective-permute-start.13
  80.9 1.3 collective-permute-start.15
  82.2 1.3 collective-permute-start.17
  83.5 5.0 %collective-permute-done.10.refs_10_ = bf16[1,4,4,128,128]{4,3,2,1,0:T(8,128)(2,1)S(1)} collective-permute-done((bf16[1,4,4,128,128]{4,3,2,1,0:T(8,128)(2,1)S(1)}, bf16[1,4,4,128,128]{4,3,2,1,0:T(8,128)(2,1)S(1)}, u32[]{:S(2)}, u32[]{:S(2)}) %collective-permute-start.10) | collective-permute-done | bytes 524320 | tf_op jit(solution)/shard_map/ppermute | solution.py:353
  88.5 4.4 %collective-permute-done.14.refs_16_.refs_5_ = bf16[1,4,4,128,128]{4,3,2,1,0:T(8,128)(2,1)S(1)} collective-permute-done((bf16[1,4,4,128,128]{4,3,2,1,0:T(8,128)(2,1)S(1)}, bf16[1,4,4,128,128]{4,3,2,1,0:T(8,128)(2,1)S(1)}, u32[]{:S(2)}, u32[]{:S(2)}) %collective-permute-start.14) | collective-permute-done | bytes 524320 | tf_op jit(solution)/shard_map/ppermute | solution.py:353
  93.0 11.5 %collective-permute-done.13.refs_15_.refs_4_ = bf16[2,4,4,128,128]{4,3,2,1,0:T(8,128)(2,1)S(1)} collective-permute-done((bf16[2,4,4,128,128]{4,3,2,1,0:T(8,128)(2,1)S(1)}, bf16[2,4,4,128,128]{4,3,2,1,0:T(8,128)(2,1)S(1)}, u32[]{:S(2)}, u32[]{:S(2)}) %collective-permute-start.13) | collective-permute-done | bytes 1048608 | tf_op jit(solution)/shard_map/ppermute | solution.py:353
  104.5 6.7 %shard_map.87 = (f32[2,4,4,128,128]{4,3,2,1,0:T(8,128)S(1)}, f32[2,4,4,128,128]{4,3,2,1,0:T(8,128)S(1)}) custom-call(s32[8,18]{1,0:T(8,128)S(1)} %dynamic-slice_bitcast_fusion.tab, bf16[1,4,4,128,128]{4,3,2,1,0:T(8,128)(2,1)S(1)} %slice.16.refs_0_, bf16[2,4,4,128,128]{4,3,2,1,0:T(8,128)(2,1)S(1)} %slice.17.refs_1_, ...), custom_call_target="tpu_custom_call" | custom-call | flops 12884901888 | bytes 8912896 | tf_op jit(solution)/shard_map/pallas_call | solution.py:204
  111.2 2.3 %shard_map.88 = (f32[4,4,128,128]{3,2,1,0:T(8,128)S(1)}, f32[4,4,128,128]{3,2,1,0:T(8,128)S(1)}) custom-call(s32[8,18]{1,0:T(8,128)S(1)} %dynamic-slice_bitcast_fusion.tab, f32[2,4,4,128,128]{4,3,2,1,0:T(8,128)S(1)} %get-tuple-element.51.kept, f32[2,4,4,128,128]{4,3,2,1,0:T(8,128)S(1)} %get-tuple-element.46.given, ...), custom_call_target="tpu_custom_call" | custom-call | flops 20000000000 | bytes 8388608 | tf_op jit(solution)/shard_map/pallas_call | solution.py:302
  113.6 1.4 %collective-permute-start.16 = (f32[4,4,128,128]{3,2,1,0:T(8,128)S(1)}, f32[4,4,128,128]{3,2,1,0:T(8,128)S(1)}, u32[]{:S(2)}, u32[]{:S(2)}) collective-permute-start(f32[4,4,128,128]{3,2,1,0:T(8,128)S(1)} %get-tuple-element.49), channel_id=1, source_target_pairs={{0,1},{1,0},{2,3},{3,2},{4,5},{5,4},{6,7},{7,6},{8,9},{9,8},{10,11... | collective-permute-start | bytes 3145736 | tf_op jit(solution)/shard_map/ppermute | solution.py:353
  115.0 1.8 %shard_map.89 = (f32[4,4,128,128]{3,2,1,0:T(8,128)S(1)}, f32[4,4,128,128]{3,2,1,0:T(8,128)S(1)}) custom-call(s32[8,18]{1,0:T(8,128)S(1)} %dynamic-slice_bitcast_fusion.tab, f32[2,4,4,128,128]{4,3,2,1,0:T(8,128)S(1)} %get-tuple-element.51.kept, f32[2,4,4,128,128]{4,3,2,1,0:T(8,128)S(1)} %get-tuple-element.46.given, ...), custom_call_target="tpu_custom_call" | custom-call | flops 20000000000 | bytes 8388608 | tf_op jit(solution)/shard_map/pallas_call | solution.py:302
  116.8 0.5 collective-permute-done.16
  117.3 0.1 add_convert_fusion.1
  117.4 4.0 %collective-permute-done.17.refs_0_ = bf16[1,4,4,128,128]{4,3,2,1,0:T(8,128)(2,1)S(1)} collective-permute-done((bf16[1,4,4,128,128]{4,3,2,1,0:T(8,128)(2,1)S(1)}, bf16[1,4,4,128,128]{4,3,2,1,0:T(8,128)(2,1)S(1)}, u32[]{:S(2)}, u32[]{:S(2)}) %collective-permute-start.17) | collective-permute-done | bytes 524320 | tf_op jit(solution)/shard_map/ppermute | solution.py:353
  121.4 1.8 %shard_map.90 = (f32[4,4,128,128]{3,2,1,0:T(8,128)S(1)}, f32[4,4,128,128]{3,2,1,0:T(8,128)S(1)}) custom-call(s32[8,18]{1,0:T(8,128)S(1)} %dynamic-slice_bitcast_fusion.tab, f32[4,4,128,128]{3,2,1,0:T(8,128)S(1)} %get-tuple-element.53.kept, f32[4,4,128,128]{3,2,1,0:T(8,128)S(1)} %get-tuple-element.57.given, ...), custom_call_target="tpu_custom_call" | custom-call | flops 20000000000 | bytes 8388608 | tf_op jit(solution)/shard_map/pallas_call | solution.py:302
  123.2 0.0 copy-start.1
  123.2 0.2 collective-permute-start.18
  123.4 3.3 %collective-permute-start.20 = (bf16[4,4,128,128]{3,2,1,0:T(8,128)(2,1)S(1)}, bf16[4,4,128,128]{3,2,1,0:T(8,128)(2,1)S(1)}, u32[]{:S(2)}, u32[]{:S(2)}) collective-permute-start(bf16[4,4,128,128]{3,2,1,0:T(8,128)(2,1)S(1)} %add_convert_fusion.1), channel_id=1, source_target_pairs={{0,0},{1,4},{2,2},{3,6},{4,1},{5,5},{6,3},{7,7},{8,8},{9,12},{10,1... | collective-permute-start | bytes 1572872 | tf_op jit(solution)/shard_map/ppermute | solution.py:353
  126.7 0.1 add_convert_fusion
  126.8 2.6 %collective-permute-start.19 = (bf16[4,4,128,128]{3,2,1,0:T(8,128)(2,1)S(1)}, bf16[4,4,128,128]{3,2,1,0:T(8,128)(2,1)S(1)}, u32[]{:S(2)}, u32[]{:S(2)}) collective-permute-start(bf16[4,4,128,128]{3,2,1,0:T(8,128)(2,1)S(1)} %add_convert_fusion), channel_id=1, source_target_pairs={{0,0},{1,4},{2,2},{3,6},{4,1},{5,5},{6,3},{7,7},{8,8},{9,12},{10,1... | collective-permute-start | bytes 1572872 | tf_op jit(solution)/shard_map/ppermute | solution.py:353
  129.5 4.4 %collective-permute-done.20 = bf16[4,4,128,128]{3,2,1,0:T(8,128)(2,1)S(1)} collective-permute-done((bf16[4,4,128,128]{3,2,1,0:T(8,128)(2,1)S(1)}, bf16[4,4,128,128]{3,2,1,0:T(8,128)(2,1)S(1)}, u32[]{:S(2)}, u32[]{:S(2)}) %collective-permute-start.20) | collective-permute-done | bytes 524320 | tf_op jit(solution)/shard_map/ppermute | solution.py:353
  133.9 5.6 %collective-permute-done.19 = bf16[4,4,128,128]{3,2,1,0:T(8,128)(2,1)S(1)} collective-permute-done((bf16[4,4,128,128]{3,2,1,0:T(8,128)(2,1)S(1)}, bf16[4,4,128,128]{3,2,1,0:T(8,128)(2,1)S(1)}, u32[]{:S(2)}, u32[]{:S(2)}) %collective-permute-start.19) | collective-permute-done | bytes 524320 | tf_op jit(solution)/shard_map/ppermute | solution.py:353
  139.5 1.1 multiply_bitcast_fusion
  (13 shorter events, 0.1 us)
Async XLA Ops:
  4.5 23.1 %collective-permute-start = (bf16[3,4,4,128,128]{4,3,2,1,0:T(8,128)(2,1)}, bf16[3,4,4,128,128]{4,3,2,1,0:T(8,128)(2,1)S(1)}, u32[]{:S(2)}, u32[]{:S(2)}) collective-permute-start(bf16[3,4,4,128,128]{4,3,2,1,0:T(8,128)(2,1)} %shard_map.86.refs_12_.refs_1_), channel_id=1, source_target_pairs={{0,0},{1,4},{2,2},{3,6},{4,1},{5,5},{6,3},{7,7},{8,8},{9,12},{10,1... | collective-permute-start | bytes 4718600 | tf_op jit(solution)/shard_map/ppermute | solution.py:353
  9.7 34.2 %copy-start = (bf16[3,4,4,128,128]{4,3,2,1,0:T(8,128)(2,1)S(1)}, bf16[3,4,4,128,128]{4,3,2,1,0:T(8,128)(2,1)}, u32[]{:S(2)}) copy-start(bf16[3,4,4,128,128]{4,3,2,1,0:T(8,128)(2,1)} %shard_map.86.refs_12_.refs_1_) | copy-start | bytes 4718596
  27.6 14.9 %collective-permute-start.2 = (bf16[2,4,4,128,128]{4,3,2,1,0:T(8,128)(2,1)S(1)}, bf16[2,4,4,128,128]{4,3,2,1,0:T(8,128)(2,1)S(1)}, u32[]{:S(2)}, u32[]{:S(2)}) collective-permute-start(bf16[2,4,4,128,128]{4,3,2,1,0:T(8,128)(2,1)S(1)} %slice.17.refs_1_), channel_id=1, source_target_pairs={{0,8},{1,9},{2,10},{3,11},{4,12},{5,13},{6,14},{7,15},{24,16},{25,... | collective-permute-start | bytes 3145736 | tf_op jit(solution)/shard_map/ppermute | solution.py:353
  30.9 13.0 %collective-permute-start.4 = (bf16[2,4,4,128,128]{4,3,2,1,0:T(8,128)(2,1)S(1)}, bf16[2,4,4,128,128]{4,3,2,1,0:T(8,128)(2,1)S(1)}, u32[]{:S(2)}, u32[]{:S(2)}) collective-permute-start(bf16[2,4,4,128,128]{4,3,2,1,0:T(8,128)(2,1)S(1)} %slice.17.refs_1_), channel_id=1, source_target_pairs={{8,16},{9,17},{10,18},{11,19},{12,20},{13,21},{14,22},{15,23},{16,... | collective-permute-start | bytes 3145736 | tf_op jit(solution)/shard_map/ppermute | solution.py:353
  31.6 27.0 %collective-permute-start.6 = (bf16[2,4,4,128,128]{4,3,2,1,0:T(8,128)(2,1)S(1)}, bf16[2,4,4,128,128]{4,3,2,1,0:T(8,128)(2,1)S(1)}, u32[]{:S(2)}, u32[]{:S(2)}) collective-permute-start(bf16[2,4,4,128,128]{4,3,2,1,0:T(8,128)(2,1)S(1)} %slice.17.refs_1_), channel_id=1, source_target_pairs={{8,0},{9,1},{10,2},{11,3},{12,4},{13,5},{14,6},{15,7},{16,24},{17,... | collective-permute-start | bytes 3145736 | tf_op jit(solution)/shard_map/ppermute | solution.py:353
  33.0 26.3 %collective-permute-start.1 = (bf16[1,4,4,128,128]{4,3,2,1,0:T(8,128)(2,1)S(1)}, bf16[1,4,4,128,128]{4,3,2,1,0:T(8,128)(2,1)S(1)}, u32[]{:S(2)}, u32[]{:S(2)}) collective-permute-start(bf16[1,4,4,128,128]{4,3,2,1,0:T(8,128)(2,1)S(1)} %slice.16.refs_0_), channel_id=1, source_target_pairs={{0,8},{1,9},{2,10},{3,11},{4,12},{5,13},{6,14},{7,15},{24,16},{25,... | collective-permute-start | bytes 1572872 | tf_op jit(solution)/shard_map/ppermute | solution.py:353
  37.1 23.6 %collective-permute-start.3 = (bf16[1,4,4,128,128]{4,3,2,1,0:T(8,128)(2,1)S(1)}, bf16[1,4,4,128,128]{4,3,2,1,0:T(8,128)(2,1)S(1)}, u32[]{:S(2)}, u32[]{:S(2)}) collective-permute-start(bf16[1,4,4,128,128]{4,3,2,1,0:T(8,128)(2,1)S(1)} %slice.16.refs_0_), channel_id=1, source_target_pairs={{8,16},{9,17},{10,18},{11,19},{12,20},{13,21},{14,22},{15,23},{16,... | collective-permute-start | bytes 1572872 | tf_op jit(solution)/shard_map/ppermute | solution.py:353
  42.6 21.4 %collective-permute-start.5 = (bf16[1,4,4,128,128]{4,3,2,1,0:T(8,128)(2,1)S(1)}, bf16[1,4,4,128,128]{4,3,2,1,0:T(8,128)(2,1)S(1)}, u32[]{:S(2)}, u32[]{:S(2)}) collective-permute-start(bf16[1,4,4,128,128]{4,3,2,1,0:T(8,128)(2,1)S(1)} %slice.16.refs_0_), channel_id=1, source_target_pairs={{8,0},{9,1},{10,2},{11,3},{12,4},{13,5},{14,6},{15,7},{16,24},{17,... | collective-permute-start | bytes 1572872 | tf_op jit(solution)/shard_map/ppermute | solution.py:353
  43.9 20.1 %collective-permute-start.7 = (bf16[3,4,4,128,128]{4,3,2,1,0:T(8,128)(2,1)S(1)}, bf16[3,4,4,128,128]{4,3,2,1,0:T(8,128)(2,1)S(1)}, u32[]{:S(2)}, u32[]{:S(2)}) collective-permute-start(bf16[3,4,4,128,128]{4,3,2,1,0:T(8,128)(2,1)S(1)} %copy-done), channel_id=1, source_target_pairs={{0,2},{1,3},{2,0},{3,1},{4,6},{5,7},{6,4},{7,5},{8,10},{9,11},{10,... | collective-permute-start | bytes 4718600 | tf_op jit(solution)/shard_map/ppermute | solution.py:353
  58.6 21.6 %collective-permute-start.9 = (bf16[2,4,4,128,128]{4,3,2,1,0:T(8,128)(2,1)S(1)}, bf16[2,4,4,128,128]{4,3,2,1,0:T(8,128)(2,1)S(1)}, u32[]{:S(2)}, u32[]{:S(2)}) collective-permute-start(bf16[2,4,4,128,128]{4,3,2,1,0:T(8,128)(2,1)S(1)} %collective-permute-done.2.refs_3_), channel_id=1, source_target_pairs={{8,16},{9,17},{10,18},{11,19},{12,20},{13,21},{14,22},{15,23},{16,... | collective-permute-start | bytes 3145736 | tf_op jit(solution)/shard_map/ppermute | solution.py:353
  59.3 21.6 %collective-permute-start.11 = (bf16[2,4,4,128,128]{4,3,2,1,0:T(8,128)(2,1)S(1)}, bf16[2,4,4,128,128]{4,3,2,1,0:T(8,128)(2,1)S(1)}, u32[]{:S(2)}, u32[]{:S(2)}) collective-permute-start(bf16[2,4,4,128,128]{4,3,2,1,0:T(8,128)(2,1)S(1)} %collective-permute-done.4.refs_5_), channel_id=1, source_target_pairs={{8,0},{9,1},{10,2},{11,3},{12,4},{13,5},{14,6},{15,7},{16,24},{17,... | collective-permute-start | bytes 3145736 | tf_op jit(solution)/shard_map/ppermute | solution.py:353
  60.7 19.4 %collective-permute-start.12 = (bf16[3,4,4,128,128]{4,3,2,1,0:T(8,128)(2,1)S(1)}, bf16[3,4,4,128,128]{4,3,2,1,0:T(8,128)(2,1)S(1)}, u32[]{:S(2)}, u32[]{:S(2)}) collective-permute-start(bf16[3,4,4,128,128]{4,3,2,1,0:T(8,128)(2,1)S(1)} %collective-permute-done), channel_id=1, source_target_pairs={{0,4},{1,0},{2,6},{3,2},{4,5},{5,1},{6,7},{7,3},{8,12},{9,8},{10,1... | collective-permute-start | bytes 4718600 | tf_op jit(solution)/shard_map/ppermute | solution.py:353
  64.0 18.2 %collective-permute-start.8 = (bf16[1,4,4,128,128]{4,3,2,1,0:T(8,128)(2,1)S(1)}, bf16[1,4,4,128,128]{4,3,2,1,0:T(8,128)(2,1)S(1)}, u32[]{:S(2)}, u32[]{:S(2)}) collective-permute-start(bf16[1,4,4,128,128]{4,3,2,1,0:T(8,128)(2,1)S(1)} %collective-permute-done.1.refs_2_), channel_id=1, source_target_pairs={{8,16},{9,17},{10,18},{11,19},{12,20},{13,21},{14,22},{15,23},{16,... | collective-permute-start | bytes 1572872 | tf_op jit(solution)/shard_map/ppermute | solution.py:353
  64.7 23.9 %collective-permute-start.10 = (bf16[1,4,4,128,128]{4,3,2,1,0:T(8,128)(2,1)S(1)}, bf16[1,4,4,128,128]{4,3,2,1,0:T(8,128)(2,1)S(1)}, u32[]{:S(2)}, u32[]{:S(2)}) collective-permute-start(bf16[1,4,4,128,128]{4,3,2,1,0:T(8,128)(2,1)S(1)} %collective-permute-done.3.refs_4_), channel_id=1, source_target_pairs={{8,0},{9,1},{10,2},{11,3},{12,4},{13,5},{14,6},{15,7},{16,24},{17,... | collective-permute-start | bytes 1572872 | tf_op jit(solution)/shard_map/ppermute | solution.py:353
  80.1 12.9 %collective-permute-start.14 = (bf16[1,4,4,128,128]{4,3,2,1,0:T(8,128)(2,1)S(1)}, bf16[1,4,4,128,128]{4,3,2,1,0:T(8,128)(2,1)S(1)}, u32[]{:S(2)}, u32[]{:S(2)}) collective-permute-start(bf16[1,4,4,128,128]{4,3,2,1,0:T(8,128)(2,1)S(1)} %slice.19), channel_id=1, source_target_pairs={{0,4},{1,5},{2,6},{3,7},{4,0},{5,1},{6,2},{7,3},{8,12},{9,13},{10,... | collective-permute-start | bytes 1572872 | tf_op jit(solution)/shard_map/ppermute | solution.py:353
  80.2 24.3 %collective-permute-start.13 = (bf16[2,4,4,128,128]{4,3,2,1,0:T(8,128)(2,1)S(1)}, bf16[2,4,4,128,128]{4,3,2,1,0:T(8,128)(2,1)S(1)}, u32[]{:S(2)}, u32[]{:S(2)}) collective-permute-start(bf16[2,4,4,128,128]{4,3,2,1,0:T(8,128)(2,1)S(1)} %slice.18), channel_id=1, source_target_pairs={{0,2},{1,3},{2,0},{3,1},{4,6},{5,7},{6,4},{7,5},{8,10},{9,11},{10,... | collective-permute-start | bytes 3145736 | tf_op jit(solution)/shard_map/ppermute | solution.py:353
  80.9 30.3 %collective-permute-start.15 = (bf16[2,4,4,128,128]{4,3,2,1,0:T(8,128)(2,1)S(1)}, bf16[2,4,4,128,128]{4,3,2,1,0:T(8,128)(2,1)S(1)}, u32[]{:S(2)}, u32[]{:S(2)}) collective-permute-start(bf16[2,4,4,128,128]{4,3,2,1,0:T(8,128)(2,1)S(1)} %collective-permute-done.9.refs_9_), channel_id=1, source_target_pairs={{8,0},{9,1},{10,2},{11,3},{12,4},{13,5},{14,6},{15,7},{16,24},{17,... | collective-permute-start | bytes 3145736 | tf_op jit(solution)/shard_map/ppermute | solution.py:353
  82.2 39.2 %collective-permute-start.17 = (bf16[1,4,4,128,128]{4,3,2,1,0:T(8,128)(2,1)S(1)}, bf16[1,4,4,128,128]{4,3,2,1,0:T(8,128)(2,1)S(1)}, u32[]{:S(2)}, u32[]{:S(2)}) collective-permute-start(bf16[1,4,4,128,128]{4,3,2,1,0:T(8,128)(2,1)S(1)} %collective-permute-done.8.refs_8_), channel_id=1, source_target_pairs={{8,0},{9,1},{10,2},{11,3},{12,4},{13,5},{14,6},{15,7},{16,24},{17,... | collective-permute-start | bytes 1572872 | tf_op jit(solution)/shard_map/ppermute | solution.py:353
  113.6 3.7 %collective-permute-start.16 = (f32[4,4,128,128]{3,2,1,0:T(8,128)S(1)}, f32[4,4,128,128]{3,2,1,0:T(8,128)S(1)}, u32[]{:S(2)}, u32[]{:S(2)}) collective-permute-start(f32[4,4,128,128]{3,2,1,0:T(8,128)S(1)} %get-tuple-element.49), channel_id=1, source_target_pairs={{0,1},{1,0},{2,3},{3,2},{4,5},{5,4},{6,7},{7,6},{8,9},{9,8},{10,11... | collective-permute-start | bytes 3145736 | tf_op jit(solution)/shard_map/ppermute | solution.py:353
  123.2 6.3 %copy-start.1 = (s32[4,1,4]{2,1,0:T(1,128)S(1)}, s32[4,1,4]{2,1,0:T(1,128)}, u32[]{:S(2)}) copy-start(s32[4,1,4]{2,1,0:T(1,128)} %refs_1_.1) | copy-start | bytes 196
  123.2 3.5 %collective-permute-start.18 = (f32[4,4,128,128]{3,2,1,0:T(8,128)S(1)}, f32[4,4,128,128]{3,2,1,0:T(8,128)S(1)}, u32[]{:S(2)}, u32[]{:S(2)}) collective-permute-start(f32[4,4,128,128]{3,2,1,0:T(8,128)S(1)} %get-tuple-element.60), channel_id=1, source_target_pairs={{0,1},{1,0},{2,3},{3,2},{4,5},{5,4},{6,7},{7,6},{8,9},{9,8},{10,11... | collective-permute-start | bytes 3145736 | tf_op jit(solution)/shard_map/ppermute | solution.py:353
  123.4 10.5 %collective-permute-start.20 = (bf16[4,4,128,128]{3,2,1,0:T(8,128)(2,1)S(1)}, bf16[4,4,128,128]{3,2,1,0:T(8,128)(2,1)S(1)}, u32[]{:S(2)}, u32[]{:S(2)}) collective-permute-start(bf16[4,4,128,128]{3,2,1,0:T(8,128)(2,1)S(1)} %add_convert_fusion.1), channel_id=1, source_target_pairs={{0,0},{1,4},{2,2},{3,6},{4,1},{5,5},{6,3},{7,7},{8,8},{9,12},{10,1... | collective-permute-start | bytes 1572872 | tf_op jit(solution)/shard_map/ppermute | solution.py:353
  126.8 12.7 %collective-permute-start.19 = (bf16[4,4,128,128]{3,2,1,0:T(8,128)(2,1)S(1)}, bf16[4,4,128,128]{3,2,1,0:T(8,128)(2,1)S(1)}, u32[]{:S(2)}, u32[]{:S(2)}) collective-permute-start(bf16[4,4,128,128]{3,2,1,0:T(8,128)(2,1)S(1)} %add_convert_fusion), channel_id=1, source_target_pairs={{0,0},{1,4},{2,2},{3,6},{4,1},{5,5},{6,3},{7,7},{8,8},{9,12},{10,1... | collective-permute-start | bytes 1572872 | tf_op jit(solution)/shard_map/ppermute | solution.py:353
